TPU v7x, 32 devices: a whole 2x2x4 slice. The times are simulated.
32 devices in a mesh: grp: 4 (over x, core), chan: 8 (over z, y).
Axes of the slice: x: 2, y: 2, z: 4, core: 2. Of those that a mesh axis runs over, the one named last changes fastest.
Arguments:
- vit_in: bfloat16 [4608, 1024], P(('grp', 'chan')), may hold values from -6 to 6
- hires: bfloat16 [8, 1536, 2304], P('grp', 'chan'), may hold values from -6 to 6
- size_class: int32 [8], P('grp'), may hold values from 24 to 48, as said below
- pool_mask: int32 [8, 2304], P('grp'), may hold values 0 or 1
- cotangent: bfloat16 [4608, 1024], P(('grp', 'chan')), may hold values from -6 to 6
- ln1_gain: bfloat16 [1024], P('chan'), may hold values from 0.5 to 1.5
- ln1_bias: bfloat16 [1024], P('chan'), may hold values from -1.75 to 1.75
- qkv_weight: bfloat16 [1024, 3072], P('chan'), may hold values from -0.1875 to 0.1875
- qv_bias: bfloat16 [2048], P('chan'), may hold values from -1.75 to 1.75
- out_weight: bfloat16 [1024, 1024], P('chan'), may hold values from -0.75 to 0.75
- out_bias: bfloat16 [1024], P('chan'), may hold values from -1.75 to 1.75
- ln2_gain: bfloat16 [1024], P('chan'), may hold values from 0.5 to 1.5
- ln2_bias: bfloat16 [1024], P('chan'), may hold values from -1.75 to 1.75
- fc1_weight: bfloat16 [1024, 4096], P('chan'), may hold values from -0.1875 to 0.1875
- fc1_bias: bfloat16 [4096], P('chan'), may hold values from -1.75 to 1.75
- fc2_weight: bfloat16 [4096, 1024], P('chan'), may hold values from -0.09375 to 0.09375
- fc2_bias: bfloat16 [1024], P('chan'), may hold values from -1.75 to 1.75
- dw7_weight: bfloat16 [49, 1536], P(None, 'chan'), may hold values from -0.875 to 0.875
- dw7_bias: bfloat16 [1536], P('chan'), may hold values from -1.75 to 1.75
- conv_gain: bfloat16 [1536], P('chan'), may hold values from 0.5 to 1.5
- conv_bias: bfloat16 [1536], P('chan'), may hold values from -1.75 to 1.75
- pw1_weight: bfloat16 [1536, 6144], P('chan'), may hold values from -0.15625 to 0.15625
- pw1_bias: bfloat16 [6144], P('chan'), may hold values from -1.75 to 1.75
- pw2_weight: bfloat16 [6144, 1536], P('chan'), may hold values from -0.078125 to 0.078125
- pw2_bias: bfloat16 [1536], P('chan'), may hold values from -1.75 to 1.75
- layer_scale: bfloat16 [1536], P('chan'), may hold values from 0.5 to 1.5
- proj_weight: bfloat16 [1536, 1024], P('chan'), may hold values from -0.15625 to 0.15625
- proj_bias: bfloat16 [1024], P('chan'), may hold values from -1.75 to 1.75
- dw3_weight: bfloat16 [9, 1024], P(None, 'chan'), may hold values from -2 to 2
- dw3_bias: bfloat16 [1024], P('chan'), may hold values from -1.75 to 1.75
- gate: bfloat16 [1024], P('chan'), may hold values from -1.5 to 1.5
Outputs:
- vit_out: float32 [4608, 1024], P(('grp', 'chan'))
- vit_grad: float32 [4608, 1024], P(('grp', 'chan'))
- hires_grad: float32 [8, 1536, 2304], P('grp', 'chan')
- grad_ln1_gain: float32 [1024], P('chan')
- grad_ln1_bias: float32 [1024], P('chan')
- grad_qkv_weight: float32 [1024, 3072], P('chan')
- grad_qv_bias: float32 [2048], P('chan')
- grad_out_weight: float32 [1024, 1024], P('chan')
- grad_out_bias: float32 [1024], P('chan')
- grad_ln2_gain: float32 [1024], P('chan')
- grad_ln2_bias: float32 [1024], P('chan')
- grad_fc1_weight: float32 [1024, 4096], P('chan')
- grad_fc1_bias: float32 [4096], P('chan')
- grad_fc2_weight: float32 [4096, 1024], P('chan')
- grad_fc2_bias: float32 [1024], P('chan')
- grad_dw7_weight: float32 [49, 1536], P(None, 'chan')
- grad_dw7_bias: float32 [1536], P('chan')
- grad_conv_gain: float32 [1536], P('chan')
- grad_conv_bias: float32 [1536], P('chan')
- grad_pw1_weight: float32 [1536, 6144], P('chan')
- grad_pw1_bias: float32 [6144], P('chan')
- grad_pw2_weight: float32 [6144, 1536], P('chan')
- grad_pw2_bias: float32 [1536], P('chan')
- grad_layer_scale: float32 [1536], P('chan')
- grad_proj_weight: float32 [1536, 1024], P('chan')
- grad_proj_bias: float32 [1024], P('chan')
- grad_dw3_weight: float32 [9, 1024], P(None, 'chan')
- grad_dw3_bias: float32 [1024], P('chan')
- grad_gate: float32 [1024], P('chan')
Inputs may be any that keep to these rules, and one draw needn't show every extreme that they name: size_class[n] is 24, 32 or 48; every draw holds an image of each end value.
All inputs are finite; a program needn't handle non-finite values. No bound on the sum of `pool_mask` on one device may be relied on, other than what follows from the above.
Results may differ from a plain program's by a relative error of at most 0.022.
Values may be sent and summed in bfloat16 or wider, within the bound.
No kernel may reach another device: no remote copies, remote signals or barrier semaphores. Data moves between devices by JAX's collectives and lax.ppermute only.
A program may use at most 512 MiB of HBM per device.

v0:
```python
import jax
import jax.numpy as jnp
from jax import lax
from jax.sharding import PartitionSpec as P

D = 1024
HEADS = 16
HEAD_DIM = 64
KERNEL = 7
GRID = 24
BANDS = 4


EPS_VIT = 1e-05
EPS_CONV = 1e-06


def swapped(shard, axis, apart):
    return lax.ppermute(shard, axis, [(i, i ^ 1 << apart) for i in range(lax.axis_size(axis))])


def shifted_2(value, axis, steps):
    count = lax.axis_size(axis)
    first, last = (max(0, -steps), min(count, count - steps))
    return lax.ppermute(value, axis, [(source, source + steps) for source in range(first, last)])


def layer_norm(inputs, gain, shift_term, epsilon):
    mean_row = jnp.mean(inputs, axis=-1, keepdims=True)
    centred = inputs - mean_row
    variance = jnp.mean(centred * centred, axis=-1, keepdims=True)
    return centred * lax.rsqrt(variance + epsilon) * gain + shift_term


def norm_vit(inputs, gain, shift_term):
    return layer_norm(inputs, gain, shift_term, EPS_VIT)


def norm_conv(inputs, gain, shift_term):
    return layer_norm(inputs, gain, shift_term, EPS_CONV)


def gelu_exact(inputs):
    return jax.nn.gelu(inputs, approximate=False)


def matmul(left, right):
    return jnp.dot(left, right, preferred_element_type=jnp.float32)


def left_grad(inputs, grads):
    return lax.dot_general(
        inputs, grads, (((0,), (0,)), ((), ())), preferred_element_type=jnp.float32
    )


def right_grad(grads, weight):
    return lax.dot_general(
        grads, weight, (((1,), (1,)), ((), ())), preferred_element_type=jnp.float32
    )


def column_sum(grads):
    return jnp.sum(grads.astype(jnp.float32), axis=0)


def depthwise(in_field, kernel_taps, kernel_bias, valid_cells):
    map_side = 2 * GRID
    map_cells = map_side * map_side
    half_kernel = KERNEL // 2
    margin = half_kernel * map_side + half_kernel
    padded = jnp.pad(in_field, ((0, 0), (0, 0), (margin, margin)))
    columns = lax.broadcasted_iota(jnp.int32, (map_cells,), 0) % map_side
    running = jnp.zeros(in_field.shape, jnp.float32) + kernel_bias[None, :, None]
    for row_step in range(KERNEL):
        for col_step in range(KERNEL):
            col_offset = col_step - half_kernel
            cell_shift = (row_step - half_kernel) * map_side + col_offset
            column_ok = ((columns + col_offset >= 0) & (columns + col_offset < map_side)).astype(
                jnp.float32
            )
            shifted = lax.slice_in_dim(
                padded, margin + cell_shift, margin + cell_shift + map_cells, axis=2
            )
            running = running + kernel_taps[row_step * KERNEL + col_step][None, :, None] * (
                shifted * column_ok
            )
    return running * valid_cells[:, None, :]


def band_layout(cell_data, classes):
    image_count = cell_data.shape[0]
    chan_count = cell_data.shape[1]
    map_side = 2 * GRID
    band_cells = map_side * map_side // BANDS
    result = jnp.zeros((image_count, BANDS, chan_count, band_cells), cell_data.dtype)
    for map_size in (GRID, 4 * GRID // 3, 2 * GRID):
        used_cells = map_size // BANDS * map_side
        banded = cell_data[:, :, : map_size * map_side].reshape(
            image_count, chan_count, BANDS, used_cells
        )
        banded = jnp.pad(banded, ((0, 0), (0, 0), (0, 0), (0, band_cells - used_cells)))
        banded = jnp.transpose(banded, (0, 2, 1, 3))
        result = jnp.where((classes == map_size)[:, None, None, None], banded, result)
    return result.reshape(image_count * BANDS, chan_count, band_cells)


def grid_layout(bands_data, classes):
    image_count = bands_data.shape[0] // BANDS
    chan_count = bands_data.shape[1]
    map_side = 2 * GRID
    map_cells = map_side * map_side
    band_cells = map_cells // BANDS
    regrouped = jnp.transpose(
        bands_data.reshape(image_count, BANDS, chan_count, band_cells), (0, 2, 1, 3)
    )
    result = jnp.zeros((image_count, chan_count, map_cells), bands_data.dtype)
    for map_size in (GRID, 4 * GRID // 3, 2 * GRID):
        used_cells = map_size // BANDS * map_side
        unbanded = regrouped[:, :, :, :used_cells].reshape(
            image_count, chan_count, map_size * map_side
        )
        unbanded = jnp.pad(unbanded, ((0, 0), (0, 0), (0, map_cells - map_size * map_side)))
        result = jnp.where((classes == map_size)[:, None, None], unbanded, result)
    return result


def share_rows(piece, chan_index):
    gathered = piece
    for bit_level in range(BANDS.bit_length() - 1):
        partner = swapped(gathered, "chan", bit_level)
        is_upper = chan_index // 2**bit_level % 2 == 1
        gathered = jnp.where(
            is_upper,
            jnp.concatenate([partner, gathered], axis=0),
            jnp.concatenate([gathered, partner], axis=0),
        )
    return gathered


def reduce_rows(full_rows, chan_index):
    current = full_rows
    for bit_level in reversed(range(BANDS.bit_length() - 1)):
        half_rows = current.shape[0] // 2
        low_half = current[:half_rows]
        high_half = current[half_rows:]
        is_upper = chan_index // 2**bit_level % 2 == 1
        kept_half = jnp.where(is_upper, high_half, low_half)
        sent_half = jnp.where(is_upper, low_half, high_half)
        current = kept_half + swapped(sent_half.astype(jnp.bfloat16), "chan", bit_level).astype(
            sent_half.dtype
        )
    return current


def body(
    vit_in,
    hires,
    size_class,
    pool_mask,
    cotangent,
    ln1_gain,
    ln1_bias,
    qkv_weight,
    qv_bias,
    out_weight,
    out_bias,
    ln2_gain,
    ln2_bias,
    fc1_weight,
    fc1_bias,
    fc2_weight,
    fc2_bias,
    dw7_weight,
    dw7_bias,
    conv_gain,
    conv_bias,
    pw1_weight,
    pw1_bias,
    pw2_weight,
    pw2_bias,
    layer_scale,
    proj_weight,
    proj_bias,
    dw3_weight,
    dw3_bias,
    gate,
):
    single = jnp.float32
    half_type = jnp.bfloat16
    chan_index = lax.axis_index("chan")
    band_index = chan_index % BANDS
    image_local = chan_index // BANDS
    map_side = 2 * GRID
    map_cells = map_side * map_side
    band_cells = map_cells // BANDS
    pooled_rows = GRID // BANDS
    tok_rows = pooled_rows * GRID
    image_tokens = GRID * GRID
    scale_factor = HEAD_DIM ** (-0.5)
    (
        full_ln1_gain,
        full_ln1_bias,
        full_qkv,
        full_qv_bias,
        full_out,
        full_out_bias,
        full_ln2_gain,
        full_ln2_bias,
        full_fc1,
        full_fc1_bias,
        full_fc2,
        full_fc2_bias,
        full_conv_gain,
        full_conv_bias,
        full_pw1,
        full_pw1_bias,
        full_pw2,
        full_pw2_bias,
        full_scale,
        full_proj,
        full_proj_bias,
        full_dw3,
        full_dw3_bias,
        full_gate,
    ) = (
        lax.all_gather(ln1_gain, "chan", axis=0, tiled=True),
        lax.all_gather(ln1_bias, "chan", axis=0, tiled=True),
        lax.all_gather(qkv_weight, "chan", axis=0, tiled=True),
        lax.all_gather(qv_bias, "chan", axis=0, tiled=True),
        lax.all_gather(out_weight, "chan", axis=0, tiled=True),
        lax.all_gather(out_bias, "chan", axis=0, tiled=True),
        lax.all_gather(ln2_gain, "chan", axis=0, tiled=True),
        lax.all_gather(ln2_bias, "chan", axis=0, tiled=True),
        lax.all_gather(fc1_weight, "chan", axis=0, tiled=True),
        lax.all_gather(fc1_bias, "chan", axis=0, tiled=True),
        lax.all_gather(fc2_weight, "chan", axis=0, tiled=True),
        lax.all_gather(fc2_bias, "chan", axis=0, tiled=True),
        lax.all_gather(conv_gain, "chan", axis=0, tiled=True),
        lax.all_gather(conv_bias, "chan", axis=0, tiled=True),
        lax.all_gather(pw1_weight, "chan", axis=0, tiled=True),
        lax.all_gather(pw1_bias, "chan", axis=0, tiled=True),
        lax.all_gather(pw2_weight, "chan", axis=0, tiled=True),
        lax.all_gather(pw2_bias, "chan", axis=0, tiled=True),
        lax.all_gather(layer_scale, "chan", axis=0, tiled=True),
        lax.all_gather(proj_weight, "chan", axis=0, tiled=True),
        lax.all_gather(proj_bias, "chan", axis=0, tiled=True),
        lax.all_gather(dw3_weight, "chan", axis=1, tiled=True),
        lax.all_gather(dw3_bias, "chan", axis=0, tiled=True),
        lax.all_gather(gate, "chan", axis=0, tiled=True),
    )
    row_ids = lax.broadcasted_iota(jnp.int32, (map_side, map_side), 0).reshape(map_cells)
    col_ids = lax.broadcasted_iota(jnp.int32, (map_side, map_side), 1).reshape(map_cells)
    valid_cells = (
        (row_ids[None, :] < size_class[:, None]) & (col_ids[None, :] < size_class[:, None])
    ).astype(single)
    masked_in = jnp.where(valid_cells[:, None, :] > 0, hires, jnp.zeros_like(hires))

    def conv_piece(in_field, kernel_taps, kernel_bias):
        return depthwise(in_field, kernel_taps, kernel_bias, valid_cells)

    conv_out, conv_pullback = jax.vjp(
        conv_piece, masked_in.astype(single), dw7_weight.astype(single), dw7_bias.astype(single)
    )
    conv_low = conv_out.astype(half_type)
    conv_band, resid_band = (
        lax.all_to_all(
            band_layout(conv_low, size_class), "chan", split_axis=0, concat_axis=1, tiled=True
        ),
        lax.all_to_all(
            band_layout(masked_in, size_class), "chan", split_axis=0, concat_axis=1, tiled=True
        ),
    )
    conv_rows = jnp.transpose(conv_band[0]).astype(single)
    resid_rows = jnp.transpose(resid_band[0]).astype(single)
    normed, conv_norm_pullback = jax.vjp(
        norm_conv, conv_rows, full_conv_gain.astype(single), full_conv_bias.astype(single)
    )
    normed_low = normed.astype(half_type)
    conv_hidden = matmul(normed_low, full_pw1) + full_pw1_bias.astype(single)
    conv_act, conv_gelu_pullback = jax.vjp(gelu_exact, conv_hidden)
    conv_act_low = conv_act.astype(half_type)
    conv_branch = matmul(conv_act_low, full_pw2) + full_pw2_bias.astype(single)
    scale_vector = full_scale.astype(single)
    refined_low = (resid_rows + scale_vector * conv_branch).astype(half_type)
    image_pick = lax.broadcasted_iota(jnp.int32, size_class.shape, 0) == image_local
    my_size = jnp.sum(jnp.where(image_pick, size_class, 0))
    mask_bands = band_layout(pool_mask.astype(single)[:, None, :], size_class)
    my_mask = lax.dynamic_index_in_dim(mask_bands, chan_index, 0, keepdims=False)[0]
    out_ids = lax.broadcasted_iota(jnp.int32, (tok_rows,), 0)
    out_row = out_ids // GRID
    out_col = out_ids % GRID
    cell_ids = lax.broadcasted_iota(jnp.int32, (band_cells,), 0)
    cell_row = cell_ids // map_side
    cell_col = cell_ids % map_side
    row_hit = ((out_row * my_size // GRID)[:, None] <= cell_row[None, :]) & (
        cell_row[None, :] < (((out_row + 1) * my_size + GRID - 1) // GRID)[:, None]
    )
    col_hit = ((out_col * my_size // GRID)[:, None] <= cell_col[None, :]) & (
        cell_col[None, :] < (((out_col + 1) * my_size + GRID - 1) // GRID)[:, None]
    )
    pool_table = jnp.where(row_hit & col_hit, my_mask[None, :], 0.0)
    pool_count = jnp.maximum(jnp.sum(pool_table, axis=1), 1.0)
    pooled = matmul(pool_table.astype(half_type), refined_low) / pool_count[:, None]
    pooled_low = pooled.astype(half_type)
    adapt_low = (
        (matmul(pooled_low, full_proj) + full_proj_bias.astype(single))
        .astype(half_type)
        .reshape(pooled_rows, GRID, D)
    )
    rows_before = shifted_2(adapt_low[pooled_rows - 1 :], "chan", 1)
    rows_after = shifted_2(adapt_low[:1], "chan", -1)
    with_rims = jnp.concatenate([rows_before, adapt_low, rows_after], axis=0)
    row_keep = jnp.concatenate(
        [
            (band_index > 0).astype(single)[None],
            jnp.ones((pooled_rows,), single),
            (band_index < BANDS - 1).astype(single)[None],
        ]
    )
    framed = jnp.pad(with_rims.astype(single) * row_keep[:, None, None], ((0, 0), (1, 1), (0, 0)))
    dw3_taps = full_dw3.astype(single)
    adapt_conv = jnp.zeros((pooled_rows, GRID, D), single) + full_dw3_bias.astype(single)
    for row_step in range(3):
        for col_step in range(3):
            adapt_conv = (
                adapt_conv
                + dw3_taps[row_step * 3 + col_step]
                * framed[row_step : row_step + pooled_rows, col_step : col_step + GRID]
            )
    adapt_flat = adapt_conv.reshape(tok_rows, D)
    gate_tanh = jnp.tanh(full_gate.astype(single))
    mixed = vit_in.astype(single) + gate_tanh * adapt_flat
    norm1, ln1_pullback = jax.vjp(
        norm_vit, mixed, full_ln1_gain.astype(single), full_ln1_bias.astype(single)
    )
    norm1_low = norm1.astype(half_type)
    qv_full = full_qv_bias.astype(single)
    bias_full = jnp.concatenate([qv_full[:D], jnp.zeros((D,), single), qv_full[D:]])
    qkv_low = (matmul(norm1_low, full_qkv) + bias_full).astype(half_type)
    queries = qkv_low[:, :D].reshape(tok_rows, HEADS, HEAD_DIM)
    kv_image = share_rows(qkv_low[:, D:], chan_index)
    key_rows = kv_image[:, :D].reshape(image_tokens, HEADS, HEAD_DIM)
    value_rows = kv_image[:, D:].reshape(image_tokens, HEADS, HEAD_DIM)
    scores = (
        jnp.einsum("qhd,khd->hqk", queries, key_rows, preferred_element_type=single) * scale_factor
    )
    row_top = jnp.max(scores, axis=-1, keepdims=True)
    weights = jnp.exp(scores - row_top)
    row_total = jnp.sum(weights, axis=-1, keepdims=True)
    attn_probs = weights / row_total
    log_total = row_top + jnp.log(row_total)
    context_low = (
        jnp.einsum(
            "hqk,khd->qhd", attn_probs.astype(half_type), value_rows, preferred_element_type=single
        )
        .reshape(tok_rows, D)
        .astype(half_type)
    )
    resid = mixed + matmul(context_low, full_out) + full_out_bias.astype(single)
    norm2, ln2_pullback = jax.vjp(
        norm_vit, resid, full_ln2_gain.astype(single), full_ln2_bias.astype(single)
    )
    norm2_low = norm2.astype(half_type)
    mlp_hidden = matmul(norm2_low, full_fc1) + full_fc1_bias.astype(single)
    mlp_act, mlp_gelu_pullback = jax.vjp(gelu_exact, mlp_hidden)
    mlp_act_low = mlp_act.astype(half_type)
    vit_out = resid + matmul(mlp_act_low, full_fc2) + full_fc2_bias.astype(single)
    grad_fc2_weight = left_grad(mlp_act_low, cotangent)
    grad_fc2_bias = column_sum(cotangent)
    grad_mlp_act = right_grad(cotangent, full_fc2)
    grad_hidden_low = mlp_gelu_pullback(grad_mlp_act)[0].astype(half_type)
    grad_fc1_weight = left_grad(norm2_low, grad_hidden_low)
    grad_fc1_bias = column_sum(grad_hidden_low)
    grad_norm2 = right_grad(grad_hidden_low, full_fc1)
    grad_resid_part, grad_ln2_gain, grad_ln2_bias = ln2_pullback(grad_norm2)
    grad_resid = cotangent.astype(single) + grad_resid_part
    grad_attn_low = grad_resid.astype(half_type)
    grad_out_weight = left_grad(context_low, grad_attn_low)
    grad_out_bias = column_sum(grad_attn_low)
    grad_context_low = (
        right_grad(grad_attn_low, full_out).astype(half_type).reshape(tok_rows, HEADS, HEAD_DIM)
    )
    scores_again = (
        jnp.einsum("qhd,khd->hqk", queries, key_rows, preferred_element_type=single) * scale_factor
    )
    probs_again = jnp.exp(scores_again - log_total)
    grad_probs = jnp.einsum(
        "qhd,khd->hqk", grad_context_low, value_rows, preferred_element_type=single
    )
    row_dot = jnp.sum(probs_again * grad_probs, axis=-1, keepdims=True)
    grad_scores_low = (probs_again * (grad_probs - row_dot)).astype(half_type)
    grad_queries = (
        jnp.einsum("hqk,khd->qhd", grad_scores_low, key_rows, preferred_element_type=single)
        * scale_factor
    )
    grad_key_part = (
        jnp.einsum("hqk,qhd->khd", grad_scores_low, queries, preferred_element_type=single)
        * scale_factor
    )
    grad_value_part = jnp.einsum(
        "hqk,qhd->khd",
        probs_again.astype(half_type),
        grad_context_low,
        preferred_element_type=single,
    )
    kv_partial = jnp.concatenate(
        [grad_key_part.reshape(image_tokens, D), grad_value_part.reshape(image_tokens, D)], axis=1
    )
    kv_mine = reduce_rows(kv_partial, chan_index)
    grad_qkv_low = jnp.concatenate([grad_queries.reshape(tok_rows, D), kv_mine], axis=1).astype(
        half_type
    )
    grad_qkv_weight = left_grad(norm1_low, grad_qkv_low)
    grad_qv_bias = jnp.concatenate(
        [column_sum(grad_qkv_low[:, :D]), column_sum(grad_qkv_low[:, 2 * D :])]
    )
    grad_norm1 = right_grad(grad_qkv_low, full_qkv)
    grad_mixed_part, grad_ln1_gain, grad_ln1_bias = ln1_pullback(grad_norm1)
    vit_grad = grad_resid + grad_mixed_part
    grad_gate = jnp.sum(vit_grad * adapt_flat, axis=0) * (1.0 - gate_tanh * gate_tanh)
    grad_conv3_low = (gate_tanh * vit_grad).astype(half_type).reshape(pooled_rows, GRID, D)
    grad_conv3 = grad_conv3_low.astype(single)
    grad_dw3_bias = jnp.sum(grad_conv3, axis=(0, 1))
    tap_grads = []
    for row_step in range(3):
        for col_step in range(3):
            tap_grads.append(
                jnp.sum(
                    grad_conv3
                    * framed[row_step : row_step + pooled_rows, col_step : col_step + GRID],
                    axis=(0, 1),
                )
            )
    grad_dw3_weight = jnp.stack(tap_grads)
    grads_before = shifted_2(grad_conv3_low[pooled_rows - 1 :], "chan", 1)
    grads_after = shifted_2(grad_conv3_low[:1], "chan", -1)
    grad_rims = jnp.concatenate([grads_before, grad_conv3_low, grads_after], axis=0)
    framed_grad = jnp.pad(
        grad_rims.astype(single) * row_keep[:, None, None], ((0, 0), (1, 1), (0, 0))
    )
    grad_adapt = jnp.zeros((pooled_rows, GRID, D), single)
    for row_step in range(3):
        for col_step in range(3):
            grad_adapt = (
                grad_adapt
                + dw3_taps[row_step * 3 + col_step]
                * framed_grad[
                    2 - row_step : 2 - row_step + pooled_rows, 2 - col_step : 2 - col_step + GRID
                ]
            )
    grad_adapt_low = grad_adapt.reshape(tok_rows, D).astype(half_type)
    grad_proj_weight = left_grad(pooled_low, grad_adapt_low)
    grad_proj_bias = column_sum(grad_adapt_low)
    grad_pooled_low = right_grad(grad_adapt_low, full_proj).astype(half_type)
    grad_pool_sum = grad_pooled_low.astype(single) / pool_count[:, None]
    grad_refined = lax.dot_general(
        pool_table,
        grad_pool_sum,
        (((0,), (0,)), ((), ())),
        precision=lax.Precision.HIGHEST,
        preferred_element_type=single,
    )
    grad_layer_scale = jnp.sum(grad_refined * conv_branch, axis=0)
    grad_branch_low = (scale_vector * grad_refined).astype(half_type)
    grad_pw2_weight = left_grad(conv_act_low, grad_branch_low)
    grad_pw2_bias = column_sum(grad_branch_low)
    grad_conv_act = right_grad(grad_branch_low, full_pw2)
    grad_conv_hidden_low = conv_gelu_pullback(grad_conv_act)[0].astype(half_type)
    grad_pw1_weight = left_grad(normed_low, grad_conv_hidden_low)
    grad_pw1_bias = column_sum(grad_conv_hidden_low)
    grad_normed = right_grad(grad_conv_hidden_low, full_pw1)
    grad_conv_rows, grad_conv_gain, grad_conv_bias = conv_norm_pullback(grad_normed)
    back_conv, back_resid = (
        lax.all_to_all(
            jnp.transpose(grad_conv_rows.astype(half_type))[None],
            "chan",
            split_axis=1,
            concat_axis=0,
            tiled=True,
        ),
        lax.all_to_all(
            jnp.transpose(grad_refined.astype(half_type))[None],
            "chan",
            split_axis=1,
            concat_axis=0,
            tiled=True,
        ),
    )
    grad_conv_grid = grid_layout(back_conv, size_class).astype(single)
    grad_resid_grid = grid_layout(back_resid, size_class).astype(single)
    grad_field, grad_dw7_weight, grad_dw7_bias = conv_pullback(grad_conv_grid)
    hires_grad = (grad_field + grad_resid_grid) * valid_cells[:, None, :]
    full_grads = [
        grad_ln1_gain,
        grad_ln1_bias,
        grad_qkv_weight,
        grad_qv_bias,
        grad_out_weight,
        grad_out_bias,
        grad_ln2_gain,
        grad_ln2_bias,
        grad_fc1_weight,
        grad_fc1_bias,
        grad_fc2_weight,
        grad_fc2_bias,
        grad_conv_gain,
        grad_conv_bias,
        grad_pw1_weight,
        grad_pw1_bias,
        grad_pw2_weight,
        grad_pw2_bias,
        grad_layer_scale,
        grad_proj_weight,
        grad_proj_bias,
        grad_dw3_weight,
        grad_dw3_bias,
        grad_gate,
    ]
    shards = (
        lax.psum_scatter(
            full_grads[0].astype(jnp.bfloat16), "chan", scatter_dimension=0, tiled=True
        ).astype(jnp.float32),
        lax.psum_scatter(
            full_grads[1].astype(jnp.bfloat16), "chan", scatter_dimension=0, tiled=True
        ).astype(jnp.float32),
        lax.psum_scatter(
            full_grads[2].astype(jnp.bfloat16), "chan", scatter_dimension=0, tiled=True
        ).astype(jnp.float32),
        lax.psum_scatter(
            full_grads[3].astype(jnp.bfloat16), "chan", scatter_dimension=0, tiled=True
        ).astype(jnp.float32),
        lax.psum_scatter(
            full_grads[4].astype(jnp.bfloat16), "chan", scatter_dimension=0, tiled=True
        ).astype(jnp.float32),
        lax.psum_scatter(
            full_grads[5].astype(jnp.bfloat16), "chan", scatter_dimension=0, tiled=True
        ).astype(jnp.float32),
        lax.psum_scatter(
            full_grads[6].astype(jnp.bfloat16), "chan", scatter_dimension=0, tiled=True
        ).astype(jnp.float32),
        lax.psum_scatter(
            full_grads[7].astype(jnp.bfloat16), "chan", scatter_dimension=0, tiled=True
        ).astype(jnp.float32),
        lax.psum_scatter(
            full_grads[8].astype(jnp.bfloat16), "chan", scatter_dimension=0, tiled=True
        ).astype(jnp.float32),
        lax.psum_scatter(
            full_grads[9].astype(jnp.bfloat16), "chan", scatter_dimension=0, tiled=True
        ).astype(jnp.float32),
        lax.psum_scatter(
            full_grads[10].astype(jnp.bfloat16), "chan", scatter_dimension=0, tiled=True
        ).astype(jnp.float32),
        lax.psum_scatter(
            full_grads[11].astype(jnp.bfloat16), "chan", scatter_dimension=0, tiled=True
        ).astype(jnp.float32),
        lax.psum_scatter(
            full_grads[12].astype(jnp.bfloat16), "chan", scatter_dimension=0, tiled=True
        ).astype(jnp.float32),
        lax.psum_scatter(
            full_grads[13].astype(jnp.bfloat16), "chan", scatter_dimension=0, tiled=True
        ).astype(jnp.float32),
        lax.psum_scatter(
            full_grads[14].astype(jnp.bfloat16), "chan", scatter_dimension=0, tiled=True
        ).astype(jnp.float32),
        lax.psum_scatter(
            full_grads[15].astype(jnp.bfloat16), "chan", scatter_dimension=0, tiled=True
        ).astype(jnp.float32),
        lax.psum_scatter(
            full_grads[16].astype(jnp.bfloat16), "chan", scatter_dimension=0, tiled=True
        ).astype(jnp.float32),
        lax.psum_scatter(
            full_grads[17].astype(jnp.bfloat16), "chan", scatter_dimension=0, tiled=True
        ).astype(jnp.float32),
        lax.psum_scatter(
            full_grads[18].astype(jnp.bfloat16), "chan", scatter_dimension=0, tiled=True
        ).astype(jnp.float32),
        lax.psum_scatter(
            full_grads[19].astype(jnp.bfloat16), "chan", scatter_dimension=0, tiled=True
        ).astype(jnp.float32),
        lax.psum_scatter(
            full_grads[20].astype(jnp.bfloat16), "chan", scatter_dimension=0, tiled=True
        ).astype(jnp.float32),
        lax.psum_scatter(
            full_grads[21].astype(jnp.bfloat16), "chan", scatter_dimension=1, tiled=True
        ).astype(jnp.float32),
        lax.psum_scatter(
            full_grads[22].astype(jnp.bfloat16), "chan", scatter_dimension=0, tiled=True
        ).astype(jnp.float32),
        lax.psum_scatter(
            full_grads[23].astype(jnp.bfloat16), "chan", scatter_dimension=0, tiled=True
        ).astype(jnp.float32),
    )
    summed = (
        lax.psum(shards[0].astype(jnp.bfloat16), "grp").astype(jnp.float32),
        lax.psum(shards[1].astype(jnp.bfloat16), "grp").astype(jnp.float32),
        lax.psum(shards[2].astype(jnp.bfloat16), "grp").astype(jnp.float32),
        lax.psum(shards[3].astype(jnp.bfloat16), "grp").astype(jnp.float32),
        lax.psum(shards[4].astype(jnp.bfloat16), "grp").astype(jnp.float32),
        lax.psum(shards[5].astype(jnp.bfloat16), "grp").astype(jnp.float32),
        lax.psum(shards[6].astype(jnp.bfloat16), "grp").astype(jnp.float32),
        lax.psum(shards[7].astype(jnp.bfloat16), "grp").astype(jnp.float32),
        lax.psum(shards[8].astype(jnp.bfloat16), "grp").astype(jnp.float32),
        lax.psum(shards[9].astype(jnp.bfloat16), "grp").astype(jnp.float32),
        lax.psum(shards[10].astype(jnp.bfloat16), "grp").astype(jnp.float32),
        lax.psum(shards[11].astype(jnp.bfloat16), "grp").astype(jnp.float32),
        lax.psum(shards[12].astype(jnp.bfloat16), "grp").astype(jnp.float32),
        lax.psum(shards[13].astype(jnp.bfloat16), "grp").astype(jnp.float32),
        lax.psum(shards[14].astype(jnp.bfloat16), "grp").astype(jnp.float32),
        lax.psum(shards[15].astype(jnp.bfloat16), "grp").astype(jnp.float32),
        lax.psum(shards[16].astype(jnp.bfloat16), "grp").astype(jnp.float32),
        lax.psum(shards[17].astype(jnp.bfloat16), "grp").astype(jnp.float32),
        lax.psum(shards[18].astype(jnp.bfloat16), "grp").astype(jnp.float32),
        lax.psum(shards[19].astype(jnp.bfloat16), "grp").astype(jnp.float32),
        lax.psum(shards[20].astype(jnp.bfloat16), "grp").astype(jnp.float32),
        lax.psum(shards[21].astype(jnp.bfloat16), "grp").astype(jnp.float32),
        lax.psum(shards[22].astype(jnp.bfloat16), "grp").astype(jnp.float32),
        lax.psum(shards[23].astype(jnp.bfloat16), "grp").astype(jnp.float32),
        lax.psum(grad_dw7_weight.astype(jnp.bfloat16), "grp").astype(jnp.float32),
        lax.psum(grad_dw7_bias.astype(jnp.bfloat16), "grp").astype(jnp.float32),
    )
    final_grads = list(summed[:24])
    dw7_sums = (summed[24], summed[25])
    return (
        vit_out,
        vit_grad,
        hires_grad,
        final_grads[0],
        final_grads[1],
        final_grads[2],
        final_grads[3],
        final_grads[4],
        final_grads[5],
        final_grads[6],
        final_grads[7],
        final_grads[8],
        final_grads[9],
        final_grads[10],
        final_grads[11],
        dw7_sums[0],
        dw7_sums[1],
        final_grads[12],
        final_grads[13],
        final_grads[14],
        final_grads[15],
        final_grads[16],
        final_grads[17],
        final_grads[18],
        final_grads[19],
        final_grads[20],
        final_grads[21],
        final_grads[22],
        final_grads[23],
    )


def solution(mesh):
    in_specs = (
        P(("grp", "chan"), None),
        P("grp", "chan", None),
        P("grp"),
        P("grp", None),
        P(("grp", "chan"), None),
        P("chan"),
        P("chan"),
        P("chan", None),
        P("chan"),
        P("chan", None),
        P("chan"),
        P("chan"),
        P("chan"),
        P("chan", None),
        P("chan"),
        P("chan", None),
        P("chan"),
        P(None, "chan"),
        P("chan"),
        P("chan"),
        P("chan"),
        P("chan", None),
        P("chan"),
        P("chan", None),
        P("chan"),
        P("chan"),
        P("chan", None),
        P("chan"),
        P(None, "chan"),
        P("chan"),
        P("chan"),
    )
    out_specs = (
        P(("grp", "chan"), None),
        P(("grp", "chan"), None),
        P("grp", "chan", None),
        P("chan"),
        P("chan"),
        P("chan", None),
        P("chan"),
        P("chan", None),
        P("chan"),
        P("chan"),
        P("chan"),
        P("chan", None),
        P("chan"),
        P("chan", None),
        P("chan"),
        P(None, "chan"),
        P("chan"),
        P("chan"),
        P("chan"),
        P("chan", None),
        P("chan"),
        P("chan", None),
        P("chan"),
        P("chan"),
        P("chan", None),
        P("chan"),
        P(None, "chan"),
        P("chan"),
        P("chan"),
    )
    return jax.shard_map(body, mesh=mesh, in_specs=in_specs, out_specs=out_specs, check_vma=False)
```

profile of v0, /device:TPU:0, one launch (start us, length us, event | category | flops | bytes accessed | tf_op | source)
XLA Modules:
  0.0 2859.6 jit_solution(17617587613424306633)
XLA Ops:
  16.3 50.7 %multiply_convert_fusion.3 = bf16[2,192,2304]{2,1,0:T(8,128)(2,1)S(1)} fusion(f32[2,192,2304]{2,1,0:T(8,128)S(1)} %get-tuple-element.188, f32[2,2304]{1,0:T(2,128)S(1)} %get-tuple-element.191, f32[192]{0:T(256)S(1)} %bitcast.383, f32[192]{0:T(256)S(1)} %bitcast.381, f32[192]{0:T(256)S(1)} %bitcast.403, f32[192]{0:T(256)S(1)} %bitcast.401, f32[192]{0:T(256)} %bitcast.55, ...), kind=kLoop, calls=%fused_computation.259 | loop fusion | flops 131825664 | bytes 5429760 | tf_op jit(solution)/shard_map/convert_element_type | solution.py:265
  84.8 6.4 select_bitcast_fusion
  92.8 7.6 all-to-all-start.1
  103.6 59.3 %all-to-all-done.1 = bf16[8,192,576]{2,1,0:T(8,128)(2,1)S(1)} async-done(((bf16[8,192,576]{2,1,0:T(8,128)(2,1)}), bf16[8,192,576]{2,1,0:T(8,128)(2,1)S(1)}, u32[]{:S(2)}, u32[]{:S(2)}) %all-to-all-start.1) | async-done | bytes 1769504 | tf_op jit(solution)/shard_map/all_to_all | solution.py:267
  162.8 5.7 all-to-all-start
  171.8 61.3 %all-gather.3 = bf16[8,1,128]{2,1,0:T(2,128)(2,1)S(1)} all-gather(bf16[1,1,128]{2,1,0:T(2,128)(2,1)S(1)} %bitcast.468), channel_id=1, replica_groups=mesh['grp'=4,'chan'=8] {'chan'}, dimensions={0}, use_global_device_ids=true | all-gather | bytes 2304 | tf_op jit(solution)/shard_map/all_gather | solution.py:247
  236.0 56.4 %all-reduce.132 = (bf16[1536]{0:T(1024)(128)(2,1)S(1)}, bf16[1536]{0:T(1024)(128)(2,1)S(1)}, bf16[1536]{0:T(1024)(128)(2,1)S(1)}, bf16[1536]{0:T(1024)(128)(2,1)S(1)}) all-reduce(bf16[1536]{0:T(1024)(128)(2,1)S(1)} %dynamic-update-slice.2, bf16[1536]{0:T(1024)(128)(2,1)S(1)} %dynamic-update-slice.1, ...), channel_id=1, replica_groups=mesh['grp'=4,'chan'=8] {'chan'}, use_global_device_ids=true, to_apply=%add.113 | all-reduce | flops 6144 | bytes 24576
  293.6 48.2 %all-gather.2 = bf16[8,1,768]{2,1,0:T(2,128)(2,1)S(1)} all-gather(bf16[1,1,768]{2,1,0:T(2,128)(2,1)S(1)} %reshape.958), channel_id=1, replica_groups=mesh['grp'=4,'chan'=8] {'chan'}, dimensions={0}, use_global_device_ids=true | all-gather | bytes 13824 | tf_op jit(solution)/shard_map/all_gather | solution.py:242
  342.7 24.3 all-gather
  369.0 23.5 all-gather.6
  392.6 28.4 all_gather.74
  441.0 46.3 %multiply_convert_fusion = (bf16[576,6144]{1,0:T(8,128)(2,1)}, f32[576,6144]{1,0:T(8,128)}, f32[576,6144]{1,0:T(8,128)}) fusion(f32[6144]{0:T(1024)} %bitcast.356, bf16[1536,6144]{1,0:T(8,128)(2,1)} %all-gather.20.cloned.1.call-done, f32[1536,576]{0,1:T(8,128)S(1)} %copy.128, f32[1536]{0:T(1024)} %convert_element_type.741, ...), kind=kOutput, calls=%fused_computation.5 | convolution fusion | flops 11109629952 | bytes 57844224 | tf_op jit(solution)/shard_map/dot_general | solution.py:48
  487.3 296.2 %all-gather.22.cloned.1.call-done = bf16[6144,1536]{1,0:T(8,128)(2,1)} async-done(((bf16[768,1536]{1,0:T(8,128)(2,1)}), bf16[6144,1536]{1,0:T(8,128)(2,1)}) %all-gather.22.cloned.1.call-update) | async-done | bytes 18874384 | tf_op jit(solution)/shard_map/all_gather | solution.py:243
  783.6 17.0 convolution_add_fusion.2
  803.3 42.8 %all-gather.24.cloned.1.call-done = bf16[1536,1024]{1,0:T(8,128)(2,1)} async-done(((bf16[192,1024]{1,0:T(8,128)(2,1)}), bf16[1536,1024]{1,0:T(8,128)(2,1)}) %all-gather.24.cloned.1.call-update) | async-done | bytes 3145744 | tf_op jit(solution)/shard_map/all_gather | solution.py:246
  852.7 20.5 all-gather.4
  873.2 16.4 all-gather.5
  889.6 18.4 all-gather.1
  910.0 36.0 %all-gather.26.cloned.1.call-done = bf16[1024,3072]{1,0:T(8,128)(2,1)} async-done(((bf16[128,3072]{1,0:T(8,128)(2,1)}), bf16[1024,3072]{1,0:T(8,128)(2,1)}) %all-gather.26.cloned.1.call-update) | async-done | bytes 6291472 | tf_op jit(solution)/shard_map/all_gather | solution.py:229
  950.7 16.9 collective-permute-done.2
  970.5 55.6 %all-gather.7 = bf16[8,1,128]{2,1,0:T(2,128)(2,1)S(1)} all-gather(bf16[1,1,128]{2,1,0:T(2,128)(2,1)S(1)} %bitcast.473), channel_id=1, replica_groups=mesh['grp'=4,'chan'=8] {'chan'}, dimensions={0}, use_global_device_ids=true | all-gather | bytes 2304 | tf_op jit(solution)/shard_map/all_gather | solution.py:232
  1026.0 16.7 all-gather.8
  1042.7 18.2 all-gather.9
  1060.9 26.6 all-gather.10
  1106.8 31.6 %all-gather.30.cloned.1.call-done = bf16[1024,4096]{1,0:T(8,128)(2,1)} async-done(((bf16[128,4096]{1,0:T(8,128)(2,1)}), bf16[1024,4096]{1,0:T(8,128)(2,1)}) %all-gather.30.cloned.1.call-update) | async-done | bytes 8388624 | tf_op jit(solution)/shard_map/all_gather | solution.py:235
  1138.4 6.4 convolution_add_fusion
  1144.7 118.8 %all-gather.32.cloned.1.call-done = bf16[4096,1024]{1,0:T(8,128)(2,1)} async-done(((bf16[512,1024]{1,0:T(8,128)(2,1)}), bf16[4096,1024]{1,0:T(8,128)(2,1)}) %all-gather.32.cloned.1.call-update) | async-done | bytes 8388624 | tf_op jit(solution)/shard_map/all_gather | solution.py:237
  1263.6 12.4 fusion.186
  1285.0 5.8 fusion.66
  1313.7 27.3 collective-permute-done.4
  1345.3 10.4 collective-permute-done.5
  1357.9 6.0 multiply_reduce_fusion.54
  1389.9 5.8 convolution_convert_fusion.3
  1400.3 5.7 convolution_convert_fusion.2
  1414.9 27.1 fusion.185
  1442.0 21.4 convolution_convert_fusion.1
  1463.9 20.2 convolution_convert_fusion
  1484.2 19.3 fusion.180
  1510.3 8.9 copy.138
  1519.7 13.9 reduce.18
  1533.6 6.8 reshape.1020
  1540.4 5.8 all-to-all-start.2
  1549.5 37.4 %all-gather.11 = bf16[8,1,128]{2,1,0:T(2,128)(2,1)S(1)} all-gather(bf16[1,1,128]{2,1,0:T(2,128)(2,1)S(1)} %bitcast.476), channel_id=1, replica_groups=mesh['grp'=4,'chan'=8] {'chan'}, dimensions={0}, use_global_device_ids=true | all-gather | bytes 2304 | tf_op jit(solution)/shard_map/all_gather | solution.py:238
  1587.0 5.7 fusion.87
  1598.7 56.7 %all-reduce.131 = (bf16[1024]{0:T(1024)(128)(2,1)S(1)}, bf16[1024]{0:T(1024)(128)(2,1)S(1)}, bf16[2048]{0:T(1024)(128)(2,1)S(1)}, bf16[1024]{0:T(1024)(128)(2,1)...) all-reduce(bf16[1024]{0:T(1024)(128)(2,1)S(1)} %copy-done.248, ...), channel_id=2, replica_groups=mesh['grp'=4,'chan'=8] {'chan'}, use_global_device_ids=true, to_apply=%region_18.19.clone | all-reduce | flops 27648 | bytes 110592
  1663.0 5.9 copy.142
  1669.0 12.7 reduce.19
  1692.2 7.5 reshape.1021
  1715.9 20.0 multiply_reduce_fusion.52
  1736.0 18.9 multiply_reduce_fusion.50
  1754.9 20.0 multiply_multiply_fusion.49
  1775.0 18.8 multiply_multiply_fusion.51
  1793.8 20.4 multiply_multiply_fusion.53
  1814.3 18.2 multiply_reduce_fusion.48
  1832.5 65.5 %reduce-scatter.15.cloned.1.call-done = bf16[128,4096]{1,0:T(8,128)(2,1)} async-done(((bf16[1024,4096]{1,0:T(8,128)(2,1)}), bf16[128,4096]{1,0:T(8,128)(2,1)}) %reduce-scatter.15.cloned.1.call-update) | async-done | bytes 1048592 | tf_op jit(solution)/shard_map/reduce_scatter | solution.py:545
  1898.0 152.1 %reduce-scatter.17.cloned.1.call-done = bf16[512,1024]{1,0:T(8,128)(2,1)} async-done(((bf16[4096,1024]{1,0:T(8,128)(2,1)}), bf16[512,1024]{1,0:T(8,128)(2,1)}) %reduce-scatter.17.cloned.1.call-update) | async-done | bytes 1048592 | tf_op jit(solution)/shard_map/reduce_scatter | solution.py:551
  2050.1 316.0 %reduce-scatter.19.cloned.1.call-done = bf16[192,6144]{1,0:T(8,128)(2,1)} async-done(((bf16[1536,6144]{1,0:T(8,128)(2,1)}), bf16[192,6144]{1,0:T(8,128)(2,1)}) %reduce-scatter.19.cloned.1.call-update) | async-done | bytes 2359312 | tf_op jit(solution)/shard_map/reduce_scatter | solution.py:563
  2366.1 315.6 %reduce-scatter.21.cloned.1.call-done = bf16[768,1536]{1,0:T(8,128)(2,1)} async-done(((bf16[6144,1536]{1,0:T(8,128)(2,1)}), bf16[768,1536]{1,0:T(8,128)(2,1)}) %reduce-scatter.21.cloned.1.call-update) | async-done | bytes 2359312 | tf_op jit(solution)/shard_map/reduce_scatter | solution.py:569
  2682.4 16.0 multiply_reduce_fusion.46
  2698.4 7.3 reshape.1023
  2721.1 14.0 all-reduce.133
  2745.6 56.2 %pad_add_fusion = f32[2,192,2598]{2,1,0:T(8,128)S(1)} fusion(f32[2,192,2304]{2,1,0:T(8,128)} %get-tuple-element.206, f32[2,192,2304]{2,1,0:T(8,128)} %get-tuple-element.204, f32[2,192,2304]{2,1,0:T(8,128)} %get-tuple-element.260, f32[2,192,2304]{2,1,0:T(8,128)} %get-tuple-element.235, f32[2,192,2304]{2,1,0:T(8,128)} %get-tuple-element.254, ...), kind=kLoop, calls=%fused_computation.82 | loop fusion | flops 41900544 | bytes 156165120 | tf_op jit(solution)/shard_map/transpose(jvp())/add_any | solution.py:82
  2801.8 11.5 fusion.61
  2813.3 24.4 all-reduce.137.cloned.1.call-done
  (829 shorter events, 263.7 us)
Async XLA Ops:
  7.2 433.8 %all-gather.20.cloned.1.call-start = ((), (), s32[]{:S(2)}) async-start(), calls=%async_computation.12 | async-start | bytes 21233664 | tf_op jit(solution)/shard_map/all_gather | solution.py:241
  8.0 775.6 %all-gather.22.cloned.1.call-start = ((), (), s32[]{:S(2)}) async-start(), calls=%async_computation.13 | async-start | bytes 21233664 | tf_op jit(solution)/shard_map/all_gather | solution.py:243
  8.7 837.5 %all-gather.24.cloned.1.call-start = ((), (), s32[]{:S(2)}) async-start(), calls=%async_computation.14 | async-start | bytes 3538944 | tf_op jit(solution)/shard_map/all_gather | solution.py:246
  9.4 936.6 %all-gather.26.cloned.1.call-start = ((), (), s32[]{:S(2)}) async-start(), calls=%async_computation.15 | async-start | bytes 7077888 | tf_op jit(solution)/shard_map/all_gather | solution.py:229
  10.0 1094.1 %all-gather.28.cloned.1.call-start = ((), (), s32[]{:S(2)}) async-start(), calls=%async_computation.16 | async-start | bytes 2359296 | tf_op jit(solution)/shard_map/all_gather | solution.py:231
  10.6 1127.8 %all-gather.30.cloned.1.call-start = ((), (), s32[]{:S(2)}) async-start(), calls=%async_computation.17 | async-start | bytes 9437184 | tf_op jit(solution)/shard_map/all_gather | solution.py:235
  84.0 85.5 %copy-start.185 = (pred[2]{0:T(512)(128)(4,1)}, pred[2]{0:T(512)(128)(4,1)S(1)}, u32[]{:S(2)}) copy-start(pred[2]{0:T(512)(128)(4,1)S(1)} %get-tuple-element.336) | copy-start | bytes 10
  84.0 85.7 %copy-start.187 = (pred[2]{0:T(512)(128)(4,1)}, pred[2]{0:T(512)(128)(4,1)S(1)}, u32[]{:S(2)}) copy-start(pred[2]{0:T(512)(128)(4,1)S(1)} %get-tuple-element.337) | copy-start | bytes 10
  84.0 87.0 %copy-start.189 = (pred[2]{0:T(512)(128)(4,1)}, pred[2]{0:T(512)(128)(4,1)S(1)}, u32[]{:S(2)}) copy-start(pred[2]{0:T(512)(128)(4,1)S(1)} %get-tuple-element.338) | copy-start | bytes 10
  92.8 70.0 %all-to-all-start.1 = ((bf16[8,192,576]{2,1,0:T(8,128)(2,1)}), bf16[8,192,576]{2,1,0:T(8,128)(2,1)S(1)}, u32[]{:S(2)}, u32[]{:S(2)}) async-start(bf16[8,192,576]{2,1,0:T(8,128)(2,1)} %bitcast.302), calls=%async_computation.1 | async-start | bytes 3932160 | tf_op jit(solution)/shard_map/all_to_all | solution.py:267
  100.4 69.0 %copy-start.127 = (s32[2,2304]{1,0:T(2,128)S(1)}, s32[2,2304]{1,0:T(2,128)}, u32[]{:S(2)}) copy-start(s32[2,2304]{1,0:T(2,128)} %param.34) | copy-start | bytes 55300
  103.5 66.0 %copy-start.261 = (bf16[256]{0:T(256)(128)(2,1)S(1)}, bf16[256]{0:T(256)(128)(2,1)}, u32[]{:S(2)}) copy-start(bf16[256]{0:T(256)(128)(2,1)} %param.39) | copy-start | bytes 1540
  103.5 68.3 %copy-start.247 = (bf16[768]{0:T(1024)(128)(2,1)S(1)}, bf16[768]{0:T(1024)(128)(2,1)}, u32[]{:S(2)}) copy-start(bf16[768]{0:T(1024)(128)(2,1)} %param.53) | copy-start | bytes 4612
  103.5 68.3 %copy-start.251 = (bf16[128]{0:T(256)(128)(2,1)S(1)}, bf16[128]{0:T(256)(128)(2,1)}, u32[]{:S(2)}) copy-start(bf16[128]{0:T(256)(128)(2,1)} %param.58) | copy-start | bytes 772
  103.5 130.2 %copy-start.246 = (u32[32]{0:T(128)S(1)}, u32[32]{0:T(128)}, u32[]{:S(2)}) copy-start(u32[32]{0:T(128)} %constant.521) | copy-start | bytes 388
  103.5 131.5 %copy-start.262 = (bf16[192]{0:T(256)(128)(2,1)S(1)}, bf16[192]{0:T(256)(128)(2,1)}, u32[]{:S(2)}) copy-start(bf16[192]{0:T(256)(128)(2,1)} %param.55) | copy-start | bytes 1156
  103.5 131.7 %copy-start.263 = (bf16[192]{0:T(256)(128)(2,1)S(1)}, bf16[192]{0:T(256)(128)(2,1)}, u32[]{:S(2)}) copy-start(bf16[192]{0:T(256)(128)(2,1)} %param.50) | copy-start | bytes 1156
  103.5 132.0 %copy-start.264 = (bf16[192]{0:T(256)(128)(2,1)S(1)}, bf16[192]{0:T(256)(128)(2,1)}, u32[]{:S(2)}) copy-start(bf16[192]{0:T(256)(128)(2,1)} %param.51) | copy-start | bytes 1156
  103.5 132.2 %copy-start.265 = (bf16[192]{0:T(256)(128)(2,1)S(1)}, bf16[192]{0:T(256)(128)(2,1)}, u32[]{:S(2)}) copy-start(bf16[192]{0:T(256)(128)(2,1)} %param.56) | copy-start | bytes 1156
  103.5 239.2 %copy-start.252 = (bf16[128]{0:T(256)(128)(2,1)S(1)}, bf16[128]{0:T(256)(128)(2,1)}, u32[]{:S(2)}) copy-start(bf16[128]{0:T(256)(128)(2,1)} %param.61) | copy-start | bytes 772
  103.5 289.0 %copy-start.238 = (bf16[9,128]{1,0:T(8,128)(2,1)S(1)}, bf16[9,128]{1,0:T(8,128)(2,1)}, u32[]{:S(2)}) copy-start(bf16[9,128]{1,0:T(8,128)(2,1)} %param.59) | copy-start | bytes 6916
  103.5 317.4 %copy-start.245 = (s32[2]{0:T(128)S(1)}, s32[2]{0:T(128)}, u32[]{:S(2)}) copy-start(s32[2]{0:T(128)} %param.33) | copy-start | bytes 28
  162.8 263.2 %copy-start.20 = (bf16[8,192,576]{2,1,0:T(8,128)(2,1)}, bf16[8,192,576]{2,1,0:T(8,128)(2,1)S(1)}, u32[]{:S(2)}) copy-start(bf16[8,192,576]{2,1,0:T(8,128)(2,1)S(1)} %all-to-all-done.1) | copy-start | bytes 5308420
  162.8 263.8 %all-to-all-start = ((bf16[8,192,576]{2,1,0:T(8,128)(2,1)}), bf16[8,192,576]{2,1,0:T(8,128)(2,1)}, u32[]{:S(2)}, u32[]{:S(2)}) async-start(bf16[8,192,576]{2,1,0:T(8,128)(2,1)} %bitcast.301), calls=%async_computation | async-start | bytes 3932160 | tf_op jit(solution)/shard_map/all_to_all | solution.py:270
  168.6 1095.0 %all-gather.32.cloned.1.call-start = ((), (), s32[]{:S(2)}) async-start(), calls=%async_computation.18 | async-start | bytes 9437184 | tf_op jit(solution)/shard_map/all_gather | solution.py:237
  169.3 1423.6 %reduce-scatter.25.cloned.1.call-start = ((), (), s32[]{:S(2)}) async-start(), calls=%async_computation.26 | async-start | bytes 294912
  293.0 148.0 %copy-start.81 = (f32[1536]{0:T(1024)}, f32[1536]{0:T(1024)S(1)}, u32[]{:S(2)}) copy-start(f32[1536]{0:T(1024)S(1)} %convert_element_type.740) | copy-start | bytes 18436
  293.0 507.6 %copy-start.79 = (f32[1536]{0:T(1024)}, f32[1536]{0:T(1024)S(1)}, u32[]{:S(2)}) copy-start(f32[1536]{0:T(1024)S(1)} %convert_element_type.726) | copy-start | bytes 18436
  803.2 70.0 %copy-start.254 = (bf16[128]{0:T(256)(128)(2,1)S(1)}, bf16[128]{0:T(256)(128)(2,1)}, u32[]{:S(2)}) copy-start(bf16[128]{0:T(256)(128)(2,1)} %param.37) | copy-start | bytes 772
  803.2 86.3 %copy-start.255 = (bf16[128]{0:T(256)(128)(2,1)S(1)}, bf16[128]{0:T(256)(128)(2,1)}, u32[]{:S(2)}) copy-start(bf16[128]{0:T(256)(128)(2,1)} %param.60) | copy-start | bytes 772
  803.3 104.9 %copy-start.105 = (f32[1,1024]{1,0:T(1,128)S(1)}, f32[1,1024]{1,0:T(1,128)}, u32[]{:S(2)}) copy-start(f32[1,1024]{1,0:T(1,128)} %get-tuple-element.270) | copy-start | bytes 12292
  803.3 104.9 %copy-start.107 = (f32[1,1024]{1,0:T(1,128)S(1)}, f32[1,1024]{1,0:T(1,128)}, u32[]{:S(2)}) copy-start(f32[1,1024]{1,0:T(1,128)} %get-tuple-element.271) | copy-start | bytes 12292
  803.3 104.9 %copy-start.109 = (f32[1,1024]{1,0:T(1,128)S(1)}, f32[1,1024]{1,0:T(1,128)}, u32[]{:S(2)}) copy-start(f32[1,1024]{1,0:T(1,128)} %get-tuple-element.272) | copy-start | bytes 12292
  803.3 104.9 %copy-start.111 = (f32[1,1024]{1,0:T(1,128)S(1)}, f32[1,1024]{1,0:T(1,128)}, u32[]{:S(2)}) copy-start(f32[1,1024]{1,0:T(1,128)} %get-tuple-element.273) | copy-start | bytes 12292
  803.3 104.9 %copy-start.113 = (f32[1,1024]{1,0:T(1,128)S(1)}, f32[1,1024]{1,0:T(1,128)}, u32[]{:S(2)}) copy-start(f32[1,1024]{1,0:T(1,128)} %get-tuple-element.274) | copy-start | bytes 12292
  803.3 104.9 %copy-start.115 = (f32[1,1024]{1,0:T(1,128)S(1)}, f32[1,1024]{1,0:T(1,128)}, u32[]{:S(2)}) copy-start(f32[1,1024]{1,0:T(1,128)} %get-tuple-element.275) | copy-start | bytes 12292
  803.3 104.9 %copy-start.117 = (f32[1,1024]{1,0:T(1,128)S(1)}, f32[1,1024]{1,0:T(1,128)}, u32[]{:S(2)}) copy-start(f32[1,1024]{1,0:T(1,128)} %get-tuple-element.276) | copy-start | bytes 12292
  803.3 104.9 %copy-start.119 = (f32[1,1024]{1,0:T(1,128)S(1)}, f32[1,1024]{1,0:T(1,128)}, u32[]{:S(2)}) copy-start(f32[1,1024]{1,0:T(1,128)} %get-tuple-element.277) | copy-start | bytes 12292
  803.3 104.9 %copy-start.121 = (f32[1,1024]{1,0:T(1,128)S(1)}, f32[1,1024]{1,0:T(1,128)}, u32[]{:S(2)}) copy-start(f32[1,1024]{1,0:T(1,128)} %get-tuple-element.278) | copy-start | bytes 12292
  848.7 59.2 %collective-permute-start = (bf16[1,24,1024]{2,1,0:T(8,128)(2,1)S(1)}, bf16[1,24,1024]{2,1,0:T(8,128)(2,1)S(1)}, u32[]{:S(2)}, u32[]{:S(2)}) collective-permute-start(bf16[1,24,1024]{2,1,0:T(8,128)(2,1)S(1)} %get-tuple-element.268), channel_id=1, source_target_pairs={{0,1},{1,2},{2,3},{3,4},{4,5},{5,6},{6,7},{8,9},{9,10},{10,11},{11... | collective-permute-start | bytes 147464 | tf_op jit(solution)/shard_map/ppermute | solution.py:25
  851.3 56.6 %collective-permute-start.1 = (bf16[1,24,1024]{2,1,0:T(8,128)(2,1)S(1)}, bf16[1,24,1024]{2,1,0:T(8,128)(2,1)S(1)}, u32[]{:S(2)}, u32[]{:S(2)}) collective-permute-start(bf16[1,24,1024]{2,1,0:T(8,128)(2,1)S(1)} %get-tuple-element.269), channel_id=1, source_target_pairs={{1,0},{2,1},{3,2},{4,3},{5,4},{6,5},{7,6},{9,8},{10,9},{11,10},{12... | collective-permute-start | bytes 147464 | tf_op jit(solution)/shard_map/ppermute | solution.py:25
  909.7 194.4 %copy-start.10 = (f32[144,1024]{1,0:T(8,128)}, f32[144,1024]{1,0:T(8,128)S(1)}, u32[]{:S(2)}) copy-start(f32[144,1024]{1,0:T(8,128)S(1)} %get-tuple-element.185) | copy-start | bytes 1769476
  950.1 76.0 %copy-start.257 = (bf16[128]{0:T(256)(128)(2,1)S(1)}, bf16[128]{0:T(256)(128)(2,1)}, u32[]{:S(2)}) copy-start(bf16[128]{0:T(256)(128)(2,1)} %param.42) | copy-start | bytes 772
  950.1 92.7 %copy-start.258 = (bf16[128]{0:T(256)(128)(2,1)S(1)}, bf16[128]{0:T(256)(128)(2,1)}, u32[]{:S(2)}) copy-start(bf16[128]{0:T(256)(128)(2,1)} %param.43) | copy-start | bytes 772
  950.1 17.5 collective-permute-start.2
  970.4 117.3 %collective-permute-start.3 = (bf16[288,2048]{1,0:T(8,128)(2,1)}, bf16[288,2048]{1,0:T(8,128)(2,1)}, u32[]{:S(2)}, u32[]{:S(2)}) collective-permute-start(bf16[288,2048]{1,0:T(8,128)(2,1)} %maximum_select_fusion.1), channel_id=1, source_target_pairs={{0,2},{1,3},{2,0},{3,1},{4,6},{5,7},{6,4},{7,5},{8,10},{9,11},{10,... | collective-permute-start | bytes 3538952 | tf_op jit(solution)/shard_map/ppermute | solution.py:19
  1106.5 282.4 %copy-start.7 = (f32[144,1024]{1,0:T(8,128)}, f32[144,1024]{1,0:T(8,128)S(1)}, u32[]{:S(2)}) copy-start(f32[144,1024]{1,0:T(8,128)S(1)} %get-tuple-element.343) | copy-start | bytes 1769476
  1106.5 173.0 %copy-start.97 = (f32[144]{0:T(256)}, f32[144]{0:T(256)S(1)}, u32[]{:S(2)}) copy-start(f32[144]{0:T(256)S(1)} %broadcast_multiply_fusion.1) | copy-start | bytes 1732
  1106.8 172.8 %copy-start.99 = (f32[144]{0:T(256)}, f32[144]{0:T(256)S(1)}, u32[]{:S(2)}) copy-start(f32[144]{0:T(256)S(1)} %fusion.171) | copy-start | bytes 1732
  1138.4 125.2 %copy-start.49 = (bf16[144,1024]{1,0:T(8,128)(2,1)S(1)}, bf16[144,1024]{1,0:T(8,128)(2,1)}, u32[]{:S(2)}) copy-start(bf16[144,1024]{1,0:T(8,128)(2,1)} %param.35) | copy-start | bytes 884740
  1313.6 27.4 collective-permute-start.4
  1341.9 13.9 collective-permute-start.5
  1368.3 464.2 %reduce-scatter.13.cloned.1.call-start = ((), (), s32[]{:S(2)}) async-start(), calls=%async_computation.20 | async-start | bytes 2359296 | tf_op jit(solution)/shard_map/reduce_scatter | solution.py:533
  1371.5 461.0 %reduce-scatter.23.cloned.1.call-start = ((), (), s32[]{:S(2)}) async-start(), calls=%async_computation.25 | async-start | bytes 3538944 | tf_op jit(solution)/shard_map/reduce_scatter | solution.py:578
  1371.5 4.2 collective-permute-start.6
  1374.0 6.0 collective-permute-start.7
  1384.0 448.5 %reduce-scatter.11.cloned.1.call-start = ((), (), s32[]{:S(2)}) async-start(), calls=%async_computation.19 | async-start | bytes 7077888 | tf_op jit(solution)/shard_map/reduce_scatter | solution.py:527
  1388.7 509.3 %reduce-scatter.15.cloned.1.call-start = ((), (), s32[]{:S(2)}) async-start(), calls=%async_computation.21 | async-start | bytes 9437184 | tf_op jit(solution)/shard_map/reduce_scatter | solution.py:545
  1395.7 654.4 %reduce-scatter.17.cloned.1.call-start = ((), (), s32[]{:S(2)}) async-start(), calls=%async_computation.22 | async-start | bytes 9437184 | tf_op jit(solution)/shard_map/reduce_scatter | solution.py:551
  1406.1 960.0 %reduce-scatter.19.cloned.1.call-start = ((), (), s32[]{:S(2)}) async-start(), calls=%async_computation.23 | async-start | bytes 21233664 | tf_op jit(solution)/shard_map/reduce_scatter | solution.py:563
  1463.5 1218.2 %reduce-scatter.21.cloned.1.call-start = ((), (), s32[]{:S(2)}) async-start(), calls=%async_computation.24 | async-start | bytes 21233664 | tf_op jit(solution)/shard_map/reduce_scatter | solution.py:569
  1540.4 147.3 %all-to-all-start.2 = ((bf16[8,2,55296]{2,1,0:T(2,128)(2,1)}), bf16[8,2,55296]{2,1,0:T(2,128)(2,1)}, u32[]{:S(2)}, u32[]{:S(2)}) async-start(bf16[8,2,55296]{2,1,0:T(2,128)(2,1)} %reshape.1020), calls=%async_computation.2 | async-start | bytes 3538944 | tf_op jit(solution)/shard_map/all_to_all | solution.py:475
  1687.8 1010.6 %all-to-all-start.3 = ((bf16[8,2,55296]{2,1,0:T(2,128)(2,1)}), bf16[8,2,55296]{2,1,0:T(2,128)(2,1)}, u32[]{:S(2)}, u32[]{:S(2)}) async-start(bf16[8,2,55296]{2,1,0:T(2,128)(2,1)} %reshape.1022), calls=%async_computation.3 | async-start | bytes 3538944 | tf_op jit(solution)/shard_map/all_to_all | solution.py:482
  1692.2 1145.5 %all-reduce.137.cloned.1.call-start = ((), (), s32[]{:S(2)}) async-start(), calls=%async_computation.27 | async-start | bytes 16515072 | tf_op jit(solution)/shard_map/psum | solution.py:597
  (234 other events, 4570.6 us)
Sparse Core Ops, SparseCore 0:
  9.6 409.8 all-gather.19
  421.0 362.4 all-gather.21
  785.7 60.4 all-gather.23
  848.2 97.7 all-gather.25
  948.0 61.2 all-gather.27
  1011.3 127.0 all-gather.29
  1140.5 123.0 all-gather.31
  1368.5 60.5 reduce-scatter.24
  1433.2 66.9 reduce-scatter.12
  1503.6 93.0 reduce-scatter.22
  1600.3 146.9 reduce-scatter.10
  1750.7 147.2 reduce-scatter.14
  1902.1 147.9 reduce-scatter.16
  2053.8 312.2 reduce-scatter.18
  2369.8 311.8 reduce-scatter.20
  2684.8 152.7 all-reduce.136
where the time goes:
time: 2870 us; the launch traced here: 2860 us
  waiting for transfers between devices  1520 us (53%)
  blocking collectives  523 us (18%)
  other arithmetic  364 us (13%)
  matrix products  244 us (9%)
  local copies, waits for them, and re-layouts  152 us (5%)
  starting transfers between devices  33.6 us (1%)
    reduce_scatter x1, waiting for transfers between devices, body(): lax.psum_scatter(full_grads[14].astype(jnp.bfloat16), 'chan', scatter_dim...  316 us
    reduce_scatter x1, waiting for transfers between devices, body(): lax.psum_scatter(full_grads[16].astype(jnp.bfloat16), 'chan', scatter_dim...  316 us
    all_gather x1, waiting for transfers between devices, body(): lax.all_gather(pw2_weight, 'chan', axis=0, tiled=True)  296 us
    reduce_scatter x1, waiting for transfers between devices, body(): lax.psum_scatter(full_grads[10].astype(jnp.bfloat16), 'chan', scatter_dim...  152 us
    all_gather x1, waiting for transfers between devices, body(): lax.all_gather(fc2_weight, 'chan', axis=0, tiled=True)  119 us
    unnamed x2, blocking collectives  113 us
    dot_general x8, matrix products, matmul(): return jnp.dot(left, right, preferred_element_type=jnp.float32)  85.1 us
    reduce_sum x4, other arithmetic, depthwise(): kernel_taps[row_step * KERNEL + col_step][None, :, None]  73.2 us
  transfers between devices with their start and end apart: 28, of which 16 were waited for; matrix products, arithmetic and copies ran while one was open for 23% of the time, Pallas kernels for 0%

commit v1 on v0

v1 whole, which is shorter than its diff:
```python
from functools import partial
from types import SimpleNamespace
from typing import Any, NamedTuple

import jax
import jax.numpy as jnp
from jax import lax
from jax.experimental import pallas as pl
from jax.experimental.pallas import tpu as pltpu
from jax.sharding import PartitionSpec as P

D = 1024
HEADS = 16
HEAD_DIM = 64
KERNEL = 7
GRID = 24
BANDS = 4
SIDE = 2 * GRID
CELLS = SIDE * SIDE
BAND_CELLS = CELLS // BANDS
ROWS = GRID // BANDS
TOKENS = ROWS * GRID
PAIR = 1

EPS_VIT = 1e-05
EPS_CONV = 1e-06

CHAN = "chan"
GRP = "grp"

f32 = jnp.float32
bf16 = jnp.bfloat16


def flip(value, axis, bit):
    return lax.ppermute(value, axis, [(i, i ^ (1 << bit)) for i in range(lax.axis_size(axis))])


def bit_at(axis, bit):
    return (lax.axis_index(axis) >> bit) & 1


def shifted(value, axis, steps):
    count = lax.axis_size(axis)
    first, last = (max(0, -steps), min(count, count - steps))
    return lax.ppermute(value, axis, [(source, source + steps) for source in range(first, last)])


def count_bits(axis):
    return lax.axis_size(axis).bit_length() - 1


def reorder(pieces, axis=GRP):
    for bit in range(count_bits(axis)):
        swap = bit_at(axis, bit) == 1
        pieces = [
            jnp.where(swap, pieces[place ^ (1 << bit)], pieces[place])
            for place in range(len(pieces))
        ]
    return pieces


def chan_merge(own, got, bit):
    upper = bit_at(CHAN, bit) == 1
    both = jnp.stack([jnp.where(upper, got, own), jnp.where(upper, own, got)], axis=1)
    return both.reshape((2 * own.shape[0],) + own.shape[1:])


def gather(block, plan):
    pieces = {0: block[None]}
    for axis, bit in plan:
        got = yield {place: flip(piece, axis, bit) for place, piece in pieces.items()}
        if axis == CHAN:
            pieces = {place: chan_merge(pieces[place], got[place], bit) for place in pieces}
        else:
            pieces.update({place ^ (1 << bit): piece for place, piece in got.items()})
    return {
        place: piece.reshape((-1,) + piece.shape[2:]) for place, piece in sorted(pieces.items())
    }


def flip_crosswise(value, swapped):
    groups, parts = lax.axis_size(GRP), lax.axis_size(CHAN)
    pairs = []
    for member in range(groups):
        for place in range(parts):
            other = (member, place ^ 1) if member % 2 == swapped else (member ^ 1 << PAIR, place)
            pairs.append((member * parts + place, other[0] * parts + other[1]))
    return lax.ppermute(value, (GRP, CHAN), pairs)


def gather_crosswise(block, plan):
    own = block[None]
    for axis, bit in plan:
        if axis == CHAN and bit > 0:
            got = yield flip(own, axis, bit)
            own = chan_merge(own, got, bit)
    first = yield flip_crosswise(own, 0)
    second = yield (flip_crosswise(own, 1), flip_crosswise(first, 1))
    even = lax.axis_index(GRP) % 2 == 0
    beside = jnp.where(even, first, second[0])
    across = jnp.where(even, second[0], first)
    pieces = {0: chan_merge(own, beside, 0), 1 << PAIR: chan_merge(across, second[1], 0)}
    for axis, bit in plan:
        if axis == GRP and bit != PAIR:
            got = yield {place: flip(piece, axis, bit) for place, piece in pieces.items()}
            pieces.update({place ^ (1 << bit): piece for place, piece in got.items()})
    return {
        place: piece.reshape((-1,) + piece.shape[2:]) for place, piece in sorted(pieces.items())
    }


class Flow:
    def __init__(self, steps):
        self.steps = steps
        self.pending = next(steps)
        self.result = None

    def advance(self, got):
        try:
            self.pending = self.steps.send(got)
        except StopIteration as stop:
            self.pending, self.result = None, stop.value

    def finish(self):
        while self.pending is not None:
            self.advance(self.pending)
        return self.result


def sync(value, *flows):
    flows = [flow for flow in flows if flow.pending is not None]
    value, arrived = lax.optimization_barrier((value, [flow.pending for flow in flows]))
    for flow, got in zip(flows, arrived):
        flow.advance(got)
    return value


def added(left, right):
    return (left.astype(f32) + right.astype(f32)).astype(left.dtype)


def scatter_sum(pieces, plan):
    parts = lax.axis_size(CHAN)
    pieces = {
        place: piece.reshape((parts, piece.shape[0] // parts) + piece.shape[1:])
        for place, piece in pieces.items()
    }
    for axis, bit in reversed(plan):
        if axis == CHAN:
            mine = bit_at(CHAN, bit)
            kept, sent = {}, {}
            for place, piece in pieces.items():
                halves = piece.reshape((piece.shape[0] // 2, 2) + piece.shape[1:])
                kept[place] = lax.dynamic_index_in_dim(halves, mine, 1, keepdims=False)
                sent[place] = lax.dynamic_index_in_dim(halves, 1 - mine, 1, keepdims=False)
        else:
            kept = {place: piece for place, piece in pieces.items() if not place >> bit & 1}
            sent = {place: pieces[place ^ (1 << bit)] for place in kept}
        got = yield {place: flip(piece, axis, bit) for place, piece in sent.items()}
        pieces = {place: added(kept[place], got[place]) for place in kept}
    return pieces[0][0]


def halve(piece, bit):
    mine = bit_at(CHAN, bit)
    halves = piece.reshape((piece.shape[0] // 2, 2) + piece.shape[1:])
    return [lax.dynamic_index_in_dim(halves, i, 1, keepdims=False) for i in (mine, 1 - mine)]


def crosswise_sum(pieces, plan):
    parts = lax.axis_size(CHAN)
    pieces = {
        place: piece.reshape((parts, piece.shape[0] // parts) + piece.shape[1:])
        for place, piece in pieces.items()
    }
    for axis, bit in reversed(plan):
        if axis == GRP and bit != PAIR:
            kept = {place: piece for place, piece in pieces.items() if not place >> bit & 1}
            sent = {place: pieces[place ^ (1 << bit)] for place in kept}
            got = yield {place: flip(piece, axis, bit) for place, piece in sent.items()}
            pieces = {place: added(kept[place], got[place]) for place in kept}
    even = lax.axis_index(GRP) % 2 == 0
    own, beside = halve(pieces[0], 0)
    across, far = halve(pieces[1 << PAIR], 0)
    got = yield (
        flip_crosswise(jnp.where(even, across, beside), 1),
        flip_crosswise(far, 1),
    )
    own = added(own, got[0])
    other = added(jnp.where(even, beside, across), got[1])
    got = yield flip_crosswise(other, 0)
    own = added(own, got)
    for axis, bit in reversed(plan):
        if axis == CHAN and bit > 0:
            kept, sent = halve(own, bit)
            got = yield flip(sent, axis, bit)
            own = added(kept, got)
    return own[0]


def scatter_and_spread(pieces, plan, sums=scatter_sum):
    block = yield from sums(pieces, plan)
    pieces = {0: lax.optimization_barrier(block)}
    for bit in reversed(range(count_bits(GRP))):
        got = yield {place: flip(piece, GRP, bit) for place, piece in pieces.items()}
        pieces.update({place ^ (1 << bit): piece for place, piece in got.items()})
    return [pieces[place] for place in range(len(pieces))]


def total_sum(bundle, plan):
    total = yield from scatter_sum({0: bundle}, [step for step in plan if step[0] == CHAN])
    for axis, bit in plan:
        if axis == GRP:
            got = yield flip(total, axis, bit)
            total = total + got
    return total


def my_part(value, dim):
    return lax.dynamic_index_in_dim(value, lax.axis_index(GRP), dim, keepdims=False)


def pick(pieces, index):
    for bit in range(len(pieces).bit_length() - 1):
        odd = (index >> bit) & 1 == 1
        pieces = [
            jnp.where(odd, pieces[2 * i + 1], pieces[2 * i]) for i in range(len(pieces) // 2)
        ]
    return pieces[0]


def band_exchange(pieces):
    band = lax.axis_index(CHAN) % BANDS
    count = lax.axis_size(CHAN)
    received = [pick(pieces, band)]
    for apart in range(1, BANDS):
        sent = pick(pieces, band ^ apart)
        received.append(lax.ppermute(sent, CHAN, [(i, i ^ apart) for i in range(count)]))
    return received


def band_return(received):
    band = lax.axis_index(CHAN) % BANDS
    count = lax.axis_size(CHAN)
    back = [received[0]]
    for apart in range(1, BANDS):
        back.append(lax.ppermute(received[apart], CHAN, [(i, i ^ apart) for i in range(count)]))
    return [pick(back, place ^ band) for place in range(BANDS)]


def all_to_all(value):
    return lax.all_to_all(value, CHAN, split_axis=0, concat_axis=0, tiled=True)


def layer_norm(inputs, gain, shift_term, epsilon):
    mean_row = jnp.mean(inputs, axis=-1, keepdims=True)
    centred = inputs - mean_row
    variance = jnp.mean(centred * centred, axis=-1, keepdims=True)
    return centred * lax.rsqrt(variance + epsilon) * gain + shift_term


def norm_vit(inputs, gain, shift_term):
    return layer_norm(inputs, gain, shift_term, EPS_VIT)


def gelu_and_slope(inputs):
    below = 0.5 * (1.0 + lax.erf(inputs * (0.5**0.5)))
    slope = below + inputs * jnp.exp(-0.5 * inputs * inputs) * 0.3989422804014327
    return (inputs * below).astype(bf16), slope.astype(bf16)


def matmul(left, right):
    return jnp.dot(left, right, preferred_element_type=f32)


def left_grad(inputs, grads):
    return lax.dot_general(
        inputs, grads, (((0,), (0,)), ((), ())), preferred_element_type=f32
    ).astype(bf16)


def right_grad(grads, weight):
    return lax.dot_general(grads, weight, (((1,), (1,)), ((), ())), preferred_element_type=f32)


def column_sum(grads):
    return jnp.sum(grads.astype(f32), axis=0)


PITCH = SIDE + 8
HALF = KERNEL // 2
FRAME = (SIDE + 2 * HALF) * PITCH + 8
LANES = 128


def frame_at(row, col):
    return pl.multiple_of((row + HALF) * PITCH, 8) + 8 + col


def valid_row(row, sizes):
    cols = lax.broadcasted_iota(jnp.int32, (SIDE, LANES), 0)
    return jnp.where(row < sizes, cols, SIDE) < sizes


def whole(*shape):
    return pl.BlockSpec(shape, lambda *grid: (0,) * len(shape))


def in_smem():
    return pl.BlockSpec(memory_space=pltpu.SMEM)


def band_rows(step, band):
    return pl.ds(pl.multiple_of(step * band, 16), BAND_CELLS)


def convolve_tiles(sizes_ref, taps_ref, bias_ref, maps_ref, cells_ref, masked_ref, turned, framed, first=0):
    framed[...] = jnp.zeros_like(framed)
    for lane in range(0, maps_ref.shape[0], LANES):
        here = slice(first + lane, first + lane + LANES)
        for begin in range(0, CELLS, LANES):
            columns = maps_ref[lane : lane + LANES, begin : begin + LANES]
            turned[begin : begin + LANES] = columns.astype(f32).T
        sizes = sizes_ref[:, here]

        def fill(row, carry):
            cells = pl.ds(pl.multiple_of(row * SIDE, 16), SIDE)
            inner = jnp.where(valid_row(row, sizes), turned[cells], 0.0)
            framed[pl.ds(frame_at(row, 0), SIDE)] = inner
            masked_ref[cells, here] = inner.astype(bf16)
            return carry

        lax.fori_loop(0, SIDE, fill, 0)

        def convolve(row, carry):
            total = jnp.zeros((SIDE, LANES), f32) + bias_ref[:, here]
            for row_step in range(KERNEL):
                for col_step in range(KERNEL):
                    tap = row_step * KERNEL + col_step
                    total = total + taps_ref[tap : tap + 1, here] * framed[
                        pl.ds(frame_at(row + row_step - HALF, col_step - HALF), SIDE)
                    ]
            cells = pl.ds(pl.multiple_of(row * SIDE, 16), SIDE)
            cells_ref[cells, here] = jnp.where(valid_row(row, sizes), total, 0.0).astype(bf16)
            return carry

        lax.fori_loop(0, SIDE, convolve, 0)


def conv_forward_kernel(sizes_ref, taps_ref, bias_ref, maps_ref, cells_ref, masked_ref, turned, framed):
    convolve_tiles(sizes_ref, taps_ref, bias_ref, maps_ref, cells_ref, masked_ref, turned, framed)


def conv_forward_last_kernel(
    step_ref,
    sizes_ref,
    taps_ref,
    bias_ref,
    maps_ref,
    early_cells_ref,
    early_masked_ref,
    conv_ref,
    bands_ref,
    masked_ref,
    turned,
    framed,
    cells_ref,
):
    early, channels = early_cells_ref.shape[1], conv_ref.shape[2]
    cells_ref[:, :early] = early_cells_ref[...]
    masked_ref[:, :early] = early_masked_ref[...]
    convolve_tiles(
        sizes_ref, taps_ref, bias_ref, maps_ref, cells_ref, masked_ref, turned, framed, early
    )
    for image in range(masked_ref.shape[1] // channels):
        here = slice(image * channels, (image + 1) * channels)
        for band in range(BANDS):
            rows = band_rows(step_ref[image], band)
            conv_ref[image * BANDS + band] = cells_ref[rows, here]
            bands_ref[image * BANDS + band] = masked_ref[rows, here]


def conv_backward_kernel(
    step_ref,
    sizes_ref,
    taps_ref,
    masked_ref,
    grad_ref,
    resid_ref,
    *refs,
    first,
):
    (
        out_ref,
        tap_grad_ref,
        framed,
        framed_grad,
        field,
        sums,
        grad_cells,
        resid_cells,
    ) = refs[-8:]
    lanes, channels = masked_ref.shape[1], grad_ref.shape[2]
    framed[...] = jnp.zeros_like(framed)
    framed_grad[...] = jnp.zeros_like(framed_grad)
    grad_cells[...] = jnp.zeros_like(grad_cells)
    resid_cells[...] = jnp.zeros_like(resid_cells)
    for image in range(lanes // channels):
        here = slice(image * channels, (image + 1) * channels)
        for band in range(BANDS):
            rows = band_rows(step_ref[image], band)
            grad_cells[rows, here] = grad_ref[image * BANDS + band]
            resid_cells[rows, here] = resid_ref[image * BANDS + band]

    def in_eights(value):
        return jnp.sum(value.reshape(SIDE // 8, 8, LANES), axis=0)

    for tile in range(0, out_ref.shape[0], LANES):
        here = slice(first + tile, first + tile + LANES)
        block = slice(tile, tile + LANES)
        sums[...] = jnp.zeros_like(sums)
        sizes = sizes_ref[:, here]

        def fill(row, carry):
            cells = pl.ds(pl.multiple_of(row * SIDE, 16), SIDE)
            framed[pl.ds(frame_at(row, 0), SIDE)] = masked_ref[cells, here].astype(f32)
            grads = jnp.where(valid_row(row, sizes), grad_cells[cells, here].astype(f32), 0.0)
            framed_grad[pl.ds(frame_at(row, 0), SIDE)] = grads
            return carry

        lax.fori_loop(0, SIDE, fill, 0)

        def convolve(row, carry):
            cells = pl.ds(pl.multiple_of(row * SIDE, 16), SIDE)
            total = resid_cells[cells, here].astype(f32)
            grads = framed_grad[pl.ds(frame_at(row, 0), SIDE)]
            for row_step in range(KERNEL):
                for col_step in range(KERNEL):
                    tap = row_step * KERNEL + col_step
                    total = total + taps_ref[tap : tap + 1, here] * framed_grad[
                        pl.ds(frame_at(row + HALF - row_step, HALF - col_step), SIDE)
                    ]
                    shifted_in = framed[
                        pl.ds(frame_at(row + row_step - HALF, col_step - HALF), SIDE)
                    ]
                    sums[tap * 8 : tap * 8 + 8] += in_eights(grads * shifted_in)
            last = KERNEL * KERNEL * 8
            sums[last : last + 8] += in_eights(grads)
            field[cells] = jnp.where(valid_row(row, sizes), total, 0.0)
            return carry

        lax.fori_loop(0, SIDE, convolve, 0)
        for begin in range(0, CELLS, LANES):
            out_ref[block, begin : begin + LANES] = field[begin : begin + LANES].T
        for tap in range(KERNEL * KERNEL + 1):
            tap_grad_ref[tap : tap + 1, block] = jnp.sum(
                sums[tap * 8 : tap * 8 + 8], axis=0, keepdims=True
            )


def kernel_call(kernel, name, in_specs, out_shape, scratch_shapes=(), vmem=40):
    return pl.pallas_call(
        kernel,
        grid=(1,),
        in_specs=in_specs,
        out_specs=[whole(*out.shape) for out in out_shape],
        out_shape=out_shape,
        scratch_shapes=list(scratch_shapes),
        compiler_params=pltpu.CompilerParams(vmem_limit_bytes=vmem << 20),
        name=name,
    )


def conv_forward(hires, size_class, taps, bias, between):
    images, channels = hires.shape[:2]
    lanes = images * channels
    maps = hires.reshape(lanes, CELLS)
    sizes = jnp.repeat(size_class, channels)[None]
    lane_taps = jnp.tile(taps.astype(f32), (1, images))
    lane_bias = jnp.tile(bias.astype(f32)[None], (1, images))
    steps = size_class // BANDS * SIDE
    early = max(1, lanes // LANES * 2 // 3) * LANES
    bands = jax.ShapeDtypeStruct((images * BANDS, BAND_CELLS, channels), bf16)
    cells = jax.ShapeDtypeStruct((CELLS, lanes), bf16)
    early_cells = jax.ShapeDtypeStruct((CELLS, early), bf16)
    vectors = [whole(1, lanes), whole(KERNEL * KERNEL, lanes), whole(1, lanes)]
    scratch = [pltpu.VMEM((CELLS, LANES), f32), pltpu.VMEM((FRAME, LANES), f32)]
    given = (sizes, lane_taps, lane_bias)
    done = kernel_call(
        conv_forward_kernel,
        "depthwise_forward",
        vectors + [whole(early, CELLS)],
        [early_cells, early_cells],
        scratch,
    )(*given, maps)
    late = lanes - early
    late_maps = pl.BlockSpec((late, CELLS), lambda i: (early // late, 0))
    conv, masked_bands, masked = kernel_call(
        conv_forward_last_kernel,
        "depthwise_forward_last",
        [in_smem()] + vectors + [late_maps, whole(CELLS, early), whole(CELLS, early)],
        [bands, bands, cells],
        scratch + [pltpu.VMEM((CELLS, lanes), bf16)],
    )(steps, *given, maps, *between(done))
    return conv, masked_bands, (steps, sizes, lane_taps, masked)


def conv_backward(saved, grad_bands, resid_bands, between):
    steps, sizes, lane_taps, masked = saved
    images, lanes, taps = steps.shape[0], sizes.shape[1], KERNEL * KERNEL
    early = max(1, lanes // LANES * 2 // 3) * LANES
    args = [steps, sizes, lane_taps, masked, grad_bands, resid_bands]
    specs = [in_smem(), whole(1, lanes), whole(taps, lanes), whole(CELLS, lanes)]
    specs += [whole(*grad_bands.shape), whole(*resid_bands.shape)]
    tap_grads = []
    for first, count in ((0, early), (early, lanes - early)):
        index = first // count
        field, tap_grad = pl.pallas_call(
            partial(conv_backward_kernel, first=first),
            grid=(1,),
            in_specs=specs,
            out_specs=[
                pl.BlockSpec((count, CELLS), lambda i, index=index: (index, 0)),
                whole(taps + 1, count),
            ],
            out_shape=[
                jax.ShapeDtypeStruct((lanes, CELLS), f32),
                jax.ShapeDtypeStruct((taps + 1, count), f32),
            ],
            input_output_aliases={6: 0} if first else {},
            scratch_shapes=[
                pltpu.VMEM((FRAME, LANES), f32),
                pltpu.VMEM((FRAME, LANES), f32),
                pltpu.VMEM((CELLS, LANES), f32),
                pltpu.VMEM(((taps + 1) * 8, LANES), f32),
                pltpu.VMEM((CELLS, lanes), bf16),
                pltpu.VMEM((CELLS, lanes), bf16),
            ],
            compiler_params=pltpu.CompilerParams(vmem_limit_bytes=40 << 20),
            name="depthwise_backward",
        )(*args)
        tap_grads.append(tap_grad)
        if not first:
            field = between(field)
            args.append(field)
            specs = specs + [pl.BlockSpec(memory_space=pl.ANY)]
    tap_grads = jnp.concatenate(tap_grads, axis=1).reshape(taps + 1, images, -1)
    return field.reshape(images, -1, CELLS), jnp.sum(tap_grads, axis=1)


def shape_of(dtype, *shape):
    return jax.ShapeDtypeStruct(shape, dtype)


def blocks_of(arrays):
    return [whole(*array.shape) for array in arrays]


def split_rows(count):
    return next(rows for rows in (96, 64, 48, 32, 16) if count % rows == 0)


def conv_norm_kernel(blocks_ref, gain_ref, bias_ref, out_ref):
    parts, rows, channels = blocks_ref.shape
    width = parts * channels
    blocks = [blocks_ref[part].astype(f32) for part in range(parts)]
    mean = sum(jnp.sum(block, axis=1, keepdims=True) for block in blocks) / width
    blocks = [block - mean for block in blocks]
    variance = sum(jnp.sum(block * block, axis=1, keepdims=True) for block in blocks) / width
    scale = lax.rsqrt(variance + EPS_CONV)
    for part in range(parts):
        here = slice(part * channels, (part + 1) * channels)
        normed = blocks[part] * scale * gain_ref[:, here] + bias_ref[:, here]
        out_ref[:, here] = normed.astype(bf16)


def conv_norm_forward(blocks, gain, bias):
    parts, cells, channels = blocks.shape
    width, rows = parts * channels, split_rows(cells)
    return pl.pallas_call(
        conv_norm_kernel,
        grid=(cells // rows,),
        in_specs=[
            pl.BlockSpec((parts, rows, channels), lambda i: (0, i, 0)),
            whole(1, width),
            whole(1, width),
        ],
        out_specs=pl.BlockSpec((rows, width), lambda i: (i, 0)),
        out_shape=shape_of(bf16, cells, width),
        compiler_params=pltpu.CompilerParams(vmem_limit_bytes=32 << 20),
        name="conv_norm_forward",
    )(blocks, gain[None], bias[None])


def conv_norm_grad_kernel(blocks_ref, gain_ref, own_ref, other_ref, out_ref, sums_ref):
    parts, rows, channels = blocks_ref.shape
    width = parts * channels

    @pl.when(pl.program_id(0) == 0)
    def _():
        sums_ref[...] = jnp.zeros_like(sums_ref)

    blocks = [blocks_ref[part].astype(f32) for part in range(parts)]
    mean = sum(jnp.sum(block, axis=1, keepdims=True) for block in blocks) / width
    blocks = [block - mean for block in blocks]
    variance = sum(jnp.sum(block * block, axis=1, keepdims=True) for block in blocks) / width
    scale = lax.rsqrt(variance + EPS_CONV)
    grads, mean_grad, mean_both = [], 0.0, 0.0
    for part in range(parts):
        here = slice(part * channels, (part + 1) * channels)
        grad = own_ref[:, here].astype(f32) + other_ref[:, here].astype(f32)
        blocks[part] = blocks[part] * scale
        both = grad * blocks[part]
        sums_ref[0:1, here] += jnp.sum(both, axis=0, keepdims=True)
        sums_ref[1:2, here] += jnp.sum(grad, axis=0, keepdims=True)
        grads.append(grad * gain_ref[:, here])
        mean_grad += jnp.sum(grads[part], axis=1, keepdims=True)
        mean_both += jnp.sum(grads[part] * blocks[part], axis=1, keepdims=True)
    for part in range(parts):
        value = grads[part] - mean_grad / width - blocks[part] * (mean_both / width)
        out_ref[part] = (scale * value).astype(bf16)


def conv_norm_backward(blocks, gain, own, other):
    parts, cells, channels = blocks.shape
    width, rows = parts * channels, split_rows(cells)
    return pl.pallas_call(
        conv_norm_grad_kernel,
        grid=(cells // rows,),
        in_specs=[
            pl.BlockSpec((parts, rows, channels), lambda i: (0, i, 0)),
            whole(1, width),
            pl.BlockSpec((rows, width), lambda i: (i, 0)),
            pl.BlockSpec((rows, width), lambda i: (i, 0)),
        ],
        out_specs=[
            pl.BlockSpec((parts, rows, channels), lambda i: (0, i, 0)),
            whole(2, width),
        ],
        out_shape=[shape_of(bf16, parts, cells, channels), shape_of(f32, 2, width)],
        compiler_params=pltpu.CompilerParams(vmem_limit_bytes=32 << 20),
        name="conv_norm_backward",
    )(blocks, gain[None], own, other)


def dot_nt(left, right):
    return lax.dot_general(left, right, (((1,), (1,)), ((), ())), preferred_element_type=f32)


def dot_tn(left, right):
    return lax.dot_general(left, right, (((0,), (0,)), ((), ())), preferred_element_type=f32)


def head_parts(joined, head, share):
    return [
        joined[:, kind * share + head * HEAD_DIM : kind * share + (head + 1) * HEAD_DIM]
        for kind in range(3)
    ]


def softmax_rows(queries, keys):
    scores = dot_nt(queries, keys) * HEAD_DIM ** (-0.5)
    weights = jnp.exp(scores - jnp.max(scores, axis=1, keepdims=True))
    return weights / jnp.sum(weights, axis=1, keepdims=True)


def attention_kernel(*refs):
    inputs, (context_ref, joined_ref) = refs[:BANDS], refs[BANDS:]
    for band in range(BANDS):
        joined_ref[band * TOKENS : (band + 1) * TOKENS] = inputs[band][...]
    share = context_ref.shape[2]
    for head in range(share // HEAD_DIM):
        queries, keys, values = head_parts(joined_ref, head, share)
        probs = softmax_rows(queries, keys).astype(bf16)
        context = jnp.dot(probs, values, preferred_element_type=f32).astype(bf16)
        for band in range(BANDS):
            context_ref[band, :, head * HEAD_DIM : (head + 1) * HEAD_DIM] = context[
                band * TOKENS : (band + 1) * TOKENS
            ]


def attention(pieces):
    share = pieces[0].shape[1] // 3
    return kernel_call(
        attention_kernel,
        "attention_forward",
        blocks_of(pieces),
        [shape_of(bf16, BANDS, TOKENS, share), shape_of(bf16, BANDS * TOKENS, 3 * share)],
    )(*pieces)


def attention_grad_kernel(joined_ref, *refs):
    inputs, (out_ref, grad_ref, result) = refs[:BANDS], refs[BANDS:]
    for band in range(BANDS):
        grad_ref[band * TOKENS : (band + 1) * TOKENS] = inputs[band][...]
    share = grad_ref.shape[1]
    for head in range(share // HEAD_DIM):
        queries, keys, values = head_parts(joined_ref, head, share)
        grads = grad_ref[:, head * HEAD_DIM : (head + 1) * HEAD_DIM]
        probs = softmax_rows(queries, keys)
        grad_probs = dot_nt(grads, values)
        row_dot = jnp.sum(probs * grad_probs, axis=1, keepdims=True)
        grad_scores = (probs * (grad_probs - row_dot)).astype(bf16)
        scale = HEAD_DIM ** (-0.5)
        parts = (
            jnp.dot(grad_scores, keys, preferred_element_type=f32) * scale,
            dot_tn(grad_scores, queries) * scale,
            dot_tn(probs.astype(bf16), grads),
        )
        for kind, part in enumerate(parts):
            begin = kind * share + head * HEAD_DIM
            result[:, begin : begin + HEAD_DIM] = part.astype(bf16)
    for band in range(BANDS):
        out_ref[band] = result[band * TOKENS : (band + 1) * TOKENS]


def attention_grad(joined, pieces):
    share = pieces[0].shape[1]
    return kernel_call(
        attention_grad_kernel,
        "attention_backward",
        [whole(*joined.shape)] + blocks_of(pieces),
        [shape_of(bf16, BANDS, TOKENS, 3 * share)],
        [
            pltpu.VMEM((BANDS * TOKENS, share), bf16),
            pltpu.VMEM((BANDS * TOKENS, 3 * share), bf16),
        ],
    )(joined, *pieces)[0]


GRID_PITCH = GRID + 8
GRID_FRAME = (ROWS + 2) * GRID_PITCH + 8


def fill_frame(frame_ref, keep_ref, before_ref, inner_ref, after_ref):
    frame_ref[...] = jnp.zeros_like(frame_ref)
    inner = inner_ref[...].astype(f32)
    rows = [before_ref[...].astype(f32) * keep_ref[0].astype(f32)]
    rows += [inner[row * GRID : (row + 1) * GRID] for row in range(ROWS)]
    rows += [after_ref[...].astype(f32) * keep_ref[1].astype(f32)]
    for row, value in enumerate(rows):
        begin = row * GRID_PITCH + 8
        frame_ref[begin : begin + GRID] = value


def frame_row(frame_ref, row, col):
    begin = row * GRID_PITCH + 8 + col
    return frame_ref[begin : begin + GRID]


def vit_norm(value):
    mean = jnp.mean(value, axis=1, keepdims=True)
    centred = value - mean
    variance = jnp.mean(centred * centred, axis=1, keepdims=True)
    scale = lax.rsqrt(variance + EPS_VIT)
    return centred * scale, scale


def mix_kernel(
    keep_ref, before_ref, inner_ref, after_ref, taps_ref, vectors_ref, vit_ref, adapt_ref, mixed_ref, norm_ref, frame
):
    fill_frame(frame, keep_ref, before_ref, inner_ref, after_ref)
    bias, gate_tanh, gain, shift = (vectors_ref[i : i + 1] for i in range(4))
    for row in range(ROWS):
        total = jnp.zeros((GRID, D), f32) + bias
        for row_step in range(3):
            for col_step in range(3):
                tap = row_step * 3 + col_step
                total = total + taps_ref[tap : tap + 1] * frame_row(
                    frame, row + row_step, col_step - 1
                )
        adapt_ref[row * GRID : (row + 1) * GRID] = total
    mixed = vit_ref[...].astype(f32) + gate_tanh * adapt_ref[...]
    mixed_ref[...] = mixed
    norm_ref[...] = (vit_norm(mixed)[0] * gain + shift).astype(bf16)


def mix_forward(keep, before, inner, after, taps, vectors, vit_in):
    return kernel_call(
        mix_kernel,
        "mix_forward",
        [in_smem()] + blocks_of((before, inner, after, taps, vectors, vit_in)),
        [shape_of(f32, TOKENS, D), shape_of(f32, TOKENS, D), shape_of(bf16, TOKENS, D)],
        [pltpu.VMEM((GRID_FRAME, D), f32)],
    )(keep, before, inner, after, taps, vectors, vit_in)


def norm_grad(value, gain, grad):
    xhat, scale = vit_norm(value)
    gained = grad * gain
    back = (
        gained
        - jnp.mean(gained, axis=1, keepdims=True)
        - xhat * jnp.mean(gained * xhat, axis=1, keepdims=True)
    )
    return (
        scale * back,
        jnp.sum(grad * xhat, axis=0, keepdims=True),
        jnp.sum(grad, axis=0, keepdims=True),
    )


def mix_grad_kernel(vectors_ref, grad_ref, mixed_ref, resid_ref, adapt_ref, out_ref, low_ref, sums_ref):
    gate_tanh, gain = vectors_ref[1:2], vectors_ref[2:3]
    back, sums_ref[0:1], sums_ref[1:2] = norm_grad(mixed_ref[...], gain, grad_ref[...])
    vit_grad = resid_ref[...] + back
    out_ref[...] = vit_grad
    low = (gate_tanh * vit_grad).astype(bf16)
    low_ref[...] = low
    gate_sum = jnp.sum(vit_grad * adapt_ref[...], axis=0, keepdims=True)
    sums_ref[2:3] = gate_sum * (1.0 - gate_tanh * gate_tanh)
    sums_ref[3:4] = jnp.sum(low.astype(f32), axis=0, keepdims=True)


def mix_grad(vectors, grad_norm1, mixed, grad_resid, adapt_flat):
    args = (vectors, grad_norm1, mixed, grad_resid, adapt_flat)
    return kernel_call(
        mix_grad_kernel,
        "mix_backward",
        blocks_of(args),
        [shape_of(f32, TOKENS, D), shape_of(bf16, TOKENS, D), shape_of(f32, 4, D)],
    )(*args)


def adapt_grad_kernel(
    keep_ref, before_ref, inner_ref, after_ref, b_ref, i_ref, a_ref, taps_ref, low_ref, sums_ref, frame, frame_in
):
    fill_frame(frame, keep_ref, before_ref, inner_ref, after_ref)
    fill_frame(frame_in, keep_ref, b_ref, i_ref, a_ref)
    tap_sums = [jnp.zeros((GRID, D), f32) for tap in range(9)]
    bias_sum = jnp.zeros((GRID, D), f32)
    rows = []
    for row in range(ROWS):
        grads = frame_row(frame, row + 1, 0)
        total = jnp.zeros((GRID, D), f32)
        for row_step in range(3):
            for col_step in range(3):
                tap = row_step * 3 + col_step
                total = total + taps_ref[tap : tap + 1] * frame_row(
                    frame, row + 2 - row_step, 1 - col_step
                )
                tap_sums[tap] += grads * frame_row(frame_in, row + row_step, col_step - 1)
        rows.append(total)
    low = jnp.concatenate(rows, axis=0).astype(bf16)
    low_ref[...] = low
    for tap in range(9):
        sums_ref[tap : tap + 1] = jnp.sum(tap_sums[tap], axis=0, keepdims=True)
    sums_ref[9:10] = jnp.sum(low.astype(f32), axis=0, keepdims=True)


def adapt_grad(keep, grad_rims, input_rims, taps):
    args = (*grad_rims, *input_rims, taps)
    return kernel_call(
        adapt_grad_kernel,
        "adapter_backward",
        [in_smem()] + blocks_of(args),
        [shape_of(bf16, TOKENS, D), shape_of(f32, 10, D)],
        [pltpu.VMEM((GRID_FRAME, D), f32), pltpu.VMEM((GRID_FRAME, D), f32)],
    )(keep, *args)


def gelu_parts(hidden):
    below = 0.5 * (1.0 + lax.erf(hidden * (0.5**0.5)))
    slope = below + hidden * jnp.exp(-0.5 * hidden * hidden) * 0.3989422804014327
    return hidden * below, slope


def mlp_kernel(
    norm_ref, cot_ref, fc1_ref, bias_ref, fc2_ref, out_in, grad_in, out_ref, grad_ref, g1_ref, gb_ref, g2_ref
):
    @pl.when(pl.program_id(0) == 0)
    def _():
        out_ref[...] = out_in[...]
        grad_ref[...] = grad_in[...]

    norm, cot, fc1, fc2 = norm_ref[...], cot_ref[...], fc1_ref[...], fc2_ref[...]
    hidden = jnp.dot(norm, fc1, preferred_element_type=f32) + bias_ref[...]
    act, slope = gelu_parts(hidden)
    act = act.astype(bf16)
    out_ref[...] += jnp.dot(act, fc2, preferred_element_type=f32)
    grad_hidden = (slope * dot_nt(cot, fc2)).astype(bf16)
    g2_ref[...] = dot_tn(act, cot).astype(bf16)
    g1_ref[...] = dot_tn(norm, grad_hidden).astype(bf16)
    gb_ref[...] = jnp.sum(grad_hidden.astype(f32), axis=0, keepdims=True)
    grad_ref[...] += dot_nt(grad_hidden, fc1)


def mlp_piece(norm, cotangent, fc1, bias, fc2, out_so_far, grad_so_far):
    hidden = fc1.shape[1]
    step = next(size for size in (512, 256, 128) if hidden % size == 0)
    columns = pl.BlockSpec((D, step), lambda i: (0, i))
    down = pl.BlockSpec((step, D), lambda i: (i, 0))
    bias_block = pl.BlockSpec((1, step), lambda i: (0, i))
    tokens = whole(TOKENS, D)
    return pl.pallas_call(
        mlp_kernel,
        grid=(hidden // step,),
        in_specs=[tokens, tokens, columns, bias_block, down, tokens, tokens],
        out_specs=[tokens, tokens, columns, bias_block, down],
        out_shape=[
            shape_of(f32, TOKENS, D),
            shape_of(f32, TOKENS, D),
            shape_of(bf16, D, hidden),
            shape_of(f32, 1, hidden),
            shape_of(bf16, hidden, D),
        ],
        compiler_params=pltpu.CompilerParams(vmem_limit_bytes=40 << 20),
        name="mlp_piece",
    )(norm, cotangent, fc1, bias[None], fc2, out_so_far, grad_so_far)


def pick_columns(weight, parts, groups):
    rows, wide = weight.shape
    width = wide // parts // groups

    def kernel(index_ref, weight_ref, out_ref):
        for index in range(groups):

            @pl.when(index_ref[0] == index)
            def _():
                for part in range(parts):
                    begin = (part * groups + index) * width
                    out_ref[:, part * width : (part + 1) * width] = weight_ref[
                        :, begin : begin + width
                    ]

    return kernel_call(
        kernel, "pick_columns", [in_smem(), whole(rows, wide)], [shape_of(bf16, rows, wide // groups)]
    )(lax.axis_index(GRP)[None], weight)[0]


def place_columns(pieces, parts):
    groups = len(pieces)
    rows, narrow = pieces[0].shape
    width = narrow // parts

    def kernel(index_ref, *refs):
        inputs, out_ref = refs[:groups], refs[groups]
        for index in range(groups):

            @pl.when(index_ref[0] == index)
            def _():
                for place in range(groups):
                    for part in range(parts):
                        begin = (part * groups + (place ^ index)) * width
                        out_ref[:, begin : begin + width] = inputs[place][
                            :, part * width : (part + 1) * width
                        ].astype(f32)

    return kernel_call(
        kernel, "place_columns", [in_smem()] + blocks_of(pieces), [shape_of(f32, rows, narrow * groups)]
    )(lax.axis_index(GRP)[None], *pieces)[0]


def bundle_rows(vectors, parts):
    vectors = [vector.reshape(1, -1) for vector in vectors]
    length = sum(vector.shape[1] for vector in vectors) // parts

    def kernel(*refs):
        inputs, out_ref = refs[:-1], refs[-1]
        begin = 0
        for ref in inputs:
            size = ref.shape[1] // parts
            for part in range(parts):
                out_ref[part : part + 1, begin : begin + size] = ref[
                    :, part * size : (part + 1) * size
                ]
            begin += size

    rows = kernel_call(kernel, "bundle_rows", blocks_of(vectors), [shape_of(f32, parts, length)])(
        *vectors
    )[0]
    return rows.reshape(-1, LANES)


def joint_grads(norm, grad_pieces, context, out_pieces):
    part, count = out_pieces[0].shape[1], len(out_pieces)

    def kernel(norm_ref, context_ref, *refs):
        for place in range(count):
            grads, outs, result = refs[place], refs[count + place], refs[2 * count + place]
            result[:, : 3 * part] = dot_tn(norm_ref[...], grads[...]).astype(bf16)
            result[:, 3 * part :] = dot_tn(context_ref[...], outs[...]).astype(bf16)

    return kernel_call(
        kernel,
        "joint_grads",
        blocks_of((norm, context, *grad_pieces, *out_pieces)),
        [shape_of(bf16, D, 4 * part)] * count,
    )(norm, context, *grad_pieces, *out_pieces)


def side_by_side(vectors):
    vectors = [vector.reshape(1, -1) for vector in vectors]

    def kernel(*refs):
        begin = 0
        for ref in refs[:-1]:
            size = ref.shape[1]
            refs[-1][:, begin : begin + size] = ref[...].astype(f32)
            begin += size

    length = sum(vector.shape[1] for vector in vectors)
    joined = kernel_call(kernel, "side_by_side", blocks_of(vectors), [shape_of(f32, 1, length)])(
        *vectors
    )[0]
    return joined.reshape(-1, LANES)


def band_slices(cells, size_class):
    bands = []
    for image, image_cells in enumerate(cells):
        step = size_class[image] // BANDS * SIDE
        for band in range(BANDS):
            bands.append(lax.dynamic_slice_in_dim(image_cells, band * step, BAND_CELLS, 0))
    return jnp.stack(bands)


def pool_tables(size_class, mask_bands):
    sizes = jnp.repeat(size_class, BANDS)[:, None, None]
    out_ids = lax.broadcasted_iota(jnp.int32, (1, TOKENS, 1), 1)
    out_row, out_col = out_ids // GRID, out_ids % GRID
    cell_ids = lax.broadcasted_iota(jnp.int32, (1, 1, BAND_CELLS), 2)
    cell_row, cell_col = cell_ids // SIDE, cell_ids % SIDE
    row_hit = (out_row * sizes // GRID <= cell_row) & (
        cell_row < ((out_row + 1) * sizes + GRID - 1) // GRID
    )
    col_hit = (out_col * sizes // GRID <= cell_col) & (
        cell_col < ((out_col + 1) * sizes + GRID - 1) // GRID
    )
    return jnp.where(row_hit & col_hit, mask_bands[:, None, :], 0).astype(bf16)


def batched(left, right, left_dim, right_dim):
    return lax.dot_general(
        left, right, (((left_dim,), (right_dim,)), ((0,), (0,))), preferred_element_type=f32
    )


class Small(NamedTuple):
    ln1_gain: Any
    ln1_bias: Any
    qv_bias: Any
    out_bias: Any
    ln2_gain: Any
    ln2_bias: Any
    fc1_bias: Any
    fc2_bias: Any
    conv_gain: Any
    conv_bias: Any
    pw1_bias: Any
    pw2_bias: Any
    layer_scale: Any
    proj_bias: Any
    dw3_weight: Any
    dw3_bias: Any
    gate: Any


def body(
    vit_in,
    hires,
    size_class,
    pool_mask,
    cotangent,
    ln1_gain,
    ln1_bias,
    qkv_weight,
    qv_bias,
    out_weight,
    out_bias,
    ln2_gain,
    ln2_bias,
    fc1_weight,
    fc1_bias,
    fc2_weight,
    fc2_bias,
    dw7_weight,
    dw7_bias,
    conv_gain,
    conv_bias,
    pw1_weight,
    pw1_bias,
    pw2_weight,
    pw2_bias,
    layer_scale,
    proj_weight,
    proj_bias,
    dw3_weight,
    dw3_bias,
    gate,
):
    parts = lax.axis_size(CHAN)
    groups = lax.axis_size(GRP)
    chan_index = lax.axis_index(CHAN)
    band_index = chan_index % BANDS
    grp_index = lax.axis_index(GRP)
    width = hires.shape[1] * parts
    places = list(range(groups))
    part = D // groups

    along_chan = [(CHAN, bit) for bit in reversed(range(count_bits(CHAN)))]
    along_grp = [(GRP, bit) for bit in reversed(range(count_bits(GRP)))]
    conv_plan = along_chan + [step for step in along_grp if step[1] != PAIR]
    vit_plan = along_chan + along_grp

    rows = qkv_weight.shape[0]
    qkv_out_own = jnp.concatenate(
        [
            my_part(qkv_weight.reshape(rows, 3, groups, -1), 2).reshape(rows, -1),
            my_part(out_weight.reshape(rows, groups, -1), 1),
        ],
        axis=1,
    )
    qkv_out_flow = Flow(gather_crosswise(qkv_out_own, vit_plan))
    proj_flow = Flow(
        gather_crosswise(my_part(proj_weight.reshape(-1, groups, part), 1), vit_plan)
    )
    smalls = Small(
        ln1_gain,
        ln1_bias,
        qv_bias,
        out_bias,
        ln2_gain,
        ln2_bias,
        fc1_bias,
        fc2_bias,
        conv_gain,
        conv_bias,
        pw1_bias,
        pw2_bias,
        layer_scale,
        proj_bias,
        dw3_weight.reshape(-1),
        dw3_bias,
        gate,
    )
    small_flow = Flow(gather(side_by_side(smalls), along_chan))
    pw1_flow = Flow(gather(pick_columns(pw1_weight, parts, groups), conv_plan))
    flows = []

    def half_way(value):
        value = sync(value, small_flow)
        value, pw2_part = sync(
            (value, pw2_weight), small_flow, qkv_out_flow, proj_flow, pw1_flow
        )
        flows.append(Flow(gather(my_part(pw2_part.reshape(groups, -1, width), 0), conv_plan)))
        return value

    conv_bands, masked_bands, conv_saved = conv_forward(
        hires, size_class, dw7_weight, dw7_bias, half_way
    )
    pw2_flow = flows[0]
    conv_bands, masked_bands = sync(
        (conv_bands, masked_bands), qkv_out_flow, proj_flow
    )
    conv_recv = all_to_all(conv_bands)
    masked_bands, fc1_late, fc2_late = lax.optimization_barrier(
        (masked_bands, fc1_weight, fc2_weight)
    )
    fc1_own = my_part(fc1_late.reshape(rows, parts, groups, -1), 2).reshape(rows, -1)
    fc2_own = my_part(fc2_late.reshape(groups, -1, D), 0)
    tables = pool_tables(size_class, band_slices(pool_mask, size_class))
    all_counts = jnp.maximum(jnp.sum(tables.astype(f32), axis=2), 1.0)
    pooled_in = (batched(tables, masked_bands, 2, 1) / all_counts[:, :, None]).astype(bf16)
    table = lax.dynamic_index_in_dim(tables, chan_index, 0, keepdims=False)
    table_pair = jnp.stack([table, flip(table, GRP, PAIR)])
    count_raw = jnp.sum(table.astype(f32), axis=1)
    pool_count = jnp.maximum(count_raw, 1.0)[:, None]
    count_part = count_raw[:, None] / pool_count
    pooled_in = sync(pooled_in, pw1_flow, pw2_flow, qkv_out_flow, proj_flow, small_flow)
    small_full = small_flow.finish()[0].reshape(parts, -1)
    full, begin = [], 0
    for value in smalls:
        full.append(small_full[:, begin : begin + value.shape[0]].reshape(-1))
        begin += value.shape[0]
    small = Small(*full)
    dw3_taps = small.dw3_weight.reshape(parts, 9, -1).transpose(1, 0, 2).reshape(9, D)

    def hidden_bias(all_units, place):
        split = all_units.reshape(parts, groups, -1)
        return lax.dynamic_index_in_dim(split, grp_index ^ place, 1, keepdims=False).reshape(-1)

    normed_own = conv_norm_forward(conv_recv, small.conv_gain, small.conv_bias)
    normed_other = flip(normed_own, GRP, PAIR)
    normed_own = sync(normed_own, pw1_flow, qkv_out_flow, proj_flow)
    normed_own = sync(normed_own, pw2_flow)
    fc1_flow = Flow(gather_crosswise(fc1_own, vit_plan))
    fc2_flow = Flow(gather_crosswise(fc2_own, vit_plan))
    normed_other = sync(normed_other, fc1_flow, fc2_flow)
    normed_low = jnp.concatenate([normed_own, normed_other], axis=0)
    pw1 = pw1_flow.finish()
    conv_places = sorted(pw1)
    conv_act, conv_slope, branch = {}, {}, None
    for place in conv_places:
        hidden = matmul(normed_low, pw1[place]) + hidden_bias(small.pw1_bias, place)
        conv_act[place], conv_slope[place] = gelu_and_slope(hidden)
    conv_act, pooled_in = sync((conv_act, pooled_in), pw2_flow, fc1_flow, fc2_flow)
    pw2 = pw2_flow.finish()
    pooled_in = all_to_all(pooled_in)
    branch = matmul(conv_act[conv_places[0]], pw2[conv_places[0]])
    branch, pooled_in = sync((branch, pooled_in), fc1_flow, fc2_flow)
    for place in conv_places[1:]:
        branch = branch + matmul(conv_act[place], pw2[place])
    pooled_part = batched(
        table_pair, branch.astype(bf16).reshape(2, BAND_CELLS, width), 2, 1
    )
    pooled_other = flip(pooled_part[1].astype(bf16), GRP, PAIR)
    pooled_sum = pooled_part[0] + pooled_other.astype(f32)
    pooled_branch = pooled_sum / pool_count + small.pw2_bias * count_part
    pooled_in = pooled_in.transpose(1, 0, 2).reshape(TOKENS, width).astype(f32)
    pooled_low = (pooled_in + small.layer_scale * pooled_branch).astype(bf16)

    def in_columns(pieces):
        return jnp.concatenate(reorder([pieces[place] for place in places]), axis=1)

    def column_parts(value):
        return reorder(jnp.split(value, groups, axis=1))

    proj = proj_flow.finish()
    qkv_out = qkv_out_flow.finish()
    adapt = in_columns({place: matmul(pooled_low, proj[place]) for place in places})
    adapt_low = (adapt + small.proj_bias).astype(bf16)
    adapt_rims = (
        shifted(adapt_low[TOKENS - GRID :], CHAN, 1),
        adapt_low,
        shifted(adapt_low[:GRID], CHAN, -1),
    )
    keep = jnp.stack([band_index > 0, band_index < BANDS - 1]).astype(jnp.int32)
    gate_tanh = jnp.tanh(small.gate)
    vectors = jnp.stack([small.dw3_bias, gate_tanh, small.ln1_gain, small.ln1_bias])
    adapt_flat, mixed, norm1_low = mix_forward(keep, *adapt_rims, dw3_taps, vectors, vit_in)
    qv_split = small.qv_bias.reshape(2, groups, part)
    qkv_parts = []
    for place in places:
        biases = lax.dynamic_index_in_dim(qv_split, grp_index ^ place, 1, keepdims=False)
        bias = jnp.concatenate([biases[0], jnp.zeros((part,), f32), biases[1]])
        qkv_parts.append((matmul(norm1_low, qkv_out[place][:, : 3 * part]) + bias).astype(bf16))
    share = D // BANDS

    def band_shares(pieces):
        ratio = max(1, groups // BANDS)
        kinds = pieces[0].shape[1] // part
        if groups <= BANDS:
            cuts = []
            for piece in pieces:
                split = piece.reshape(TOKENS, kinds, BANDS // groups, share)
                cuts += [split[:, :, i].reshape(TOKENS, -1) for i in range(BANDS // groups)]
            return cuts
        joined = []
        for band in range(BANDS):
            own = [p.reshape(TOKENS, kinds, part) for p in pieces[band * ratio : (band + 1) * ratio]]
            joined.append(jnp.concatenate(own, axis=2).reshape(TOKENS, -1))
        return joined

    def grp_parts(shares):
        ratio = max(1, groups // BANDS)
        kinds = shares[0].shape[1] // share
        split = [s.reshape(TOKENS, kinds, share) for s in shares]
        if groups <= BANDS:
            each = BANDS // groups
            return [
                jnp.concatenate(split[i * each : (i + 1) * each], axis=2).reshape(TOKENS, -1)
                for i in range(groups)
            ]
        return [
            split[i // ratio][:, :, i % ratio * part : (i % ratio + 1) * part].reshape(TOKENS, -1)
            for i in range(groups)
        ]

    received = sync(band_exchange(band_shares(qkv_parts)), fc1_flow, fc2_flow)
    context, qkv_heads = attention(received)
    context_back = band_return(list(context))
    context_low = jnp.concatenate(reorder(grp_parts(context_back)), axis=1)
    attn = in_columns(
        {place: matmul(context_low, qkv_out[place][:, 3 * part :]) for place in places}
    )
    resid = mixed + attn + small.out_bias
    norm2, ln2_pullback = jax.vjp(norm_vit, resid, small.ln2_gain, small.ln2_bias)
    norm2_low = norm2.astype(bf16)
    vit_out = resid + small.fc2_bias
    grad_norm2 = jnp.zeros((TOKENS, D), f32)
    fc1, fc2 = fc1_flow.finish(), fc2_flow.finish()
    fc1_grads, fc2_grads, fc1_bias_grads = {}, {}, []
    for place in places:
        vit_out, grad_norm2, fc1_grads[place], bias_grad, fc2_grads[place] = mlp_piece(
            norm2_low,
            cotangent,
            fc1[place],
            hidden_bias(small.fc1_bias, place),
            fc2[place],
            vit_out,
            grad_norm2,
        )
        fc1_bias_grads.append(bias_grad.reshape(parts, -1))

    fc2_sum = Flow(scatter_and_spread(fc2_grads, vit_plan, crosswise_sum))
    fc1_sum = Flow(scatter_and_spread(fc1_grads, vit_plan, crosswise_sum))
    grads = SimpleNamespace(fc2_bias=column_sum(cotangent))

    def hidden_bias_grad(parts_rel):
        return jnp.stack(reorder(parts_rel), axis=1).reshape(-1)

    grads.fc1_bias = hidden_bias_grad(fc1_bias_grads)
    grad_resid_part, grads.ln2_gain, grads.ln2_bias = ln2_pullback(grad_norm2)
    grad_resid = cotangent.astype(f32) + grad_resid_part
    grad_attn_low = grad_resid.astype(bf16)
    grads.out_bias = column_sum(grad_attn_low)
    grad_attn_rel = column_parts(grad_attn_low)
    grad_context = sum(
        right_grad(grad_attn_rel[place], qkv_out[place][:, 3 * part :]) for place in places
    )
    context_grad_rel = band_shares(column_parts(grad_context.astype(bf16)))
    context_grads = sync(band_exchange(context_grad_rel), fc2_sum)
    qkv_grad_heads = attention_grad(qkv_heads, context_grads)
    qkv_grad_parts = grp_parts(band_return(list(qkv_grad_heads)))
    bias_rel = reorder([column_sum(g) for g in qkv_grad_parts])
    grads.qv_bias = jnp.concatenate(
        [g[:part] for g in bias_rel] + [g[2 * part :] for g in bias_rel]
    )
    grad_norm1 = sum(
        right_grad(qkv_grad_parts[place], qkv_out[place][:, : 3 * part]) for place in places
    )
    vit_grad, grad_conv3_low, mix_sums = mix_grad(vectors, grad_norm1, mixed, grad_resid, adapt_flat)
    grads.ln1_gain, grads.ln1_bias, grads.gate, grads.dw3_bias = mix_sums
    grad_rims = (
        shifted(grad_conv3_low[TOKENS - GRID :], CHAN, 1),
        grad_conv3_low,
        shifted(grad_conv3_low[:GRID], CHAN, -1),
    )
    grad_rims = sync(grad_rims, fc1_sum)
    joint = joint_grads(norm1_low, qkv_grad_parts, context_low, grad_attn_rel)
    joint_sum = Flow(
        scatter_and_spread(dict(enumerate(joint)), vit_plan, crosswise_sum)
    )
    grad_adapt_low, adapt_sums = adapt_grad(keep, grad_rims, adapt_rims, dw3_taps)
    grads.dw3_weight = adapt_sums[:9].reshape(9, parts, -1).transpose(1, 0, 2).reshape(-1)
    grads.proj_bias = adapt_sums[9]
    grad_adapt_rel = column_parts(grad_adapt_low)
    grad_pooled = sum(right_grad(grad_adapt_rel[place], proj[place]) for place in places)
    grad_pooled = grad_pooled.astype(bf16).astype(f32)
    grad_pool_sum = grad_pooled / pool_count
    scaled_own = (small.layer_scale * grad_pool_sum).astype(bf16)
    scaled_other = flip(scaled_own, GRP, PAIR)
    grads.layer_scale = jnp.sum(grad_pooled * pooled_branch, axis=0)
    grads.pw2_bias = small.layer_scale * jnp.sum(grad_pooled * count_part, axis=0)
    proj_sum = Flow(
        scatter_and_spread(
            {place: left_grad(pooled_low, grad_adapt_rel[place]) for place in places},
            vit_plan,
            crosswise_sum,
        )
    )
    scaled_other = sync(scaled_other, fc2_sum)
    grad_branch_low = (
        batched(table_pair, jnp.stack([scaled_own, scaled_other]), 1, 1)
        .astype(bf16)
        .reshape(2 * BAND_CELLS, width)
    )
    resid_back = all_to_all(
        grad_pool_sum.astype(bf16).reshape(TOKENS, parts, -1).transpose(1, 0, 2)
    )
    pw2_grads = {
        place: left_grad(conv_act[place], grad_branch_low) for place in reversed(conv_places)
    }
    grad_branch_low, pw2_grads = sync(
        (grad_branch_low, pw2_grads), fc1_sum, joint_sum, proj_sum
    )
    pw2_sum = Flow(scatter_and_spread(pw2_grads, conv_plan))
    grad_hidden, grad_normed_pair = {}, None
    for place in reversed(conv_places):
        grad_act = right_grad(grad_branch_low, pw2[place])
        grad_hidden[place] = (conv_slope[place].astype(f32) * grad_act).astype(bf16)
        if place == conv_places[-1]:
            grad_branch_low, grad_hidden = sync(
                (grad_branch_low, grad_hidden), pw2_sum, fc2_sum
            )
    for place in reversed(conv_places):
        product = right_grad(grad_hidden[place], pw1[place])
        grad_normed_pair = product if grad_normed_pair is None else grad_normed_pair + product
    grad_normed_pair, grad_hidden = sync(
        (grad_normed_pair, grad_hidden), joint_sum, fc1_sum, fc2_sum
    )
    grad_normed_other = flip(grad_normed_pair[BAND_CELLS:].astype(bf16), GRP, PAIR)
    pw1_grads = {}
    pw1_bias_grads = [jnp.zeros((parts, pw1_weight.shape[1] // parts // groups), f32)] * groups
    for place in reversed(conv_places):
        pw1_grads[place] = left_grad(normed_low, grad_hidden[place])
        pw1_bias_grads[place] = column_sum(grad_hidden[place]).reshape(parts, -1)
    pw1_sum = Flow(scatter_and_spread(pw1_grads, conv_plan))
    grads.pw1_bias = hidden_bias_grad(pw1_bias_grads)
    grad_normed_other, resid_back = sync(
        (grad_normed_other, resid_back), pw1_sum, pw2_sum, fc2_sum, fc1_sum, proj_sum
    )
    grad_conv_bands, norm_sums = conv_norm_backward(
        conv_recv, small.conv_gain, grad_normed_pair[:BAND_CELLS], grad_normed_other
    )
    grads.conv_gain, grads.conv_bias = norm_sums
    grad_conv_back = all_to_all(grad_conv_bands)
    resid_bands = batched(tables, resid_back, 1, 1).astype(bf16)
    others = (pw1_sum, pw2_sum, joint_sum, proj_sum, fc2_sum, fc1_sum)
    grad_conv_back = sync(grad_conv_back, *others)

    def half_way_back(value):
        value, bundle = lax.optimization_barrier(
            (sync(value, *others), bundle_rows(Small(**vars(grads)), parts))
        )
        flows.append(Flow(total_sum(bundle, vit_plan)))
        return value

    hires_grad, dw7_grads = conv_backward(conv_saved, grad_conv_back, resid_bands, half_way_back)
    bundle_sum = flows[1]
    hires_grad, dw7_grads = sync((hires_grad, dw7_grads), bundle_sum, *others)
    for axis, bit in along_grp:
        dw7_grads = dw7_grads + flip(dw7_grads, axis, bit)
    total = bundle_sum.finish().reshape(-1)
    sums, begin = [], 0
    for value in smalls:
        sums.append(total[begin : begin + value.shape[0]])
        begin += value.shape[0]
    sums = Small(*sums)

    grad_fc1 = place_columns(fc1_sum.finish(), parts)
    grad_fc2 = jnp.concatenate(reorder(fc2_sum.finish()), axis=0)
    grad_proj = jnp.concatenate(reorder(proj_sum.finish()), axis=1)
    joint_all = reorder(joint_sum.finish())
    grad_qkv = jnp.concatenate(
        [piece[:, kind * part : (kind + 1) * part] for kind in range(3) for piece in joint_all],
        axis=1,
    )
    grad_out = jnp.concatenate([piece[:, 3 * part :] for piece in joint_all], axis=1)
    grad_pw2 = jnp.concatenate(reorder(pw2_sum.finish()), axis=0)
    grad_pw1 = place_columns(pw1_sum.finish(), parts)
    return (
        vit_out,
        vit_grad,
        hires_grad,
        sums.ln1_gain,
        sums.ln1_bias,
        grad_qkv.astype(f32),
        sums.qv_bias,
        grad_out.astype(f32),
        sums.out_bias,
        sums.ln2_gain,
        sums.ln2_bias,
        grad_fc1,
        sums.fc1_bias,
        grad_fc2.astype(f32),
        sums.fc2_bias,
        dw7_grads[: KERNEL * KERNEL],
        dw7_grads[KERNEL * KERNEL],
        sums.conv_gain,
        sums.conv_bias,
        grad_pw1,
        sums.pw1_bias,
        grad_pw2.astype(f32),
        sums.pw2_bias,
        sums.layer_scale,
        grad_proj.astype(f32),
        sums.proj_bias,
        sums.dw3_weight.reshape(9, -1),
        sums.dw3_bias,
        sums.gate,
    )


def solution(mesh):
    in_specs = (
        P((GRP, CHAN), None),
        P(GRP, CHAN, None),
        P(GRP),
        P(GRP, None),
        P((GRP, CHAN), None),
        P(CHAN),
        P(CHAN),
        P(CHAN, None),
        P(CHAN),
        P(CHAN, None),
        P(CHAN),
        P(CHAN),
        P(CHAN),
        P(CHAN, None),
        P(CHAN),
        P(CHAN, None),
        P(CHAN),
        P(None, CHAN),
        P(CHAN),
        P(CHAN),
        P(CHAN),
        P(CHAN, None),
        P(CHAN),
        P(CHAN, None),
        P(CHAN),
        P(CHAN),
        P(CHAN, None),
        P(CHAN),
        P(None, CHAN),
        P(CHAN),
        P(CHAN),
    )
    out_specs = (
        P((GRP, CHAN), None),
        P((GRP, CHAN), None),
        P(GRP, CHAN, None),
        P(CHAN),
        P(CHAN),
        P(CHAN, None),
        P(CHAN),
        P(CHAN, None),
        P(CHAN),
        P(CHAN),
        P(CHAN),
        P(CHAN, None),
        P(CHAN),
        P(CHAN, None),
        P(CHAN),
        P(None, CHAN),
        P(CHAN),
        P(CHAN),
        P(CHAN),
        P(CHAN, None),
        P(CHAN),
        P(CHAN, None),
        P(CHAN),
        P(CHAN),
        P(CHAN, None),
        P(CHAN),
        P(None, CHAN),
        P(CHAN),
        P(CHAN),
    )
    return jax.shard_map(body, mesh=mesh, in_specs=in_specs, out_specs=out_specs, check_vma=False)
```

time: 2870 us -> 1030 us (0.36)
  waiting for transfers between devices: 1520 us -> 250 us
  blocking collectives: 523 us -> 0 us
  other arithmetic: 364 us -> 123 us
  starting transfers between devices: 33.6 us -> 190 us
  Pallas kernels: 0 us -> 131 us
  matrix products: 244 us -> 178 us
    reduce_scatter x7 -> x0, waiting for transfers between devices: 849 us -> none  [the longest x1 316 us: body(): lax.psum_scatter(full_grads[14].astype(jnp.bfloat16), 'chan', scatter_dim...]
    all_gather x7 -> x0, waiting for transfers between devices: 525 us -> none  [the longest x1 296 us: body(): lax.all_gather(pw2_weight, 'chan', axis=0, tiled=True)]
    all_gather x13 -> x0, blocking collectives: 395 us -> none  [the longest x1 61.3 us: body(): lax.all_gather(proj_bias, 'chan', axis=0, tiled=True)]
    ppermute x8 -> x121, waiting for transfers between devices: 59.3 us -> 218 us  [the longest x81 167 us: flip(): lax.ppermute(value, axis, [(i, i ^ 1 << bit) for i in range(lax.axis_size...]
    ppermute x8 -> x121, starting transfers between devices: 8.93 us -> 166 us  [the longest x81 107 us: flip(): lax.ppermute(value, axis, [(i, i ^ 1 << bit) for i in range(lax.axis_size...]
    pallas_call x0 -> x21, Pallas kernels: none -> 131 us  [the longest x2 38.8 us: conv_backward(): pl.pallas_call(partial(conv_backward_kernel, first=first), grid=(1,), in_...]
    unnamed x2 -> x0, blocking collectives: 113 us -> none
    reduce_sum x14 -> x7, other arithmetic: 84.3 us -> 3.42 us  [the longest x4 1.63 us: column_sum(): return jnp.sum(grads.astype(f32), axis=0)]
  transfers between devices with their start and end apart: 28 -> 125, of which waited for: 16 -> 33; matrix products, arithmetic and copies ran while one was open for 23% -> 37% of each run, Pallas kernels for 0% -> 11%
where the time goes in v1:
time: 1030 us; the launch traced here: 1020 us
  waiting for transfers between devices  250 us (24%)
  starting transfers between devices  190 us (18%)
  matrix products  178 us (17%)
  local copies, waits for them, and re-layouts  137 us (13%)
  Pallas kernels  131 us (13%)
  other arithmetic  123 us (12%)
  between operations  10.5 us (1%)
    ppermute x81, waiting for transfers between devices, flip(): lax.ppermute(value, axis, [(i, i ^ 1 << bit) for i in range(lax.axis_size...  167 us
    ppermute x81, starting transfers between devices, flip(): lax.ppermute(value, axis, [(i, i ^ 1 << bit) for i in range(lax.axis_size...  107 us
    dot_general x16, matrix products, right_grad(): lax.dot_general(grads, weight, (((1,), (1,)), ((), ())), preferred_elemen...  65.3 us
    dot_general x16, matrix products, matmul(): return jnp.dot(left, right, preferred_element_type=f32)  63.8 us
    convert_element_type x26, other arithmetic, added(): return (left.astype(f32) + right.astype(f32)).astype(left.dtype)  48 us
    unnamed x492, local copies, waits for them, and re-layouts  45.5 us
    ppermute x24, waiting for transfers between devices, flip_crosswise(): return lax.ppermute(value, (GRP, CHAN), pairs)  40.4 us
    pallas_call x2, Pallas kernels, conv_backward(): pl.pallas_call(partial(conv_backward_kernel, first=first), grid=(1,), in_...  38.8 us
  transfers between devices with their start and end apart: 125, of which 33 were waited for; matrix products, arithmetic and copies ran while one was open for 37% of the time, Pallas kernels for 11%

profile of v1, /device:TPU:0, one launch (start us, length us, event | category | flops | bytes accessed | tf_op | source)
XLA Modules:
  0.0 1020.0 jit_solution(16506805224430148397)
XLA Ops:
  4.4 4.0 collective-permute-start.2
  26.8 16.2 %depthwise_forward.1 = (bf16[2304,256]{1,0:T(8,128)(2,1)S(1)}, bf16[2304,256]{1,0:T(8,128)(2,1)S(1)}) custom-call(s32[1,384]{1,0:T(1,128)S(1)} %broadcast_in_dim_reshape.18.sizes_ref, f32[49,384]{1,0:T(8,128)S(1)} %tile.18.taps_ref, f32[1,384]{1,0:T(1,128)S(1)} %tile.20.bias_ref, bf16[384,2304]{1,0:T(8,128)(2,1)S(1)} %bitcast.684), custom_call_target="tpu_custom_call" | custom-call | tf_op jit(solution)/shard_map/depthwise_forward/pallas_call | solution.py:490
  47.7 4.1 collective-permute-done.1
  61.3 9.7 depthwise_forward_last.1
  81.8 4.0 collective-permute-start.8
  91.4 4.7 all-to-all-start
  98.8 14.2 %collective-permute-done.8 = bf16[1,192,1536]{2,1,0:T(8,128)(2,1)} collective-permute-done((bf16[1,192,1536]{2,1,0:T(8,128)(2,1)}, bf16[1,192,1536]{2,1,0:T(8,128)(2,1)}, u32[]{:S(2)}, u32[]{:S(2)}) %collective-permute-start.8) | collective-permute-done | bytes 589856 | tf_op jit(solution)/shard_map/ppermute | solution.py:36
  116.2 4.5 collective-permute-start.12
  129.2 25.0 %all-to-all-done = bf16[8,576,192]{1,2,0:T(8,128)(2,1)} async-done(((bf16[8,576,192]{1,2,0:T(8,128)(2,1)}), bf16[8,576,192]{1,2,0:T(8,128)(2,1)}, u32[]{:S(2)}, u32[]{:S(2)}) %all-to-all-start) | async-done | bytes 1769504 | tf_op jit(solution)/shard_map/all_to_all | solution.py:253
  157.1 4.4 conv_norm_forward.1
  161.5 20.8 %collective-permute-done.12 = bf16[4,192,1536]{2,1,0:T(8,128)(2,1)} collective-permute-done((bf16[4,192,1536]{2,1,0:T(8,128)(2,1)}, bf16[4,192,1536]{2,1,0:T(8,128)(2,1)}, u32[]{:S(2)}, u32[]{:S(2)}) %collective-permute-start.12) | collective-permute-done | bytes 2359328 | tf_op jit(solution)/shard_map/ppermute | solution.py:36
  187.8 29.2 %collective-permute-start.21 = (bf16[8,192,1536]{2,1,0:T(8,128)(2,1)}, bf16[8,192,1536]{2,1,0:T(8,128)(2,1)}, u32[]{:S(2)}, u32[]{:S(2)}) collective-permute-start(bf16[8,192,1536]{2,1,0:T(8,128)(2,1)} %bitcast.57), channel_id=1, source_target_pairs={{0,8},{8,0},{16,24},{24,16},{1,9},{9,1},{17,25},{25,17},{2,10},{10... | collective-permute-start | bytes 14155784 | tf_op jit(solution)/shard_map/ppermute | solution.py:36
  232.2 12.0 %collective-permute-done.19 = bf16[1,128,1024]{1,2,0:T(8,128)(2,1)} collective-permute-done((bf16[1,128,1024]{1,2,0:T(8,128)(2,1)}, bf16[1,128,1024]{1,2,0:T(8,128)(2,1)}, u32[]{:S(2)}, u32[]{:S(2)}) %collective-permute-start.19) | collective-permute-done | bytes 262176 | tf_op jit(solution)/shard_map/ppermute | solution.py:36
  244.1 4.2 collective-permute-done.20
  248.4 9.5 collective-permute-done.18
  263.6 11.7 %multiply_convert_fusion.1 = (bf16[1152,1536]{1,0:T(8,128)(2,1)}, f32[1152,1536]{1,0:T(8,128)}) fusion(f32[1536]{0:T(1024)S(1)} %add.565, bf16[1152,1536]{1,0:T(8,128)(2,1)S(1)} %constant_dynamic-update-slice_fusion, bf16[1536,1536]{1,0:T(8,128)(2,1)} %bitcast.56), kind=kOutput, calls=%fused_computation.32 | convolution fusion | flops 5446434816 | bytes 18880512 | tf_op jit(solution)/shard_map/dot_general | solution.py:274
  275.3 11.1 %multiply_convert_fusion = (bf16[1152,1536]{1,0:T(8,128)(2,1)}, f32[1152,1536]{1,0:T(8,128)}) fusion(f32[1536]{0:T(1024)S(1)} %add.570, bf16[1152,1536]{1,0:T(8,128)(2,1)S(1)} %constant_dynamic-update-slice_fusion, bf16[1536,1536]{1,0:T(8,128)(2,1)} %bitcast.58), kind=kOutput, calls=%fused_computation.30 | convolution fusion | flops 5446434816 | bytes 18880512 | tf_op jit(solution)/shard_map/dot_general | solution.py:274
  295.0 3.8 select_bitcast_fusion.17
  314.2 8.7 all-to-all-start.1
  322.9 10.4 %fusion.187 = f32[1152,1536]{1,0:T(8,128)} fusion(bf16[1152,1536]{1,0:T(8,128)(2,1)} %get-tuple-element.228, bf16[1536,1536]{1,0:T(8,128)(2,1)} %bitcast.70), kind=kOutput, calls=%fused_computation.625 | convolution fusion | flops 5435817984 | bytes 15335424 | tf_op jit(solution)/shard_map/dot_general | solution.py:274
  333.3 7.0 all-to-all-done.1
  340.3 10.6 %fusion.188 = f32[1152,1536]{1,0:T(8,128)} fusion(bf16[1152,1536]{1,0:T(8,128)(2,1)} %get-tuple-element.235, bf16[1536,1536]{1,0:T(8,128)(2,1)} %bitcast.81), kind=kOutput, calls=%fused_computation.626 | convolution fusion | flops 5435817984 | bytes 15335424 | tf_op jit(solution)/shard_map/dot_general | solution.py:274
  351.0 4.2 add_convert_fusion
  375.1 4.1 collective-permute-start.32
  399.1 5.8 collective-permute-start.37
  407.9 6.1 collective-permute-start.38
  418.3 11.2 %collective-permute-done.42 = bf16[4,128,1024]{2,1,0:T(8,128)(2,1)} collective-permute-done((bf16[4,128,1024]{2,1,0:T(8,128)(2,1)}, bf16[4,128,1024]{2,1,0:T(8,128)(2,1)}, u32[]{:S(2)}, u32[]{:S(2)}) %collective-permute-start.42) | collective-permute-done | bytes 1048608 | tf_op jit(solution)/shard_map/ppermute | solution.py:89
  438.2 4.6 attention_forward.1
  442.9 6.2 collective-permute-start.43
  449.7 8.9 collective-permute-start.49
  473.3 5.9 mlp_piece.4
  479.3 5.5 mlp_piece.5
  487.6 5.5 mlp_piece.6
  493.1 6.8 mlp_piece.7
  517.7 6.6 attention_backward.1
  575.8 7.1 collective-permute-done.62
  586.4 8.3 convolution_convert_fusion.2
  596.1 8.0 convolution_convert_fusion.3
  604.1 5.4 collective-permute-done.65
  616.2 6.9 all-to-all-start.2
  641.4 10.2 %fusion.2 = bf16[1152,1536]{1,0:T(8,128)(2,1)S(1)} fusion(bf16[1152,1536]{1,0:T(8,128)(2,1)S(1)} %bitcast.772, bf16[1536,1536]{1,0:T(8,128)(2,1)} %bitcast.81, f32[1152,1536]{1,0:T(8,128)} %get-tuple-element.605), kind=kOutput, calls=%fused_computation.11 | convolution fusion | flops 5457051648 | bytes 18874368 | tf_op jit(solution)/shard_map/dot_general | solution.py:284
  657.7 10.1 fusion.3
  667.8 11.4 %fusion.192 = f32[1152,1536]{1,0:T(8,128)} fusion(bf16[1152,1536]{1,0:T(8,128)(2,1)S(1)} %fusion.3, bf16[1536,1536]{1,0:T(8,128)(2,1)} %bitcast.56), kind=kOutput, calls=%fused_computation.630 | convolution fusion | flops 5435817984 | bytes 15335424 | tf_op jit(solution)/shard_map/dot_general | solution.py:284
  679.2 11.5 %convolution_add_fusion = f32[1152,1536]{1,0:T(8,128)} fusion(f32[1152,1536]{1,0:T(8,128)} %fusion.192, bf16[1152,1536]{1,0:T(8,128)(2,1)S(1)} %fusion.2, bf16[1536,1536]{1,0:T(8,128)(2,1)} %bitcast.58), kind=kOutput, calls=%fused_computation.8 | convolution fusion | flops 5437587456 | bytes 22413312 | tf_op jit(solution)/shard_map/dot_general | solution.py:284
  690.7 8.0 convolution_convert_fusion.1
  704.2 5.2 fusion.1
  711.1 5.3 slice.598
  716.9 8.0 convolution_convert_fusion
  737.6 11.5 %collective-permute-done.80 = bf16[1,128,1024]{2,1,0:T(8,128)(2,1)S(1)} collective-permute-done((bf16[1,128,1024]{2,1,0:T(8,128)(2,1)S(1)}, bf16[1,128,1024]{2,1,0:T(8,128)(2,1)S(1)}, u32[]{:S(2)}, u32[]{:S(2)}) %collective-permute-start.80) | collective-permute-done | bytes 262176 | tf_op jit(solution)/shard_map/ppermute | solution.py:36
  750.9 7.3 collective-permute-done.77.other_ref
  758.3 6.1 collective-permute-done.79
  766.4 12.6 %conv_norm_backward.1 = (bf16[8,576,192]{2,1,0:T(8,128)(2,1)S(1)}, f32[2,1536]{1,0:T(2,128)S(1)}) custom-call(bf16[8,576,192]{2,1,0:T(8,128)(2,1)S(1)} %copy.200.blocks_ref, f32[1,1536]{1,0:T(1,128)S(1)} %copy-done.40, f32[576,1536]{1,0:T(8,128)S(1)} %copy-done.2, bf16[576,1536]{1,0:T(8,128)(2,1)} %collective-permute-done.77.other_ref), custom_call_target="tpu_custom_call" | custom-call | tf_op jit(solution)/shard_map/conv_norm_backward/pallas_call | solution.py:628
  780.4 4.2 copy.242
  784.6 4.3 all-to-all-start.3
  788.9 5.2 fusion
  813.4 37.9 %collective-permute-done.89 = bf16[1,128,1024]{2,1,0:T(8,128)(2,1)S(1)} collective-permute-done((bf16[1,128,1024]{2,1,0:T(8,128)(2,1)}, bf16[1,128,1024]{2,1,0:T(8,128)(2,1)S(1)}, u32[]{:S(2)}, u32[]{:S(2)}) %collective-permute-start.89) | collective-permute-done | bytes 262176 | tf_op jit(solution)/shard_map/ppermute | solution.py:36
  851.3 15.7 %collective-permute-done.87 = bf16[4,192,256]{2,1,0:T(8,128)(2,1)} collective-permute-done((bf16[4,192,256]{2,1,0:T(8,128)(2,1)}, bf16[4,192,256]{2,1,0:T(8,128)(2,1)}, u32[]{:S(2)}, u32[]{:S(2)}) %collective-permute-start.87) | collective-permute-done | bytes 393248 | tf_op jit(solution)/shard_map/ppermute | solution.py:89
  882.8 4.2 collective-permute-start.91
  888.0 4.1 convolution_convert_fusion.9.resid_ref
  898.2 25.1 %depthwise_backward.2 = (f32[384,2304]{1,0:T(8,128)}, f32[50,256]{1,0:T(8,128)S(1)}) custom-call(s32[2]{0:T(128)S(1)} %copy-done.44, s32[1,384]{1,0:T(1,128)S(1)} %copy-done.42, f32[49,384]{1,0:T(8,128)S(1)} %copy-done.19, bf16[2304,384]{1,0:T(8,128)(2,1)S(1)} %copy-done.8, bf16[8,576,192]{2,1,0:T(8,128)(2,1)S(1)} %copy.255.grad_ref, ...), custom_call_target="tpu_custom_call" | custom-call | tf_op jit(solution)/shard_map/depthwise_backward/pallas_call | solution.py:519
  943.4 13.7 %depthwise_backward.3 = (f32[384,2304]{1,0:T(8,128)}, f32[50,128]{1,0:T(8,128)S(1)}) custom-call(s32[2]{0:T(128)S(1)} %copy-done.44, s32[1,384]{1,0:T(1,128)S(1)} %copy-done.42, f32[49,384]{1,0:T(8,128)S(1)} %copy-done.19, bf16[2304,384]{1,0:T(8,128)(2,1)S(1)} %copy-done.9, ...), custom_call_target="tpu_custom_call", output_to_operand_aliasing={{0}: (6, {})} | custom-call | tf_op jit(solution)/shard_map/depthwise_backward/pallas_call | solution.py:519
  957.3 4.6 collective-permute-done.97
  962.2 8.2 collective-permute-done.101
  993.7 14.6 %collective-permute-done.108 = bf16[128,1024]{1,0:T(8,128)(2,1)S(1)} collective-permute-done((bf16[128,1024]{1,0:T(8,128)(2,1)S(1)}, bf16[128,1024]{1,0:T(8,128)(2,1)S(1)}, u32[]{:S(2)}, u32[]{:S(2)}) %collective-permute-start.108) | collective-permute-done | bytes 262176 | tf_op jit(solution)/shard_map/ppermute | solution.py:36
  (1022 shorter events, 413.4 us)
Async XLA Ops:
  4.4 47.4 %collective-permute-start.2 = (bf16[1,128,1024]{1,2,0:T(8,128)(2,1)}, bf16[1,128,1024]{1,2,0:T(8,128)(2,1)}, u32[]{:S(2)}, u32[]{:S(2)}) collective-permute-start(bf16[1,128,1024]{1,2,0:T(8,128)(2,1)} %maximum_bitcast_fusion.5), channel_id=1, source_target_pairs={{0,4},{1,5},{2,6},{3,7},{4,0},{5,1},{6,2},{7,3},{8,12},{9,13},{10,... | collective-permute-start | bytes 786440 | tf_op jit(solution)/shard_map/ppermute | solution.py:36
  8.8 36.2 %collective-permute-start = (f32[1,36,128]{2,1,0:T(8,128)S(1)}, f32[1,36,128]{2,1,0:T(8,128)}, u32[]{:S(2)}, u32[]{:S(2)}) collective-permute-start(f32[1,36,128]{2,1,0:T(8,128)S(1)} %bitcast.802), channel_id=1, source_target_pairs={{0,4},{1,5},{2,6},{3,7},{4,0},{5,1},{6,2},{7,3},{8,12},{9,13},{10,... | collective-permute-start | bytes 55304 | tf_op jit(solution)/shard_map/ppermute | solution.py:36
  10.1 41.7 %collective-permute-start.3 = (bf16[1,192,256]{2,1,0:T(8,128)(2,1)}, bf16[1,192,256]{2,1,0:T(8,128)(2,1)}, u32[]{:S(2)}, u32[]{:S(2)}) collective-permute-start(bf16[1,192,256]{2,1,0:T(8,128)(2,1)} %bitcast.676), channel_id=1, source_target_pairs={{0,4},{1,5},{2,6},{3,7},{4,0},{5,1},{6,2},{7,3},{8,12},{9,13},{10,... | collective-permute-start | bytes 294920 | tf_op jit(solution)/shard_map/ppermute | solution.py:36
  15.7 36.1 %collective-permute-start.4 = (bf16[1,192,1536]{2,1,0:T(8,128)(2,1)}, bf16[1,192,1536]{2,1,0:T(8,128)(2,1)}, u32[]{:S(2)}, u32[]{:S(2)}) collective-permute-start(bf16[1,192,1536]{2,1,0:T(8,128)(2,1)} %bitcast.21), channel_id=1, source_target_pairs={{0,4},{1,5},{2,6},{3,7},{4,0},{5,1},{6,2},{7,3},{8,12},{9,13},{10,... | collective-permute-start | bytes 1769480 | tf_op jit(solution)/shard_map/ppermute | solution.py:36
  56.9 41.9 %collective-permute-start.11 = (f32[4,36,128]{2,0,1:T(4,128)}, f32[4,36,128]{2,0,1:T(4,128)}, u32[]{:S(2)}, u32[]{:S(2)}) collective-permute-start(f32[4,36,128]{2,0,1:T(4,128)} %bitcast.42), channel_id=1, source_target_pairs={{0,1},{1,0},{2,3},{3,2},{4,5},{5,4},{6,7},{7,6},{8,9},{9,8},{10,11... | collective-permute-start | bytes 221192 | tf_op jit(solution)/shard_map/ppermute | solution.py:36
  61.2 51.8 %collective-permute-start.7 = (bf16[2,192,1536]{2,1,0:T(8,128)(2,1)}, bf16[2,192,1536]{2,1,0:T(8,128)(2,1)}, u32[]{:S(2)}, u32[]{:S(2)}) collective-permute-start(bf16[2,192,1536]{2,1,0:T(8,128)(2,1)} %maximum_bitcast_fusion), channel_id=1, source_target_pairs={{0,2},{1,3},{2,0},{3,1},{4,6},{5,7},{6,4},{7,5},{8,10},{9,11},{10,... | collective-permute-start | bytes 3538952 | tf_op jit(solution)/shard_map/ppermute | solution.py:36
  79.2 33.8 %collective-permute-start.9 = (bf16[4,128,1024]{2,1,0:T(8,128)(2,1)}, bf16[4,128,1024]{2,1,0:T(8,128)(2,1)}, u32[]{:S(2)}, u32[]{:S(2)}) collective-permute-start(bf16[4,128,1024]{2,1,0:T(8,128)(2,1)} %bitcast.755), channel_id=1, source_target_pairs={{0,1},{1,0},{2,3},{3,2},{4,5},{5,4},{6,7},{7,6},{8,24},{9,25},{10,... | collective-permute-start | bytes 3145736 | tf_op jit(solution)/shard_map/ppermute | solution.py:89
  81.8 31.2 %collective-permute-start.8 = (bf16[1,192,1536]{2,1,0:T(8,128)(2,1)}, bf16[1,192,1536]{2,1,0:T(8,128)(2,1)}, u32[]{:S(2)}, u32[]{:S(2)}) collective-permute-start(bf16[1,192,1536]{2,1,0:T(8,128)(2,1)} %constant_dynamic-slice_fusion.29), channel_id=1, source_target_pairs={{0,4},{1,5},{2,6},{3,7},{4,0},{5,1},{6,2},{7,3},{8,12},{9,13},{10,... | collective-permute-start | bytes 1769480 | tf_op jit(solution)/shard_map/ppermute | solution.py:36
  91.4 62.8 %all-to-all-start = ((bf16[8,576,192]{1,2,0:T(8,128)(2,1)}), bf16[8,576,192]{1,2,0:T(8,128)(2,1)}, u32[]{:S(2)}, u32[]{:S(2)}) async-start(bf16[8,576,192]{1,2,0:T(8,128)(2,1)} %copy.194), calls=%async_computation | async-start | bytes 3932160 | tf_op jit(solution)/shard_map/all_to_all | solution.py:253
  116.2 66.0 %collective-permute-start.12 = (bf16[4,192,1536]{2,1,0:T(8,128)(2,1)}, bf16[4,192,1536]{2,1,0:T(8,128)(2,1)}, u32[]{:S(2)}, u32[]{:S(2)}) collective-permute-start(bf16[4,192,1536]{2,1,0:T(8,128)(2,1)} %bitcast.47), channel_id=1, source_target_pairs={{0,1},{1,0},{2,3},{3,2},{4,5},{5,4},{6,7},{7,6},{8,9},{9,8},{10,11... | collective-permute-start | bytes 7077896 | tf_op jit(solution)/shard_map/ppermute | solution.py:36
  120.7 40.7 %collective-permute-start.15 = (bf16[4,192,256]{2,1,0:T(8,128)(2,1)}, bf16[4,192,256]{2,1,0:T(8,128)(2,1)}, u32[]{:S(2)}, u32[]{:S(2)}) collective-permute-start(bf16[4,192,256]{2,1,0:T(8,128)(2,1)} %bitcast.39), channel_id=1, source_target_pairs={{0,16},{1,17},{2,18},{3,19},{4,20},{5,21},{6,22},{7,23},{8,9},{9,8... | collective-permute-start | bytes 1179656 | tf_op jit(solution)/shard_map/ppermute | solution.py:89
  120.7 40.7 %collective-permute-start.13 = (bf16[4,128,1024]{2,1,0:T(8,128)(2,1)}, bf16[4,128,1024]{2,1,0:T(8,128)(2,1)}, u32[]{:S(2)}, u32[]{:S(2)}) collective-permute-start(bf16[4,128,1024]{2,1,0:T(8,128)(2,1)} %bitcast.756), channel_id=1, source_target_pairs={{0,16},{1,17},{2,18},{3,19},{4,20},{5,21},{6,22},{7,23},{8,9},{9,8... | collective-permute-start | bytes 3145736 | tf_op jit(solution)/shard_map/ppermute | solution.py:89
  122.7 38.7 %collective-permute-start.14 = (bf16[4,128,1024]{2,1,0:T(8,128)(2,1)}, bf16[4,128,1024]{2,1,0:T(8,128)(2,1)}, u32[]{:S(2)}, u32[]{:S(2)}) collective-permute-start(bf16[4,128,1024]{2,1,0:T(8,128)(2,1)} %collective-permute-done.9), channel_id=1, source_target_pairs={{0,16},{1,17},{2,18},{3,19},{4,20},{5,21},{6,22},{7,23},{8,9},{9,8... | collective-permute-start | bytes 3145736 | tf_op jit(solution)/shard_map/ppermute | solution.py:89
  123.9 37.6 %collective-permute-start.16 = (bf16[4,192,256]{2,1,0:T(8,128)(2,1)}, bf16[4,192,256]{2,1,0:T(8,128)(2,1)}, u32[]{:S(2)}, u32[]{:S(2)}) collective-permute-start(bf16[4,192,256]{2,1,0:T(8,128)(2,1)} %collective-permute-done.10), channel_id=1, source_target_pairs={{0,16},{1,17},{2,18},{3,19},{4,20},{5,21},{6,22},{7,23},{8,9},{9,8... | collective-permute-start | bytes 1179656 | tf_op jit(solution)/shard_map/ppermute | solution.py:89
  161.4 66.9 %collective-permute-start.17 = (bf16[2,192,1536]{2,1,0:T(8,128)(2,1)}, bf16[2,192,1536]{2,1,0:T(8,128)(2,1)}, u32[]{:S(2)}, u32[]{:S(2)}) collective-permute-start(bf16[2,192,1536]{2,1,0:T(8,128)(2,1)} %maximum_bitcast_fusion.1), channel_id=1, source_target_pairs={{0,2},{1,3},{2,0},{3,1},{4,6},{5,7},{6,4},{7,5},{8,10},{9,11},{10,... | collective-permute-start | bytes 3538952 | tf_op jit(solution)/shard_map/ppermute | solution.py:36
  187.8 87.5 %collective-permute-start.21 = (bf16[8,192,1536]{2,1,0:T(8,128)(2,1)}, bf16[8,192,1536]{2,1,0:T(8,128)(2,1)}, u32[]{:S(2)}, u32[]{:S(2)}) collective-permute-start(bf16[8,192,1536]{2,1,0:T(8,128)(2,1)} %bitcast.57), channel_id=1, source_target_pairs={{0,8},{8,0},{16,24},{24,16},{1,9},{9,1},{17,25},{25,17},{2,10},{10... | collective-permute-start | bytes 14155784 | tf_op jit(solution)/shard_map/ppermute | solution.py:36
  217.0 40.8 %collective-permute-start.18 = (bf16[576,1536]{1,0:T(8,128)(2,1)}, bf16[576,1536]{1,0:T(8,128)(2,1)}, u32[]{:S(2)}, u32[]{:S(2)}) collective-permute-start(bf16[576,1536]{1,0:T(8,128)(2,1)} %conv_norm_forward.1), channel_id=1, source_target_pairs={{0,16},{8,24},{16,0},{24,8},{1,17},{9,25},{17,1},{25,9},{2,18},{10... | collective-permute-start | bytes 5308424 | tf_op jit(solution)/shard_map/ppermute | solution.py:36
  230.5 56.0 %collective-permute-start.22 = (bf16[4,192,1536]{2,1,0:T(8,128)(2,1)S(1)}, bf16[4,192,1536]{2,1,0:T(8,128)(2,1)S(1)}, u32[]{:S(2)}, u32[]{:S(2)}) collective-permute-start(bf16[4,192,1536]{2,1,0:T(8,128)(2,1)S(1)} %bitcast.746), channel_id=1, source_target_pairs={{0,1},{1,0},{2,3},{3,2},{4,5},{5,4},{6,7},{7,6},{8,9},{9,8},{10,11... | collective-permute-start | bytes 7077896 | tf_op jit(solution)/shard_map/ppermute | solution.py:36
  290.6 49.7 %collective-permute-start.28 = (bf16[8,192,1536]{2,1,0:T(8,128)(2,1)}, bf16[8,192,1536]{2,1,0:T(8,128)(2,1)}, u32[]{:S(2)}, u32[]{:S(2)}) collective-permute-start(bf16[8,192,1536]{2,1,0:T(8,128)(2,1)} %bitcast.80), channel_id=1, source_target_pairs={{0,8},{8,0},{16,24},{24,16},{1,9},{9,1},{17,25},{25,17},{2,10},{10... | collective-permute-start | bytes 14155784 | tf_op jit(solution)/shard_map/ppermute | solution.py:36
  292.0 63.2 %collective-permute-start.27 = (bf16[144,576]{1,0:T(8,128)(2,1)S(1)}, bf16[144,576]{1,0:T(8,128)(2,1)}, u32[]{:S(2)}, u32[]{:S(2)}) collective-permute-start(bf16[144,576]{1,0:T(8,128)(2,1)S(1)} %bitcast.777), channel_id=1, source_target_pairs={{0,16},{8,24},{16,0},{24,8},{1,17},{9,25},{17,1},{25,9},{2,18},{10... | collective-permute-start | bytes 497672 | tf_op jit(solution)/shard_map/ppermute | solution.py:36
  303.8 66.7 %collective-permute-start.31 = (bf16[8,192,256]{2,1,0:T(8,128)(2,1)}, bf16[8,192,256]{2,1,0:T(8,128)(2,1)}, u32[]{:S(2)}, u32[]{:S(2)}) collective-permute-start(bf16[8,192,256]{2,1,0:T(8,128)(2,1)} %bitcast.92), channel_id=1, source_target_pairs={{0,8},{8,0},{16,24},{24,16},{1,9},{9,1},{17,25},{25,17},{2,10},{10... | collective-permute-start | bytes 2359304 | tf_op jit(solution)/shard_map/ppermute | solution.py:36
  307.8 32.6 %collective-permute-start.26 = (bf16[4,128,1024]{2,1,0:T(8,128)(2,1)}, bf16[4,128,1024]{2,1,0:T(8,128)(2,1)}, u32[]{:S(2)}, u32[]{:S(2)}) collective-permute-start(bf16[4,128,1024]{2,1,0:T(8,128)(2,1)} %bitcast.757), channel_id=1, source_target_pairs={{0,1},{1,0},{2,3},{3,2},{4,5},{5,4},{6,7},{7,6},{8,24},{9,25},{10,... | collective-permute-start | bytes 3145736 | tf_op jit(solution)/shard_map/ppermute | solution.py:89
  359.4 32.1 %collective-permute-start.34 = (bf16[8,128,1024]{2,1,0:T(8,128)(2,1)}, bf16[8,128,1024]{2,1,0:T(8,128)(2,1)}, u32[]{:S(2)}, u32[]{:S(2)}) collective-permute-start(bf16[8,128,1024]{2,1,0:T(8,128)(2,1)} %bitcast.104), channel_id=1, source_target_pairs={{0,8},{8,0},{16,24},{24,16},{1,9},{9,1},{17,25},{25,17},{2,10},{10... | collective-permute-start | bytes 6291464 | tf_op jit(solution)/shard_map/ppermute | solution.py:36
  361.7 34.0 %collective-permute-start.35 = (bf16[8,128,1024]{2,1,0:T(8,128)(2,1)}, bf16[8,128,1024]{2,1,0:T(8,128)(2,1)}, u32[]{:S(2)}, u32[]{:S(2)}) collective-permute-start(bf16[8,128,1024]{2,1,0:T(8,128)(2,1)} %bitcast.113), channel_id=1, source_target_pairs={{0,8},{8,0},{16,24},{24,16},{1,9},{9,1},{17,25},{25,17},{2,10},{10... | collective-permute-start | bytes 6291464 | tf_op jit(solution)/shard_map/ppermute | solution.py:36
  385.8 32.5 %collective-permute-start.40 = (bf16[4,128,1024]{2,1,0:T(8,128)(2,1)}, bf16[4,128,1024]{2,1,0:T(8,128)(2,1)}, u32[]{:S(2)}, u32[]{:S(2)}) collective-permute-start(bf16[4,128,1024]{2,1,0:T(8,128)(2,1)} %collective-permute-done.25), channel_id=1, source_target_pairs={{0,16},{1,17},{2,18},{3,19},{4,20},{5,21},{6,22},{7,23},{8,9},{9,8... | collective-permute-start | bytes 3145736 | tf_op jit(solution)/shard_map/ppermute | solution.py:89
  391.6 38.0 %collective-permute-start.42 = (bf16[4,128,1024]{2,1,0:T(8,128)(2,1)}, bf16[4,128,1024]{2,1,0:T(8,128)(2,1)}, u32[]{:S(2)}, u32[]{:S(2)}) collective-permute-start(bf16[4,128,1024]{2,1,0:T(8,128)(2,1)} %collective-permute-done.26), channel_id=1, source_target_pairs={{0,16},{1,17},{2,18},{3,19},{4,20},{5,21},{6,22},{7,23},{8,9},{9,8... | collective-permute-start | bytes 3145736 | tf_op jit(solution)/shard_map/ppermute | solution.py:89
  398.5 31.1 %collective-permute-start.36 = (bf16[144,768]{1,0:T(8,128)(2,1)}, bf16[144,768]{1,0:T(8,128)(2,1)S(1)}, u32[]{:S(2)}, u32[]{:S(2)}) collective-permute-start(bf16[144,768]{1,0:T(8,128)(2,1)} %get-tuple-element.458), channel_id=1, source_target_pairs={{0,1},{1,0},{2,3},{3,2},{4,5},{5,4},{6,7},{7,6},{8,9},{9,8},{10,11... | collective-permute-start | bytes 663560 | tf_op jit(solution)/shard_map/ppermute | solution.py:239
  462.0 31.0 %collective-permute-start.47 = (bf16[8,128,1024]{2,1,0:T(8,128)(2,1)}, bf16[8,128,1024]{2,1,0:T(8,128)(2,1)}, u32[]{:S(2)}, u32[]{:S(2)}) collective-permute-start(bf16[8,128,1024]{2,1,0:T(8,128)(2,1)} %bitcast.135), channel_id=1, source_target_pairs={{0,8},{8,0},{16,24},{24,16},{1,9},{9,1},{17,25},{25,17},{2,10},{10... | collective-permute-start | bytes 6291464 | tf_op jit(solution)/shard_map/ppermute | solution.py:36
  462.5 30.5 %collective-permute-start.46 = (bf16[8,128,1024]{2,1,0:T(8,128)(2,1)}, bf16[8,128,1024]{2,1,0:T(8,128)(2,1)}, u32[]{:S(2)}, u32[]{:S(2)}) collective-permute-start(bf16[8,128,1024]{2,1,0:T(8,128)(2,1)} %bitcast.129), channel_id=1, source_target_pairs={{0,8},{8,0},{16,24},{24,16},{1,9},{9,1},{17,25},{25,17},{2,10},{10... | collective-permute-start | bytes 6291464 | tf_op jit(solution)/shard_map/ppermute | solution.py:36
  512.2 42.7 %collective-permute-start.61 = (bf16[8,128,1024]{2,1,0:T(8,128)(2,1)}, bf16[8,128,1024]{2,1,0:T(8,128)(2,1)}, u32[]{:S(2)}, u32[]{:S(2)}) collective-permute-start(bf16[8,128,1024]{2,1,0:T(8,128)(2,1)} %bitcast.160), channel_id=1, source_target_pairs={{0,8},{8,0},{16,24},{24,16},{1,9},{9,1},{17,25},{25,17},{2,10},{10... | collective-permute-start | bytes 6291464 | tf_op jit(solution)/shard_map/ppermute | solution.py:36
  514.3 40.9 %collective-permute-start.60 = (bf16[8,128,1024]{2,1,0:T(8,128)(2,1)S(1)}, bf16[8,128,1024]{2,1,0:T(8,128)(2,1)}, u32[]{:S(2)}, u32[]{:S(2)}) collective-permute-start(bf16[8,128,1024]{2,1,0:T(8,128)(2,1)S(1)} %bitcast.715), channel_id=1, source_target_pairs={{0,8},{8,0},{16,24},{24,16},{1,9},{9,1},{17,25},{25,17},{2,10},{10... | collective-permute-start | bytes 6291464 | tf_op jit(solution)/shard_map/ppermute | solution.py:36
  533.6 49.3 %collective-permute-start.64 = (bf16[4,128,1024]{2,1,0:T(8,128)(2,1)}, bf16[4,128,1024]{2,1,0:T(8,128)(2,1)S(1)}, u32[]{:S(2)}, u32[]{:S(2)}) collective-permute-start(bf16[4,128,1024]{2,1,0:T(8,128)(2,1)} %dynamic-slice_bitcast_fusion.6), channel_id=1, source_target_pairs={{0,16},{1,17},{2,18},{3,19},{4,20},{5,21},{6,22},{7,23},{8,9},{9,8... | collective-permute-start | bytes 3145736 | tf_op jit(solution)/shard_map/ppermute | solution.py:89
  555.2 54.3 %collective-permute-start.67 = (bf16[8,128,1024]{2,1,0:T(8,128)(2,1)S(1)}, bf16[8,128,1024]{2,1,0:T(8,128)(2,1)S(1)}, u32[]{:S(2)}, u32[]{:S(2)}) collective-permute-start(bf16[8,128,1024]{2,1,0:T(8,128)(2,1)S(1)} %bitcast.718), channel_id=1, source_target_pairs={{0,8},{8,0},{16,24},{24,16},{1,9},{9,1},{17,25},{25,17},{2,10},{10... | collective-permute-start | bytes 6291464 | tf_op jit(solution)/shard_map/ppermute | solution.py:36
  556.4 53.2 %collective-permute-start.68 = (bf16[8,128,1024]{2,1,0:T(8,128)(2,1)S(1)}, bf16[8,128,1024]{2,1,0:T(8,128)(2,1)S(1)}, u32[]{:S(2)}, u32[]{:S(2)}) collective-permute-start(bf16[8,128,1024]{2,1,0:T(8,128)(2,1)S(1)} %bitcast.716), channel_id=1, source_target_pairs={{0,8},{8,0},{16,24},{24,16},{1,9},{9,1},{17,25},{25,17},{2,10},{10... | collective-permute-start | bytes 6291464 | tf_op jit(solution)/shard_map/ppermute | solution.py:36
  609.6 45.1 %collective-permute-start.71 = (bf16[8,192,1536]{2,1,0:T(8,128)(2,1)}, bf16[8,192,1536]{2,1,0:T(8,128)(2,1)}, u32[]{:S(2)}, u32[]{:S(2)}) collective-permute-start(bf16[8,192,1536]{2,1,0:T(8,128)(2,1)} %bitcast.181), channel_id=1, source_target_pairs={{0,8},{8,0},{16,24},{24,16},{1,9},{9,1},{17,25},{25,17},{2,10},{10... | collective-permute-start | bytes 14155784 | tf_op jit(solution)/shard_map/ppermute | solution.py:36
  616.2 134.7 %all-to-all-start.2 = ((bf16[8,144,192]{2,1,0:T(8,128)(2,1)}), bf16[8,144,192]{2,1,0:T(8,128)(2,1)}, u32[]{:S(2)}, u32[]{:S(2)}) async-start(bf16[8,144,192]{2,1,0:T(8,128)(2,1)} %bitcast.774), calls=%async_computation.2 | async-start | bytes 1179648 | tf_op jit(solution)/shard_map/all_to_all | solution.py:253
  635.4 55.3 %collective-permute-start.75 = (bf16[4,128,1024]{2,1,0:T(8,128)(2,1)}, bf16[4,128,1024]{2,1,0:T(8,128)(2,1)}, u32[]{:S(2)}, u32[]{:S(2)}) collective-permute-start(bf16[4,128,1024]{2,1,0:T(8,128)(2,1)} %fusion.30), channel_id=1, source_target_pairs={{0,1},{1,0},{2,3},{3,2},{4,5},{5,4},{6,7},{7,6},{8,24},{9,25},{10,... | collective-permute-start | bytes 3145736 | tf_op jit(solution)/shard_map/ppermute | solution.py:89
  637.1 53.6 %collective-permute-start.74 = (bf16[4,128,1024]{2,1,0:T(8,128)(2,1)S(1)}, bf16[4,128,1024]{2,1,0:T(8,128)(2,1)S(1)}, u32[]{:S(2)}, u32[]{:S(2)}) collective-permute-start(bf16[4,128,1024]{2,1,0:T(8,128)(2,1)S(1)} %dynamic-slice_bitcast_fusion.4), channel_id=1, source_target_pairs={{0,16},{1,17},{2,18},{3,19},{4,20},{5,21},{6,22},{7,23},{8,9},{9,8... | collective-permute-start | bytes 3145736 | tf_op jit(solution)/shard_map/ppermute | solution.py:89
  640.9 49.8 %collective-permute-start.73 = (bf16[4,128,1024]{2,1,0:T(8,128)(2,1)}, bf16[4,128,1024]{2,1,0:T(8,128)(2,1)S(1)}, u32[]{:S(2)}, u32[]{:S(2)}) collective-permute-start(bf16[4,128,1024]{2,1,0:T(8,128)(2,1)} %fusion.86), channel_id=1, source_target_pairs={{0,16},{1,17},{2,18},{3,19},{4,20},{5,21},{6,22},{7,23},{8,9},{9,8... | collective-permute-start | bytes 3145736 | tf_op jit(solution)/shard_map/ppermute | solution.py:89
  655.4 35.3 %collective-permute-start.76 = (bf16[2,128,1024]{2,1,0:T(8,128)(2,1)S(1)}, bf16[2,128,1024]{2,1,0:T(8,128)(2,1)S(1)}, u32[]{:S(2)}, u32[]{:S(2)}) collective-permute-start(bf16[2,128,1024]{2,1,0:T(8,128)(2,1)S(1)} %dynamic-slice_bitcast_fusion.9), channel_id=1, source_target_pairs={{0,2},{1,3},{2,0},{3,1},{4,6},{5,7},{6,4},{7,5},{8,10},{9,11},{10,... | collective-permute-start | bytes 1572872 | tf_op jit(solution)/shard_map/ppermute | solution.py:36
  698.7 65.6 %collective-permute-start.78 = (bf16[8,192,1536]{2,1,0:T(8,128)(2,1)}, bf16[8,192,1536]{2,1,0:T(8,128)(2,1)}, u32[]{:S(2)}, u32[]{:S(2)}) collective-permute-start(bf16[8,192,1536]{2,1,0:T(8,128)(2,1)} %bitcast.196), channel_id=1, source_target_pairs={{0,8},{8,0},{16,24},{24,16},{1,9},{9,1},{17,25},{25,17},{2,10},{10... | collective-permute-start | bytes 14155784 | tf_op jit(solution)/shard_map/ppermute | solution.py:36
  701.1 30.4 %collective-permute-start.83 = (bf16[4,192,256]{2,1,0:T(8,128)(2,1)}, bf16[4,192,256]{2,1,0:T(8,128)(2,1)}, u32[]{:S(2)}, u32[]{:S(2)}) collective-permute-start(bf16[4,192,256]{2,1,0:T(8,128)(2,1)} %dynamic-slice_bitcast_fusion.10), channel_id=1, source_target_pairs={{0,16},{1,17},{2,18},{3,19},{4,20},{5,21},{6,22},{7,23},{8,9},{9,8... | collective-permute-start | bytes 1179656 | tf_op jit(solution)/shard_map/ppermute | solution.py:89
  702.2 30.7 %collective-permute-start.82 = (bf16[4,192,256]{2,1,0:T(8,128)(2,1)}, bf16[4,192,256]{2,1,0:T(8,128)(2,1)}, u32[]{:S(2)}, u32[]{:S(2)}) collective-permute-start(bf16[4,192,256]{2,1,0:T(8,128)(2,1)} %fusion.121), channel_id=1, source_target_pairs={{0,16},{1,17},{2,18},{3,19},{4,20},{5,21},{6,22},{7,23},{8,9},{9,8... | collective-permute-start | bytes 1179656 | tf_op jit(solution)/shard_map/ppermute | solution.py:89
  711.1 53.3 %collective-permute-start.79 = (bf16[4,192,1536]{2,1,0:T(8,128)(2,1)}, bf16[4,192,1536]{2,1,0:T(8,128)(2,1)}, u32[]{:S(2)}, u32[]{:S(2)}) collective-permute-start(bf16[4,192,1536]{2,1,0:T(8,128)(2,1)} %dynamic-slice_bitcast_fusion.1), channel_id=1, source_target_pairs={{0,1},{1,0},{2,3},{3,2},{4,5},{5,4},{6,7},{7,6},{8,9},{9,8},{10,11... | collective-permute-start | bytes 7077896 | tf_op jit(solution)/shard_map/ppermute | solution.py:36
  716.4 41.8 %collective-permute-start.77 = (bf16[576,1536]{1,0:T(8,128)(2,1)}, bf16[576,1536]{1,0:T(8,128)(2,1)}, u32[]{:S(2)}, u32[]{:S(2)}) collective-permute-start(bf16[576,1536]{1,0:T(8,128)(2,1)} %slice.598), channel_id=1, source_target_pairs={{0,16},{8,24},{16,0},{24,8},{1,17},{9,25},{17,1},{25,9},{2,18},{10... | collective-permute-start | bytes 5308424 | tf_op jit(solution)/shard_map/ppermute | solution.py:36
  749.8 62.9 %collective-permute-start.86 = (bf16[4,128,1024]{2,1,0:T(8,128)(2,1)}, bf16[4,128,1024]{2,1,0:T(8,128)(2,1)}, u32[]{:S(2)}, u32[]{:S(2)}) collective-permute-start(bf16[4,128,1024]{2,1,0:T(8,128)(2,1)} %fusion.27), channel_id=1, source_target_pairs={{0,1},{1,0},{2,3},{3,2},{4,5},{5,4},{6,7},{7,6},{8,24},{9,25},{10,... | collective-permute-start | bytes 3145736 | tf_op jit(solution)/shard_map/ppermute | solution.py:89
  784.6 82.5 %all-to-all-start.3 = ((bf16[8,576,192]{1,2,0:T(8,128)(2,1)}), bf16[8,576,192]{1,2,0:T(8,128)(2,1)}, u32[]{:S(2)}, u32[]{:S(2)}) async-start(bf16[8,576,192]{1,2,0:T(8,128)(2,1)} %copy.242), calls=%async_computation.3 | async-start | bytes 3932160 | tf_op jit(solution)/shard_map/all_to_all | solution.py:253
  797.9 69.2 %collective-permute-start.84 = (bf16[4,192,1536]{2,1,0:T(8,128)(2,1)}, bf16[4,192,1536]{2,1,0:T(8,128)(2,1)}, u32[]{:S(2)}, u32[]{:S(2)}) collective-permute-start(bf16[4,192,1536]{2,1,0:T(8,128)(2,1)} %dynamic-slice_bitcast_fusion), channel_id=1, source_target_pairs={{0,1},{1,0},{2,3},{3,2},{4,5},{5,4},{6,7},{7,6},{8,9},{9,8},{10,11... | collective-permute-start | bytes 7077896 | tf_op jit(solution)/shard_map/ppermute | solution.py:36
  804.5 62.6 %collective-permute-start.85 = (bf16[2,192,1536]{2,1,0:T(8,128)(2,1)}, bf16[2,192,1536]{2,1,0:T(8,128)(2,1)}, u32[]{:S(2)}, u32[]{:S(2)}) collective-permute-start(bf16[2,192,1536]{2,1,0:T(8,128)(2,1)} %dynamic-slice_bitcast_fusion.3), channel_id=1, source_target_pairs={{0,2},{1,3},{2,0},{3,1},{4,6},{5,7},{6,4},{7,5},{8,10},{9,11},{10,... | collective-permute-start | bytes 3538952 | tf_op jit(solution)/shard_map/ppermute | solution.py:36
  807.0 44.3 %collective-permute-start.89 = (bf16[1,128,1024]{2,1,0:T(8,128)(2,1)}, bf16[1,128,1024]{2,1,0:T(8,128)(2,1)S(1)}, u32[]{:S(2)}, u32[]{:S(2)}) collective-permute-start(bf16[1,128,1024]{2,1,0:T(8,128)(2,1)} %constant_dynamic-slice_fusion.14), channel_id=1, source_target_pairs={{0,4},{1,5},{2,6},{3,7},{4,0},{5,1},{6,2},{7,3},{8,12},{9,13},{10,... | collective-permute-start | bytes 786440 | tf_op jit(solution)/shard_map/ppermute | solution.py:36
  810.2 41.2 %collective-permute-start.88 = (bf16[128,1024]{1,0:T(8,128)(2,1)}, bf16[128,1024]{1,0:T(8,128)(2,1)}, u32[]{:S(2)}, u32[]{:S(2)}) collective-permute-start(bf16[128,1024]{1,0:T(8,128)(2,1)} %fusion.123), channel_id=1, source_target_pairs={{0,16},{8,24},{16,0},{24,8},{1,17},{9,25},{17,1},{25,9},{2,18},{10... | collective-permute-start | bytes 786440 | tf_op jit(solution)/shard_map/ppermute | solution.py:36
  812.7 54.4 %collective-permute-start.87 = (bf16[4,192,256]{2,1,0:T(8,128)(2,1)}, bf16[4,192,256]{2,1,0:T(8,128)(2,1)}, u32[]{:S(2)}, u32[]{:S(2)}) collective-permute-start(bf16[4,192,256]{2,1,0:T(8,128)(2,1)} %fusion.101), channel_id=1, source_target_pairs={{0,1},{1,0},{2,3},{3,2},{4,5},{5,4},{6,7},{7,6},{8,24},{9,25},{10,... | collective-permute-start | bytes 1179656 | tf_op jit(solution)/shard_map/ppermute | solution.py:89
  851.3 35.8 %collective-permute-start.94 = (bf16[128,1024]{1,0:T(8,128)(2,1)}, bf16[128,1024]{1,0:T(8,128)(2,1)}, u32[]{:S(2)}, u32[]{:S(2)}) collective-permute-start(bf16[128,1024]{1,0:T(8,128)(2,1)} %fusion.123), channel_id=1, source_target_pairs={{0,8},{8,0},{16,24},{24,16},{1,9},{9,1},{17,25},{25,17},{2,10},{10... | collective-permute-start | bytes 786440 | tf_op jit(solution)/shard_map/ppermute | solution.py:36
  873.3 50.1 %collective-permute-start.92 = (bf16[2,128,1024]{2,1,0:T(8,128)(2,1)}, bf16[2,128,1024]{2,1,0:T(8,128)(2,1)}, u32[]{:S(2)}, u32[]{:S(2)}) collective-permute-start(bf16[2,128,1024]{2,1,0:T(8,128)(2,1)} %dynamic-slice_bitcast_fusion.7), channel_id=1, source_target_pairs={{0,2},{1,3},{2,0},{3,1},{4,6},{5,7},{6,4},{7,5},{8,10},{9,11},{10,... | collective-permute-start | bytes 1572872 | tf_op jit(solution)/shard_map/ppermute | solution.py:36
  878.6 44.8 %collective-permute-start.90 = (bf16[2,192,1536]{2,1,0:T(8,128)(2,1)}, bf16[2,192,1536]{2,1,0:T(8,128)(2,1)}, u32[]{:S(2)}, u32[]{:S(2)}) collective-permute-start(bf16[2,192,1536]{2,1,0:T(8,128)(2,1)} %dynamic-slice_bitcast_fusion.2), channel_id=1, source_target_pairs={{0,2},{1,3},{2,0},{3,1},{4,6},{5,7},{6,4},{7,5},{8,10},{9,11},{10,... | collective-permute-start | bytes 3538952 | tf_op jit(solution)/shard_map/ppermute | solution.py:36
  882.8 40.5 %collective-permute-start.91 = (bf16[1,192,1536]{2,1,0:T(8,128)(2,1)}, bf16[1,192,1536]{2,1,0:T(8,128)(2,1)}, u32[]{:S(2)}, u32[]{:S(2)}) collective-permute-start(bf16[1,192,1536]{2,1,0:T(8,128)(2,1)} %constant_dynamic-slice_fusion.13), channel_id=1, source_target_pairs={{0,4},{1,5},{2,6},{3,7},{4,0},{5,1},{6,2},{7,3},{8,12},{9,13},{10,... | collective-permute-start | bytes 1769480 | tf_op jit(solution)/shard_map/ppermute | solution.py:36
  887.1 36.3 %collective-permute-start.96 = (bf16[128,1024]{1,0:T(8,128)(2,1)S(1)}, bf16[128,1024]{1,0:T(8,128)(2,1)S(1)}, u32[]{:S(2)}, u32[]{:S(2)}) collective-permute-start(bf16[128,1024]{1,0:T(8,128)(2,1)S(1)} %fusion.124.refs_0_), channel_id=1, source_target_pairs={{0,16},{8,24},{16,0},{24,8},{1,17},{9,25},{17,1},{25,9},{2,18},{10... | collective-permute-start | bytes 786440 | tf_op jit(solution)/shard_map/ppermute | solution.py:36
  887.3 36.0 %collective-permute-start.95 = (bf16[128,1024]{1,0:T(8,128)(2,1)}, bf16[128,1024]{1,0:T(8,128)(2,1)}, u32[]{:S(2)}, u32[]{:S(2)}) collective-permute-start(bf16[128,1024]{1,0:T(8,128)(2,1)} %collective-permute-done.88), channel_id=1, source_target_pairs={{0,8},{8,0},{16,24},{24,16},{1,9},{9,1},{17,25},{25,17},{2,10},{10... | collective-permute-start | bytes 786440 | tf_op jit(solution)/shard_map/ppermute | solution.py:36
  923.3 33.8 %collective-permute-start.102 = (bf16[128,1024]{1,0:T(8,128)(2,1)S(1)}, bf16[128,1024]{1,0:T(8,128)(2,1)S(1)}, u32[]{:S(2)}, u32[]{:S(2)}) collective-permute-start(bf16[128,1024]{1,0:T(8,128)(2,1)S(1)} %fusion.124.refs_0_), channel_id=1, source_target_pairs={{0,8},{8,0},{16,24},{24,16},{1,9},{9,1},{17,25},{25,17},{2,10},{10... | collective-permute-start | bytes 786440 | tf_op jit(solution)/shard_map/ppermute | solution.py:36
  925.6 44.8 %collective-permute-start.100 = (bf16[1,128,1024]{2,1,0:T(8,128)(2,1)}, bf16[1,128,1024]{2,1,0:T(8,128)(2,1)}, u32[]{:S(2)}, u32[]{:S(2)}) collective-permute-start(bf16[1,128,1024]{2,1,0:T(8,128)(2,1)} %constant_dynamic-slice_fusion.10), channel_id=1, source_target_pairs={{0,4},{1,5},{2,6},{3,7},{4,0},{5,1},{6,2},{7,3},{8,12},{9,13},{10,... | collective-permute-start | bytes 786440 | tf_op jit(solution)/shard_map/ppermute | solution.py:36
  928.7 41.7 %collective-permute-start.99 = (bf16[192,1536]{1,0:T(8,128)(2,1)}, bf16[192,1536]{1,0:T(8,128)(2,1)}, u32[]{:S(2)}, u32[]{:S(2)}) collective-permute-start(bf16[192,1536]{1,0:T(8,128)(2,1)} %fusion.102), channel_id=1, source_target_pairs={{0,16},{8,24},{16,0},{24,8},{1,17},{9,25},{17,1},{25,9},{2,18},{10... | collective-permute-start | bytes 1769480 | tf_op jit(solution)/shard_map/ppermute | solution.py:36
  932.3 38.1 %collective-permute-start.98 = (bf16[1,192,1536]{2,1,0:T(8,128)(2,1)}, bf16[1,192,1536]{2,1,0:T(8,128)(2,1)}, u32[]{:S(2)}, u32[]{:S(2)}) collective-permute-start(bf16[1,192,1536]{2,1,0:T(8,128)(2,1)} %constant_dynamic-slice_fusion.11), channel_id=1, source_target_pairs={{0,4},{1,5},{2,6},{3,7},{4,0},{5,1},{6,2},{7,3},{8,12},{9,13},{10,... | collective-permute-start | bytes 1769480 | tf_op jit(solution)/shard_map/ppermute | solution.py:36
  935.2 35.2 %collective-permute-start.103 = (bf16[128,1024]{1,0:T(8,128)(2,1)S(1)}, bf16[128,1024]{1,0:T(8,128)(2,1)}, u32[]{:S(2)}, u32[]{:S(2)}) collective-permute-start(bf16[128,1024]{1,0:T(8,128)(2,1)S(1)} %collective-permute-done.96.refs_2_), channel_id=1, source_target_pairs={{0,8},{8,0},{16,24},{24,16},{1,9},{9,1},{17,25},{25,17},{2,10},{10... | collective-permute-start | bytes 786440 | tf_op jit(solution)/shard_map/ppermute | solution.py:36
  970.4 42.1 %collective-permute-start.117 = (bf16[192,1536]{1,0:T(8,128)(2,1)}, bf16[192,1536]{1,0:T(8,128)(2,1)S(1)}, u32[]{:S(2)}, u32[]{:S(2)}) collective-permute-start(bf16[192,1536]{1,0:T(8,128)(2,1)} %fusion.102), channel_id=1, source_target_pairs={{0,8},{8,0},{16,24},{24,16},{1,9},{9,1},{17,25},{25,17},{2,10},{10... | collective-permute-start | bytes 1769480 | tf_op jit(solution)/shard_map/ppermute | solution.py:36
  (294 other events, 4788.2 us)

commit v2 on v1

--- a/solution.py
+++ b/solution.py
@@ -1380,9 +1380,9 @@
         product = right_grad(grad_hidden[place], pw1[place])
         grad_normed_pair = product if grad_normed_pair is None else grad_normed_pair + product
     grad_normed_pair, grad_hidden = sync(
-        (grad_normed_pair, grad_hidden), joint_sum, fc1_sum, fc2_sum
-    )
-    grad_normed_other = flip(grad_normed_pair[BAND_CELLS:].astype(bf16), GRP, PAIR)
+        (grad_normed_pair.astype(bf16), grad_hidden), joint_sum, fc1_sum, fc2_sum
+    )
+    grad_normed_other = flip(grad_normed_pair[BAND_CELLS:], GRP, PAIR)
     pw1_grads = {}
     pw1_bias_grads = [jnp.zeros((parts, pw1_weight.shape[1] // parts // groups), f32)] * groups
     for place in reversed(conv_places):
@@ -1394,13 +1394,15 @@
         (grad_normed_other, resid_back), pw1_sum, pw2_sum, fc2_sum, fc1_sum, proj_sum
     )
     grad_conv_bands, norm_sums = conv_norm_backward(
-        conv_recv, small.conv_gain, grad_normed_pair[:BAND_CELLS], grad_normed_other
+        conv_recv, small.conv_gain, grad_normed_pair, grad_normed_other
     )
     grads.conv_gain, grads.conv_bias = norm_sums
     grad_conv_back = all_to_all(grad_conv_bands)
     resid_bands = batched(tables, resid_back, 1, 1).astype(bf16)
     others = (pw1_sum, pw2_sum, joint_sum, proj_sum, fc2_sum, fc1_sum)
-    grad_conv_back = sync(grad_conv_back, *others)
+    grad_conv_back, resid_bands = sync(
+        (grad_conv_back, resid_bands), pw1_sum, pw2_sum, joint_sum, fc2_sum, fc1_sum
+    )
 
     def half_way_back(value):
         value, bundle = lax.optimization_barrier(

time: 1030 us -> 1020 us (level)
    ppermute x24, waiting for transfers between devices: 40.4 us -> 22.8 us  [flip_crosswise(): return lax.ppermute(value, (GRP, CHAN), pairs)]
    ppermute x81, waiting for transfers between devices: 167 us -> 182 us  [flip(): lax.ppermute(value, axis, [(i, i ^ 1 << bit) for i in range(lax.axis_size...]
  transfers between devices with their start and end apart: 125 -> 125, of which waited for: 33 -> 36; matrix products, arithmetic and copies ran while one was open for 37% -> 37% of each run, Pallas kernels for 11% -> 11%
where the time goes in v2:
time: 1020 us; the launch traced here: 1010 us
  waiting for transfers between devices  248 us (24%)
  starting transfers between devices  198 us (19%)
  matrix products  176 us (17%)
  Pallas kernels  130 us (13%)
  local copies, waits for them, and re-layouts  128 us (13%)
  other arithmetic  121 us (12%)
  between operations  10.5 us (1%)
    ppermute x81, waiting for transfers between devices, flip(): lax.ppermute(value, axis, [(i, i ^ 1 << bit) for i in range(lax.axis_size...  182 us
    ppermute x81, starting transfers between devices, flip(): lax.ppermute(value, axis, [(i, i ^ 1 << bit) for i in range(lax.axis_size...  112 us
    dot_general x16, matrix products, matmul(): return jnp.dot(left, right, preferred_element_type=f32)  63.5 us
    dot_general x16, matrix products, right_grad(): lax.dot_general(grads, weight, (((1,), (1,)), ((), ())), preferred_elemen...  63.3 us
    convert_element_type x26, other arithmetic, added(): return (left.astype(f32) + right.astype(f32)).astype(left.dtype)  46.4 us
    unnamed x492, local copies, waits for them, and re-layouts  44.7 us
    pallas_call x2, Pallas kernels, conv_backward(): pl.pallas_call(partial(conv_backward_kernel, first=first), grid=(1,), in_...  38.8 us
    dot_general x8, matrix products, left_grad(): lax.dot_general(inputs, grads, (((0,), (0,)), ((), ())), preferred_elemen...  37.8 us
  transfers between devices with their start and end apart: 125, of which 36 were waited for; matrix products, arithmetic and copies ran while one was open for 37% of the time, Pallas kernels for 11%

profile of v2, /device:TPU:0, one launch (start us, length us, event | category | flops | bytes accessed | tf_op | source)
XLA Modules:
  0.0 1011.9 jit_solution(5162313153671901705)
XLA Ops:
  4.4 4.0 collective-permute-start.2
  26.8 16.2 %depthwise_forward.1 = (bf16[2304,256]{1,0:T(8,128)(2,1)S(1)}, bf16[2304,256]{1,0:T(8,128)(2,1)S(1)}) custom-call(s32[1,384]{1,0:T(1,128)S(1)} %broadcast_in_dim_reshape.18.sizes_ref, f32[49,384]{1,0:T(8,128)S(1)} %tile.18.taps_ref, f32[1,384]{1,0:T(1,128)S(1)} %tile.20.bias_ref, bf16[384,2304]{1,0:T(8,128)(2,1)S(1)} %bitcast.684), custom_call_target="tpu_custom_call" | custom-call | tf_op jit(solution)/shard_map/depthwise_forward/pallas_call | solution.py:490
  47.7 4.1 collective-permute-done.1
  61.3 9.7 depthwise_forward_last.1
  81.8 4.0 collective-permute-start.8
  91.4 4.7 all-to-all-start
  98.8 14.2 %collective-permute-done.8 = bf16[1,192,1536]{2,1,0:T(8,128)(2,1)} collective-permute-done((bf16[1,192,1536]{2,1,0:T(8,128)(2,1)}, bf16[1,192,1536]{2,1,0:T(8,128)(2,1)}, u32[]{:S(2)}, u32[]{:S(2)}) %collective-permute-start.8) | collective-permute-done | bytes 589856 | tf_op jit(solution)/shard_map/ppermute | solution.py:36
  116.3 4.6 collective-permute-start.12
  129.3 24.9 %all-to-all-done = bf16[8,576,192]{1,2,0:T(8,128)(2,1)} async-done(((bf16[8,576,192]{1,2,0:T(8,128)(2,1)}), bf16[8,576,192]{1,2,0:T(8,128)(2,1)}, u32[]{:S(2)}, u32[]{:S(2)}) %all-to-all-start) | async-done | bytes 1769504 | tf_op jit(solution)/shard_map/all_to_all | solution.py:253
  157.1 4.4 conv_norm_forward.1
  161.5 20.8 %collective-permute-done.12 = bf16[4,192,1536]{2,1,0:T(8,128)(2,1)} collective-permute-done((bf16[4,192,1536]{2,1,0:T(8,128)(2,1)}, bf16[4,192,1536]{2,1,0:T(8,128)(2,1)}, u32[]{:S(2)}, u32[]{:S(2)}) %collective-permute-start.12) | collective-permute-done | bytes 2359328 | tf_op jit(solution)/shard_map/ppermute | solution.py:36
  187.9 29.1 %collective-permute-start.21 = (bf16[8,192,1536]{2,1,0:T(8,128)(2,1)}, bf16[8,192,1536]{2,1,0:T(8,128)(2,1)}, u32[]{:S(2)}, u32[]{:S(2)}) collective-permute-start(bf16[8,192,1536]{2,1,0:T(8,128)(2,1)} %bitcast.57), channel_id=1, source_target_pairs={{0,8},{8,0},{16,24},{24,16},{1,9},{9,1},{17,25},{25,17},{2,10},{10... | collective-permute-start | bytes 14155784 | tf_op jit(solution)/shard_map/ppermute | solution.py:36
  232.2 12.0 %collective-permute-done.19 = bf16[1,128,1024]{1,2,0:T(8,128)(2,1)} collective-permute-done((bf16[1,128,1024]{1,2,0:T(8,128)(2,1)}, bf16[1,128,1024]{1,2,0:T(8,128)(2,1)}, u32[]{:S(2)}, u32[]{:S(2)}) %collective-permute-start.19) | collective-permute-done | bytes 262176 | tf_op jit(solution)/shard_map/ppermute | solution.py:36
  244.1 4.2 collective-permute-done.20
  248.4 9.4 collective-permute-done.18
  263.6 11.7 %multiply_convert_fusion.1 = (bf16[1152,1536]{1,0:T(8,128)(2,1)}, f32[1152,1536]{1,0:T(8,128)}) fusion(f32[1536]{0:T(1024)S(1)} %add.565, bf16[1152,1536]{1,0:T(8,128)(2,1)S(1)} %constant_dynamic-update-slice_fusion, bf16[1536,1536]{1,0:T(8,128)(2,1)} %bitcast.56), kind=kOutput, calls=%fused_computation.33 | convolution fusion | flops 5446434816 | bytes 18880512 | tf_op jit(solution)/shard_map/dot_general | solution.py:274
  275.3 10.8 %multiply_convert_fusion = (bf16[1152,1536]{1,0:T(8,128)(2,1)}, f32[1152,1536]{1,0:T(8,128)}) fusion(f32[1536]{0:T(1024)S(1)} %add.570, bf16[1152,1536]{1,0:T(8,128)(2,1)S(1)} %constant_dynamic-update-slice_fusion, bf16[1536,1536]{1,0:T(8,128)(2,1)} %bitcast.58), kind=kOutput, calls=%fused_computation.31 | convolution fusion | flops 5446434816 | bytes 18880512 | tf_op jit(solution)/shard_map/dot_general | solution.py:274
  294.8 3.8 select_bitcast_fusion.17
  314.0 8.7 all-to-all-start.1
  322.6 10.4 %fusion.188 = f32[1152,1536]{1,0:T(8,128)} fusion(bf16[1152,1536]{1,0:T(8,128)(2,1)} %get-tuple-element.228, bf16[1536,1536]{1,0:T(8,128)(2,1)} %bitcast.70), kind=kOutput, calls=%fused_computation.625 | convolution fusion | flops 5435817984 | bytes 15335424 | tf_op jit(solution)/shard_map/dot_general | solution.py:274
  333.1 7.0 all-to-all-done.1
  340.1 10.6 %fusion.189 = f32[1152,1536]{1,0:T(8,128)} fusion(bf16[1152,1536]{1,0:T(8,128)(2,1)} %get-tuple-element.235, bf16[1536,1536]{1,0:T(8,128)(2,1)} %bitcast.81), kind=kOutput, calls=%fused_computation.626 | convolution fusion | flops 5435817984 | bytes 15335424 | tf_op jit(solution)/shard_map/dot_general | solution.py:274
  350.7 4.2 add_convert_fusion
  374.8 4.1 collective-permute-start.32
  398.8 5.7 collective-permute-start.37
  407.7 6.1 collective-permute-start.38
  418.0 11.2 %collective-permute-done.42 = bf16[4,128,1024]{2,1,0:T(8,128)(2,1)} collective-permute-done((bf16[4,128,1024]{2,1,0:T(8,128)(2,1)}, bf16[4,128,1024]{2,1,0:T(8,128)(2,1)}, u32[]{:S(2)}, u32[]{:S(2)}) %collective-permute-start.42) | collective-permute-done | bytes 1048608 | tf_op jit(solution)/shard_map/ppermute | solution.py:89
  437.9 4.6 attention_forward.1
  442.6 6.2 collective-permute-start.43
  449.4 8.9 collective-permute-start.49
  473.0 5.9 mlp_piece.4
  479.0 5.5 mlp_piece.5
  487.2 5.5 mlp_piece.6
  492.8 6.8 mlp_piece.7
  517.4 6.6 attention_backward.1
  575.5 7.1 collective-permute-done.62
  586.1 8.3 convolution_convert_fusion.2
  595.8 8.0 convolution_convert_fusion.3
  603.8 5.4 collective-permute-done.65
  615.9 6.9 all-to-all-start.2
  641.9 10.2 %fusion.3 = bf16[1152,1536]{1,0:T(8,128)(2,1)S(1)} fusion(bf16[1152,1536]{1,0:T(8,128)(2,1)S(1)} %bitcast.770, bf16[1536,1536]{1,0:T(8,128)(2,1)} %bitcast.81, f32[1152,1536]{1,0:T(8,128)} %get-tuple-element.605), kind=kOutput, calls=%fused_computation.12 | convolution fusion | flops 5457051648 | bytes 18874368 | tf_op jit(solution)/shard_map/dot_general | solution.py:284
  657.0 10.2 %fusion.4 = bf16[1152,1536]{1,0:T(8,128)(2,1)S(1)} fusion(bf16[1152,1536]{1,0:T(8,128)(2,1)S(1)} %bitcast.771, bf16[1536,1536]{1,0:T(8,128)(2,1)} %bitcast.70, f32[1152,1536]{1,0:T(8,128)} %get-tuple-element.603), kind=kOutput, calls=%fused_computation.13 | convolution fusion | flops 5457051648 | bytes 18874368 | tf_op jit(solution)/shard_map/dot_general | solution.py:284
  667.2 11.4 %fusion.193 = f32[1152,1536]{1,0:T(8,128)} fusion(bf16[1152,1536]{1,0:T(8,128)(2,1)S(1)} %fusion.4, bf16[1536,1536]{1,0:T(8,128)(2,1)} %bitcast.56), kind=kOutput, calls=%fused_computation.630 | convolution fusion | flops 5435817984 | bytes 15335424 | tf_op jit(solution)/shard_map/dot_general | solution.py:284
  678.5 9.5 fusion.2.own_ref
  688.1 8.0 convolution_convert_fusion.1
  701.7 5.2 fusion.1
  713.1 7.9 convolution_convert_fusion
  730.1 12.1 %collective-permute-done.80 = bf16[1,128,1024]{2,1,0:T(8,128)(2,1)S(1)} collective-permute-done((bf16[1,128,1024]{2,1,0:T(8,128)(2,1)S(1)}, bf16[1,128,1024]{2,1,0:T(8,128)(2,1)S(1)}, u32[]{:S(2)}, u32[]{:S(2)}) %collective-permute-start.80) | collective-permute-done | bytes 262176 | tf_op jit(solution)/shard_map/ppermute | solution.py:36
  744.7 7.1 collective-permute-done.77.other_ref
  751.8 10.1 collective-permute-done.79
  763.9 12.6 %conv_norm_backward.1 = (bf16[8,576,192]{2,1,0:T(8,128)(2,1)S(1)}, f32[2,1536]{1,0:T(2,128)S(1)}) custom-call(bf16[8,576,192]{2,1,0:T(8,128)(2,1)S(1)} %copy.200.blocks_ref, f32[1,1536]{1,0:T(1,128)S(1)} %copy-done.39, bf16[1152,1536]{1,0:T(8,128)(2,1)S(1)} %copy-done.4, bf16[576,1536]{1,0:T(8,128)(2,1)} %collective-permute-done.77.other_ref), custom_call_target="tpu_custom_call" | custom-call | tf_op jit(solution)/shard_map/conv_norm_backward/pallas_call | solution.py:628
  777.9 4.2 copy.242
  782.1 4.5 all-to-all-start.3
  786.6 5.2 fusion
  808.4 4.5 convolution_convert_fusion.9.resid_ref
  814.7 34.2 %collective-permute-done.88 = bf16[1,128,1024]{2,1,0:T(8,128)(2,1)S(1)} collective-permute-done((bf16[1,128,1024]{2,1,0:T(8,128)(2,1)S(1)}, bf16[1,128,1024]{2,1,0:T(8,128)(2,1)S(1)}, u32[]{:S(2)}, u32[]{:S(2)}) %collective-permute-start.88) | collective-permute-done | bytes 262176 | tf_op jit(solution)/shard_map/ppermute | solution.py:36
  851.8 8.8 collective-permute-done.84
  872.1 5.0 collective-permute-start.90
  883.7 24.9 %depthwise_backward.2 = (f32[384,2304]{1,0:T(8,128)}, f32[50,256]{1,0:T(8,128)S(1)}) custom-call(s32[2]{0:T(128)S(1)} %copy-done.43, s32[1,384]{1,0:T(1,128)S(1)} %copy-done.41, f32[49,384]{1,0:T(8,128)S(1)} %copy-done.18, bf16[2304,384]{1,0:T(8,128)(2,1)S(1)} %copy-done.8, bf16[8,576,192]{2,1,0:T(8,128)(2,1)S(1)} %copy.254.grad_ref, ...), custom_call_target="tpu_custom_call" | custom-call | tf_op jit(solution)/shard_map/depthwise_backward/pallas_call | solution.py:519
  909.1 4.4 collective-permute-done.90
  917.7 3.4 collective-permute-start.100
  927.7 13.9 %depthwise_backward.3 = (f32[384,2304]{1,0:T(8,128)}, f32[50,128]{1,0:T(8,128)S(1)}) custom-call(s32[2]{0:T(128)S(1)} %copy-done.43, s32[1,384]{1,0:T(1,128)S(1)} %copy-done.41, f32[49,384]{1,0:T(8,128)S(1)} %copy-done.18, bf16[2304,384]{1,0:T(8,128)(2,1)S(1)} %copy-done.8, ...), custom_call_target="tpu_custom_call", output_to_operand_aliasing={{0}: (6, {})} | custom-call | tf_op jit(solution)/shard_map/depthwise_backward/pallas_call | solution.py:519
  950.0 13.9 %collective-permute-done.99 = bf16[1,128,1024]{2,1,0:T(8,128)(2,1)} collective-permute-done((bf16[1,128,1024]{2,1,0:T(8,128)(2,1)S(1)}, bf16[1,128,1024]{2,1,0:T(8,128)(2,1)}, u32[]{:S(2)}, u32[]{:S(2)}) %collective-permute-start.99) | collective-permute-done | bytes 262176 | tf_op jit(solution)/shard_map/ppermute | solution.py:36
  985.0 12.5 %collective-permute-done.118 = bf16[192,256]{1,0:T(8,128)(2,1)S(1)} collective-permute-done((bf16[192,256]{1,0:T(8,128)(2,1)S(1)}, bf16[192,256]{1,0:T(8,128)(2,1)S(1)}, u32[]{:S(2)}, u32[]{:S(2)}) %collective-permute-start.118) | collective-permute-done | bytes 98336 | tf_op jit(solution)/shard_map/ppermute | solution.py:36
  (1020 shorter events, 411.4 us)
Async XLA Ops:
  4.4 47.4 %collective-permute-start.2 = (bf16[1,128,1024]{1,2,0:T(8,128)(2,1)}, bf16[1,128,1024]{1,2,0:T(8,128)(2,1)}, u32[]{:S(2)}, u32[]{:S(2)}) collective-permute-start(bf16[1,128,1024]{1,2,0:T(8,128)(2,1)} %maximum_bitcast_fusion.5), channel_id=1, source_target_pairs={{0,4},{1,5},{2,6},{3,7},{4,0},{5,1},{6,2},{7,3},{8,12},{9,13},{10,... | collective-permute-start | bytes 786440 | tf_op jit(solution)/shard_map/ppermute | solution.py:36
  8.8 36.2 %collective-permute-start = (f32[1,36,128]{2,1,0:T(8,128)S(1)}, f32[1,36,128]{2,1,0:T(8,128)}, u32[]{:S(2)}, u32[]{:S(2)}) collective-permute-start(f32[1,36,128]{2,1,0:T(8,128)S(1)} %bitcast.800), channel_id=1, source_target_pairs={{0,4},{1,5},{2,6},{3,7},{4,0},{5,1},{6,2},{7,3},{8,12},{9,13},{10,... | collective-permute-start | bytes 55304 | tf_op jit(solution)/shard_map/ppermute | solution.py:36
  10.1 41.7 %collective-permute-start.3 = (bf16[1,192,256]{2,1,0:T(8,128)(2,1)}, bf16[1,192,256]{2,1,0:T(8,128)(2,1)}, u32[]{:S(2)}, u32[]{:S(2)}) collective-permute-start(bf16[1,192,256]{2,1,0:T(8,128)(2,1)} %bitcast.676), channel_id=1, source_target_pairs={{0,4},{1,5},{2,6},{3,7},{4,0},{5,1},{6,2},{7,3},{8,12},{9,13},{10,... | collective-permute-start | bytes 294920 | tf_op jit(solution)/shard_map/ppermute | solution.py:36
  15.7 36.1 %collective-permute-start.4 = (bf16[1,192,1536]{2,1,0:T(8,128)(2,1)}, bf16[1,192,1536]{2,1,0:T(8,128)(2,1)}, u32[]{:S(2)}, u32[]{:S(2)}) collective-permute-start(bf16[1,192,1536]{2,1,0:T(8,128)(2,1)} %bitcast.21), channel_id=1, source_target_pairs={{0,4},{1,5},{2,6},{3,7},{4,0},{5,1},{6,2},{7,3},{8,12},{9,13},{10,... | collective-permute-start | bytes 1769480 | tf_op jit(solution)/shard_map/ppermute | solution.py:36
  56.9 41.9 %collective-permute-start.11 = (f32[4,36,128]{2,0,1:T(4,128)}, f32[4,36,128]{2,0,1:T(4,128)}, u32[]{:S(2)}, u32[]{:S(2)}) collective-permute-start(f32[4,36,128]{2,0,1:T(4,128)} %bitcast.42), channel_id=1, source_target_pairs={{0,1},{1,0},{2,3},{3,2},{4,5},{5,4},{6,7},{7,6},{8,9},{9,8},{10,11... | collective-permute-start | bytes 221192 | tf_op jit(solution)/shard_map/ppermute | solution.py:36
  61.2 51.8 %collective-permute-start.7 = (bf16[2,192,1536]{2,1,0:T(8,128)(2,1)}, bf16[2,192,1536]{2,1,0:T(8,128)(2,1)}, u32[]{:S(2)}, u32[]{:S(2)}) collective-permute-start(bf16[2,192,1536]{2,1,0:T(8,128)(2,1)} %maximum_bitcast_fusion), channel_id=1, source_target_pairs={{0,2},{1,3},{2,0},{3,1},{4,6},{5,7},{6,4},{7,5},{8,10},{9,11},{10,... | collective-permute-start | bytes 3538952 | tf_op jit(solution)/shard_map/ppermute | solution.py:36
  79.2 33.8 %collective-permute-start.9 = (bf16[4,128,1024]{2,1,0:T(8,128)(2,1)}, bf16[4,128,1024]{2,1,0:T(8,128)(2,1)}, u32[]{:S(2)}, u32[]{:S(2)}) collective-permute-start(bf16[4,128,1024]{2,1,0:T(8,128)(2,1)} %bitcast.755), channel_id=1, source_target_pairs={{0,1},{1,0},{2,3},{3,2},{4,5},{5,4},{6,7},{7,6},{8,24},{9,25},{10,... | collective-permute-start | bytes 3145736 | tf_op jit(solution)/shard_map/ppermute | solution.py:89
  81.8 31.2 %collective-permute-start.8 = (bf16[1,192,1536]{2,1,0:T(8,128)(2,1)}, bf16[1,192,1536]{2,1,0:T(8,128)(2,1)}, u32[]{:S(2)}, u32[]{:S(2)}) collective-permute-start(bf16[1,192,1536]{2,1,0:T(8,128)(2,1)} %constant_dynamic-slice_fusion.29), channel_id=1, source_target_pairs={{0,4},{1,5},{2,6},{3,7},{4,0},{5,1},{6,2},{7,3},{8,12},{9,13},{10,... | collective-permute-start | bytes 1769480 | tf_op jit(solution)/shard_map/ppermute | solution.py:36
  91.4 62.8 %all-to-all-start = ((bf16[8,576,192]{1,2,0:T(8,128)(2,1)}), bf16[8,576,192]{1,2,0:T(8,128)(2,1)}, u32[]{:S(2)}, u32[]{:S(2)}) async-start(bf16[8,576,192]{1,2,0:T(8,128)(2,1)} %copy.194), calls=%async_computation | async-start | bytes 3932160 | tf_op jit(solution)/shard_map/all_to_all | solution.py:253
  116.3 66.0 %collective-permute-start.12 = (bf16[4,192,1536]{2,1,0:T(8,128)(2,1)}, bf16[4,192,1536]{2,1,0:T(8,128)(2,1)}, u32[]{:S(2)}, u32[]{:S(2)}) collective-permute-start(bf16[4,192,1536]{2,1,0:T(8,128)(2,1)} %bitcast.47), channel_id=1, source_target_pairs={{0,1},{1,0},{2,3},{3,2},{4,5},{5,4},{6,7},{7,6},{8,9},{9,8},{10,11... | collective-permute-start | bytes 7077896 | tf_op jit(solution)/shard_map/ppermute | solution.py:36
  120.8 40.6 %collective-permute-start.15 = (bf16[4,192,256]{2,1,0:T(8,128)(2,1)}, bf16[4,192,256]{2,1,0:T(8,128)(2,1)}, u32[]{:S(2)}, u32[]{:S(2)}) collective-permute-start(bf16[4,192,256]{2,1,0:T(8,128)(2,1)} %bitcast.39), channel_id=1, source_target_pairs={{0,16},{1,17},{2,18},{3,19},{4,20},{5,21},{6,22},{7,23},{8,9},{9,8... | collective-permute-start | bytes 1179656 | tf_op jit(solution)/shard_map/ppermute | solution.py:89
  120.8 40.6 %collective-permute-start.13 = (bf16[4,128,1024]{2,1,0:T(8,128)(2,1)}, bf16[4,128,1024]{2,1,0:T(8,128)(2,1)}, u32[]{:S(2)}, u32[]{:S(2)}) collective-permute-start(bf16[4,128,1024]{2,1,0:T(8,128)(2,1)} %bitcast.756), channel_id=1, source_target_pairs={{0,16},{1,17},{2,18},{3,19},{4,20},{5,21},{6,22},{7,23},{8,9},{9,8... | collective-permute-start | bytes 3145736 | tf_op jit(solution)/shard_map/ppermute | solution.py:89
  122.8 38.6 %collective-permute-start.14 = (bf16[4,128,1024]{2,1,0:T(8,128)(2,1)}, bf16[4,128,1024]{2,1,0:T(8,128)(2,1)}, u32[]{:S(2)}, u32[]{:S(2)}) collective-permute-start(bf16[4,128,1024]{2,1,0:T(8,128)(2,1)} %collective-permute-done.9), channel_id=1, source_target_pairs={{0,16},{1,17},{2,18},{3,19},{4,20},{5,21},{6,22},{7,23},{8,9},{9,8... | collective-permute-start | bytes 3145736 | tf_op jit(solution)/shard_map/ppermute | solution.py:89
  124.0 37.5 %collective-permute-start.16 = (bf16[4,192,256]{2,1,0:T(8,128)(2,1)}, bf16[4,192,256]{2,1,0:T(8,128)(2,1)}, u32[]{:S(2)}, u32[]{:S(2)}) collective-permute-start(bf16[4,192,256]{2,1,0:T(8,128)(2,1)} %collective-permute-done.10), channel_id=1, source_target_pairs={{0,16},{1,17},{2,18},{3,19},{4,20},{5,21},{6,22},{7,23},{8,9},{9,8... | collective-permute-start | bytes 1179656 | tf_op jit(solution)/shard_map/ppermute | solution.py:89
  161.5 66.9 %collective-permute-start.17 = (bf16[2,192,1536]{2,1,0:T(8,128)(2,1)}, bf16[2,192,1536]{2,1,0:T(8,128)(2,1)}, u32[]{:S(2)}, u32[]{:S(2)}) collective-permute-start(bf16[2,192,1536]{2,1,0:T(8,128)(2,1)} %maximum_bitcast_fusion.1), channel_id=1, source_target_pairs={{0,2},{1,3},{2,0},{3,1},{4,6},{5,7},{6,4},{7,5},{8,10},{9,11},{10,... | collective-permute-start | bytes 3538952 | tf_op jit(solution)/shard_map/ppermute | solution.py:36
  187.9 87.4 %collective-permute-start.21 = (bf16[8,192,1536]{2,1,0:T(8,128)(2,1)}, bf16[8,192,1536]{2,1,0:T(8,128)(2,1)}, u32[]{:S(2)}, u32[]{:S(2)}) collective-permute-start(bf16[8,192,1536]{2,1,0:T(8,128)(2,1)} %bitcast.57), channel_id=1, source_target_pairs={{0,8},{8,0},{16,24},{24,16},{1,9},{9,1},{17,25},{25,17},{2,10},{10... | collective-permute-start | bytes 14155784 | tf_op jit(solution)/shard_map/ppermute | solution.py:36
  217.0 40.8 %collective-permute-start.18 = (bf16[576,1536]{1,0:T(8,128)(2,1)}, bf16[576,1536]{1,0:T(8,128)(2,1)}, u32[]{:S(2)}, u32[]{:S(2)}) collective-permute-start(bf16[576,1536]{1,0:T(8,128)(2,1)} %conv_norm_forward.1), channel_id=1, source_target_pairs={{0,16},{8,24},{16,0},{24,8},{1,17},{9,25},{17,1},{25,9},{2,18},{10... | collective-permute-start | bytes 5308424 | tf_op jit(solution)/shard_map/ppermute | solution.py:36
  230.5 55.8 %collective-permute-start.22 = (bf16[4,192,1536]{2,1,0:T(8,128)(2,1)S(1)}, bf16[4,192,1536]{2,1,0:T(8,128)(2,1)S(1)}, u32[]{:S(2)}, u32[]{:S(2)}) collective-permute-start(bf16[4,192,1536]{2,1,0:T(8,128)(2,1)S(1)} %bitcast.746), channel_id=1, source_target_pairs={{0,1},{1,0},{2,3},{3,2},{4,5},{5,4},{6,7},{7,6},{8,9},{9,8},{10,11... | collective-permute-start | bytes 7077896 | tf_op jit(solution)/shard_map/ppermute | solution.py:36
  290.4 49.7 %collective-permute-start.28 = (bf16[8,192,1536]{2,1,0:T(8,128)(2,1)}, bf16[8,192,1536]{2,1,0:T(8,128)(2,1)}, u32[]{:S(2)}, u32[]{:S(2)}) collective-permute-start(bf16[8,192,1536]{2,1,0:T(8,128)(2,1)} %bitcast.80), channel_id=1, source_target_pairs={{0,8},{8,0},{16,24},{24,16},{1,9},{9,1},{17,25},{25,17},{2,10},{10... | collective-permute-start | bytes 14155784 | tf_op jit(solution)/shard_map/ppermute | solution.py:36
  291.8 63.1 %collective-permute-start.27 = (bf16[144,576]{1,0:T(8,128)(2,1)S(1)}, bf16[144,576]{1,0:T(8,128)(2,1)}, u32[]{:S(2)}, u32[]{:S(2)}) collective-permute-start(bf16[144,576]{1,0:T(8,128)(2,1)S(1)} %bitcast.775), channel_id=1, source_target_pairs={{0,16},{8,24},{16,0},{24,8},{1,17},{9,25},{17,1},{25,9},{2,18},{10... | collective-permute-start | bytes 497672 | tf_op jit(solution)/shard_map/ppermute | solution.py:36
  303.6 66.6 %collective-permute-start.31 = (bf16[8,192,256]{2,1,0:T(8,128)(2,1)}, bf16[8,192,256]{2,1,0:T(8,128)(2,1)}, u32[]{:S(2)}, u32[]{:S(2)}) collective-permute-start(bf16[8,192,256]{2,1,0:T(8,128)(2,1)} %bitcast.92), channel_id=1, source_target_pairs={{0,8},{8,0},{16,24},{24,16},{1,9},{9,1},{17,25},{25,17},{2,10},{10... | collective-permute-start | bytes 2359304 | tf_op jit(solution)/shard_map/ppermute | solution.py:36
  307.5 32.6 %collective-permute-start.26 = (bf16[4,128,1024]{2,1,0:T(8,128)(2,1)}, bf16[4,128,1024]{2,1,0:T(8,128)(2,1)}, u32[]{:S(2)}, u32[]{:S(2)}) collective-permute-start(bf16[4,128,1024]{2,1,0:T(8,128)(2,1)} %bitcast.757), channel_id=1, source_target_pairs={{0,1},{1,0},{2,3},{3,2},{4,5},{5,4},{6,7},{7,6},{8,24},{9,25},{10,... | collective-permute-start | bytes 3145736 | tf_op jit(solution)/shard_map/ppermute | solution.py:89
  359.2 32.1 %collective-permute-start.34 = (bf16[8,128,1024]{2,1,0:T(8,128)(2,1)}, bf16[8,128,1024]{2,1,0:T(8,128)(2,1)}, u32[]{:S(2)}, u32[]{:S(2)}) collective-permute-start(bf16[8,128,1024]{2,1,0:T(8,128)(2,1)} %bitcast.104), channel_id=1, source_target_pairs={{0,8},{8,0},{16,24},{24,16},{1,9},{9,1},{17,25},{25,17},{2,10},{10... | collective-permute-start | bytes 6291464 | tf_op jit(solution)/shard_map/ppermute | solution.py:36
  361.4 34.0 %collective-permute-start.35 = (bf16[8,128,1024]{2,1,0:T(8,128)(2,1)}, bf16[8,128,1024]{2,1,0:T(8,128)(2,1)}, u32[]{:S(2)}, u32[]{:S(2)}) collective-permute-start(bf16[8,128,1024]{2,1,0:T(8,128)(2,1)} %bitcast.113), channel_id=1, source_target_pairs={{0,8},{8,0},{16,24},{24,16},{1,9},{9,1},{17,25},{25,17},{2,10},{10... | collective-permute-start | bytes 6291464 | tf_op jit(solution)/shard_map/ppermute | solution.py:36
  385.5 32.5 %collective-permute-start.40 = (bf16[4,128,1024]{2,1,0:T(8,128)(2,1)}, bf16[4,128,1024]{2,1,0:T(8,128)(2,1)}, u32[]{:S(2)}, u32[]{:S(2)}) collective-permute-start(bf16[4,128,1024]{2,1,0:T(8,128)(2,1)} %collective-permute-done.25), channel_id=1, source_target_pairs={{0,16},{1,17},{2,18},{3,19},{4,20},{5,21},{6,22},{7,23},{8,9},{9,8... | collective-permute-start | bytes 3145736 | tf_op jit(solution)/shard_map/ppermute | solution.py:89
  391.3 38.0 %collective-permute-start.42 = (bf16[4,128,1024]{2,1,0:T(8,128)(2,1)}, bf16[4,128,1024]{2,1,0:T(8,128)(2,1)}, u32[]{:S(2)}, u32[]{:S(2)}) collective-permute-start(bf16[4,128,1024]{2,1,0:T(8,128)(2,1)} %collective-permute-done.26), channel_id=1, source_target_pairs={{0,16},{1,17},{2,18},{3,19},{4,20},{5,21},{6,22},{7,23},{8,9},{9,8... | collective-permute-start | bytes 3145736 | tf_op jit(solution)/shard_map/ppermute | solution.py:89
  398.2 31.1 %collective-permute-start.36 = (bf16[144,768]{1,0:T(8,128)(2,1)}, bf16[144,768]{1,0:T(8,128)(2,1)S(1)}, u32[]{:S(2)}, u32[]{:S(2)}) collective-permute-start(bf16[144,768]{1,0:T(8,128)(2,1)} %get-tuple-element.458), channel_id=1, source_target_pairs={{0,1},{1,0},{2,3},{3,2},{4,5},{5,4},{6,7},{7,6},{8,9},{9,8},{10,11... | collective-permute-start | bytes 663560 | tf_op jit(solution)/shard_map/ppermute | solution.py:239
  398.8 30.4 %collective-permute-start.37 = (bf16[144,768]{1,0:T(8,128)(2,1)}, bf16[144,768]{1,0:T(8,128)(2,1)S(1)}, u32[]{:S(2)}, u32[]{:S(2)}) collective-permute-start(bf16[144,768]{1,0:T(8,128)(2,1)} %get-tuple-element.457), channel_id=1, source_target_pairs={{0,2},{1,3},{2,0},{3,1},{4,6},{5,7},{6,4},{7,5},{8,10},{9,11},{10,... | collective-permute-start | bytes 663560 | tf_op jit(solution)/shard_map/ppermute | solution.py:239
  449.4 29.6 %collective-permute-start.49 = (bf16[8,128,1024]{2,1,0:T(8,128)(2,1)}, bf16[8,128,1024]{2,1,0:T(8,128)(2,1)}, u32[]{:S(2)}, u32[]{:S(2)}) collective-permute-start(bf16[8,128,1024]{2,1,0:T(8,128)(2,1)} %bitcast.147), channel_id=1, source_target_pairs={{0,8},{8,0},{16,24},{24,16},{1,9},{9,1},{17,25},{25,17},{2,10},{10... | collective-permute-start | bytes 6291464 | tf_op jit(solution)/shard_map/ppermute | solution.py:36
  461.7 31.0 %collective-permute-start.47 = (bf16[8,128,1024]{2,1,0:T(8,128)(2,1)}, bf16[8,128,1024]{2,1,0:T(8,128)(2,1)}, u32[]{:S(2)}, u32[]{:S(2)}) collective-permute-start(bf16[8,128,1024]{2,1,0:T(8,128)(2,1)} %bitcast.135), channel_id=1, source_target_pairs={{0,8},{8,0},{16,24},{24,16},{1,9},{9,1},{17,25},{25,17},{2,10},{10... | collective-permute-start | bytes 6291464 | tf_op jit(solution)/shard_map/ppermute | solution.py:36
  462.3 30.5 %collective-permute-start.46 = (bf16[8,128,1024]{2,1,0:T(8,128)(2,1)}, bf16[8,128,1024]{2,1,0:T(8,128)(2,1)}, u32[]{:S(2)}, u32[]{:S(2)}) collective-permute-start(bf16[8,128,1024]{2,1,0:T(8,128)(2,1)} %bitcast.129), channel_id=1, source_target_pairs={{0,8},{8,0},{16,24},{24,16},{1,9},{9,1},{17,25},{25,17},{2,10},{10... | collective-permute-start | bytes 6291464 | tf_op jit(solution)/shard_map/ppermute | solution.py:36
  511.9 42.7 %collective-permute-start.61 = (bf16[8,128,1024]{2,1,0:T(8,128)(2,1)}, bf16[8,128,1024]{2,1,0:T(8,128)(2,1)}, u32[]{:S(2)}, u32[]{:S(2)}) collective-permute-start(bf16[8,128,1024]{2,1,0:T(8,128)(2,1)} %bitcast.160), channel_id=1, source_target_pairs={{0,8},{8,0},{16,24},{24,16},{1,9},{9,1},{17,25},{25,17},{2,10},{10... | collective-permute-start | bytes 6291464 | tf_op jit(solution)/shard_map/ppermute | solution.py:36
  514.0 40.9 %collective-permute-start.60 = (bf16[8,128,1024]{2,1,0:T(8,128)(2,1)S(1)}, bf16[8,128,1024]{2,1,0:T(8,128)(2,1)}, u32[]{:S(2)}, u32[]{:S(2)}) collective-permute-start(bf16[8,128,1024]{2,1,0:T(8,128)(2,1)S(1)} %bitcast.715), channel_id=1, source_target_pairs={{0,8},{8,0},{16,24},{24,16},{1,9},{9,1},{17,25},{25,17},{2,10},{10... | collective-permute-start | bytes 6291464 | tf_op jit(solution)/shard_map/ppermute | solution.py:36
  533.3 49.3 %collective-permute-start.64 = (bf16[4,128,1024]{2,1,0:T(8,128)(2,1)}, bf16[4,128,1024]{2,1,0:T(8,128)(2,1)S(1)}, u32[]{:S(2)}, u32[]{:S(2)}) collective-permute-start(bf16[4,128,1024]{2,1,0:T(8,128)(2,1)} %dynamic-slice_bitcast_fusion.6), channel_id=1, source_target_pairs={{0,16},{1,17},{2,18},{3,19},{4,20},{5,21},{6,22},{7,23},{8,9},{9,8... | collective-permute-start | bytes 3145736 | tf_op jit(solution)/shard_map/ppermute | solution.py:89
  554.6 28.5 %collective-permute-start.63 = (bf16[4,128,1024]{2,1,0:T(8,128)(2,1)}, bf16[4,128,1024]{2,1,0:T(8,128)(2,1)S(1)}, u32[]{:S(2)}, u32[]{:S(2)}) collective-permute-start(bf16[4,128,1024]{2,1,0:T(8,128)(2,1)} %fusion.91), channel_id=1, source_target_pairs={{0,16},{1,17},{2,18},{3,19},{4,20},{5,21},{6,22},{7,23},{8,9},{9,8... | collective-permute-start | bytes 3145736 | tf_op jit(solution)/shard_map/ppermute | solution.py:89
  554.9 54.3 %collective-permute-start.67 = (bf16[8,128,1024]{2,1,0:T(8,128)(2,1)S(1)}, bf16[8,128,1024]{2,1,0:T(8,128)(2,1)S(1)}, u32[]{:S(2)}, u32[]{:S(2)}) collective-permute-start(bf16[8,128,1024]{2,1,0:T(8,128)(2,1)S(1)} %bitcast.718), channel_id=1, source_target_pairs={{0,8},{8,0},{16,24},{24,16},{1,9},{9,1},{17,25},{25,17},{2,10},{10... | collective-permute-start | bytes 6291464 | tf_op jit(solution)/shard_map/ppermute | solution.py:36
  556.1 53.2 %collective-permute-start.68 = (bf16[8,128,1024]{2,1,0:T(8,128)(2,1)S(1)}, bf16[8,128,1024]{2,1,0:T(8,128)(2,1)S(1)}, u32[]{:S(2)}, u32[]{:S(2)}) collective-permute-start(bf16[8,128,1024]{2,1,0:T(8,128)(2,1)S(1)} %bitcast.716), channel_id=1, source_target_pairs={{0,8},{8,0},{16,24},{24,16},{1,9},{9,1},{17,25},{25,17},{2,10},{10... | collective-permute-start | bytes 6291464 | tf_op jit(solution)/shard_map/ppermute | solution.py:36
  609.3 44.0 %collective-permute-start.71 = (bf16[8,192,1536]{2,1,0:T(8,128)(2,1)}, bf16[8,192,1536]{2,1,0:T(8,128)(2,1)}, u32[]{:S(2)}, u32[]{:S(2)}) collective-permute-start(bf16[8,192,1536]{2,1,0:T(8,128)(2,1)} %bitcast.181), channel_id=1, source_target_pairs={{0,8},{8,0},{16,24},{24,16},{1,9},{9,1},{17,25},{25,17},{2,10},{10... | collective-permute-start | bytes 14155784 | tf_op jit(solution)/shard_map/ppermute | solution.py:36
  615.9 128.8 %all-to-all-start.2 = ((bf16[8,144,192]{2,1,0:T(8,128)(2,1)}), bf16[8,144,192]{2,1,0:T(8,128)(2,1)}, u32[]{:S(2)}, u32[]{:S(2)}) async-start(bf16[8,144,192]{2,1,0:T(8,128)(2,1)} %bitcast.772), calls=%async_computation.2 | async-start | bytes 1179648 | tf_op jit(solution)/shard_map/all_to_all | solution.py:253
  635.1 52.9 %collective-permute-start.75 = (bf16[4,128,1024]{2,1,0:T(8,128)(2,1)}, bf16[4,128,1024]{2,1,0:T(8,128)(2,1)S(1)}, u32[]{:S(2)}, u32[]{:S(2)}) collective-permute-start(bf16[4,128,1024]{2,1,0:T(8,128)(2,1)} %fusion.31), channel_id=1, source_target_pairs={{0,1},{1,0},{2,3},{3,2},{4,5},{5,4},{6,7},{7,6},{8,24},{9,25},{10,... | collective-permute-start | bytes 3145736 | tf_op jit(solution)/shard_map/ppermute | solution.py:89
  637.8 50.3 %collective-permute-start.74 = (bf16[4,128,1024]{2,1,0:T(8,128)(2,1)}, bf16[4,128,1024]{2,1,0:T(8,128)(2,1)S(1)}, u32[]{:S(2)}, u32[]{:S(2)}) collective-permute-start(bf16[4,128,1024]{2,1,0:T(8,128)(2,1)} %dynamic-slice_bitcast_fusion.4), channel_id=1, source_target_pairs={{0,16},{1,17},{2,18},{3,19},{4,20},{5,21},{6,22},{7,23},{8,9},{9,8... | collective-permute-start | bytes 3145736 | tf_op jit(solution)/shard_map/ppermute | solution.py:89
  641.0 47.1 %collective-permute-start.73 = (bf16[4,128,1024]{2,1,0:T(8,128)(2,1)}, bf16[4,128,1024]{2,1,0:T(8,128)(2,1)S(1)}, u32[]{:S(2)}, u32[]{:S(2)}) collective-permute-start(bf16[4,128,1024]{2,1,0:T(8,128)(2,1)} %fusion.87), channel_id=1, source_target_pairs={{0,16},{1,17},{2,18},{3,19},{4,20},{5,21},{6,22},{7,23},{8,9},{9,8... | collective-permute-start | bytes 3145736 | tf_op jit(solution)/shard_map/ppermute | solution.py:89
  654.8 33.3 %collective-permute-start.76 = (bf16[2,128,1024]{2,1,0:T(8,128)(2,1)}, bf16[2,128,1024]{2,1,0:T(8,128)(2,1)S(1)}, u32[]{:S(2)}, u32[]{:S(2)}) collective-permute-start(bf16[2,128,1024]{2,1,0:T(8,128)(2,1)} %dynamic-slice_bitcast_fusion.9), channel_id=1, source_target_pairs={{0,2},{1,3},{2,0},{3,1},{4,6},{5,7},{6,4},{7,5},{8,10},{9,11},{10,... | collective-permute-start | bytes 1572872 | tf_op jit(solution)/shard_map/ppermute | solution.py:36
  696.2 65.7 %collective-permute-start.78 = (bf16[8,192,1536]{2,1,0:T(8,128)(2,1)}, bf16[8,192,1536]{2,1,0:T(8,128)(2,1)}, u32[]{:S(2)}, u32[]{:S(2)}) collective-permute-start(bf16[8,192,1536]{2,1,0:T(8,128)(2,1)} %bitcast.196), channel_id=1, source_target_pairs={{0,8},{8,0},{16,24},{24,16},{1,9},{9,1},{17,25},{25,17},{2,10},{10... | collective-permute-start | bytes 14155784 | tf_op jit(solution)/shard_map/ppermute | solution.py:36
  708.6 53.3 %collective-permute-start.79 = (bf16[4,192,1536]{2,1,0:T(8,128)(2,1)}, bf16[4,192,1536]{2,1,0:T(8,128)(2,1)}, u32[]{:S(2)}, u32[]{:S(2)}) collective-permute-start(bf16[4,192,1536]{2,1,0:T(8,128)(2,1)} %dynamic-slice_bitcast_fusion.1), channel_id=1, source_target_pairs={{0,1},{1,0},{2,3},{3,2},{4,5},{5,4},{6,7},{7,6},{8,9},{9,8},{10,11... | collective-permute-start | bytes 7077896 | tf_op jit(solution)/shard_map/ppermute | solution.py:36
  710.0 41.8 %collective-permute-start.77 = (bf16[576,1536]{1,0:T(8,128)(2,1)}, bf16[576,1536]{1,0:T(8,128)(2,1)}, u32[]{:S(2)}, u32[]{:S(2)}) collective-permute-start(bf16[576,1536]{1,0:T(8,128)(2,1)} %slice.360), channel_id=1, source_target_pairs={{0,16},{8,24},{16,0},{24,8},{1,17},{9,25},{17,1},{25,9},{2,18},{10... | collective-permute-start | bytes 5308424 | tf_op jit(solution)/shard_map/ppermute | solution.py:36
  743.0 71.8 %collective-permute-start.86 = (bf16[4,128,1024]{2,1,0:T(8,128)(2,1)}, bf16[4,128,1024]{2,1,0:T(8,128)(2,1)}, u32[]{:S(2)}, u32[]{:S(2)}) collective-permute-start(bf16[4,128,1024]{2,1,0:T(8,128)(2,1)} %fusion.28), channel_id=1, source_target_pairs={{0,1},{1,0},{2,3},{3,2},{4,5},{5,4},{6,7},{7,6},{8,24},{9,25},{10,... | collective-permute-start | bytes 3145736 | tf_op jit(solution)/shard_map/ppermute | solution.py:89
  782.1 78.5 %all-to-all-start.3 = ((bf16[8,576,192]{1,2,0:T(8,128)(2,1)}), bf16[8,576,192]{1,2,0:T(8,128)(2,1)}, u32[]{:S(2)}, u32[]{:S(2)}) async-start(bf16[8,576,192]{1,2,0:T(8,128)(2,1)} %copy.242), calls=%async_computation.3 | async-start | bytes 3932160 | tf_op jit(solution)/shard_map/all_to_all | solution.py:253
  795.6 65.0 %collective-permute-start.84 = (bf16[4,192,1536]{2,1,0:T(8,128)(2,1)}, bf16[4,192,1536]{2,1,0:T(8,128)(2,1)}, u32[]{:S(2)}, u32[]{:S(2)}) collective-permute-start(bf16[4,192,1536]{2,1,0:T(8,128)(2,1)} %dynamic-slice_bitcast_fusion), channel_id=1, source_target_pairs={{0,1},{1,0},{2,3},{3,2},{4,5},{5,4},{6,7},{7,6},{8,9},{9,8},{10,11... | collective-permute-start | bytes 7077896 | tf_op jit(solution)/shard_map/ppermute | solution.py:36
  801.2 49.5 %collective-permute-start.85 = (bf16[2,192,1536]{2,1,0:T(8,128)(2,1)S(1)}, bf16[2,192,1536]{2,1,0:T(8,128)(2,1)S(1)}, u32[]{:S(2)}, u32[]{:S(2)}) collective-permute-start(bf16[2,192,1536]{2,1,0:T(8,128)(2,1)S(1)} %dynamic-slice_bitcast_fusion.3), channel_id=1, source_target_pairs={{0,2},{1,3},{2,0},{3,1},{4,6},{5,7},{6,4},{7,5},{8,10},{9,11},{10,... | collective-permute-start | bytes 3538952 | tf_op jit(solution)/shard_map/ppermute | solution.py:36
  804.4 44.6 %collective-permute-start.88 = (bf16[1,128,1024]{2,1,0:T(8,128)(2,1)S(1)}, bf16[1,128,1024]{2,1,0:T(8,128)(2,1)S(1)}, u32[]{:S(2)}, u32[]{:S(2)}) collective-permute-start(bf16[1,128,1024]{2,1,0:T(8,128)(2,1)S(1)} %constant_dynamic-slice_fusion.14), channel_id=1, source_target_pairs={{0,4},{1,5},{2,6},{3,7},{4,0},{5,1},{6,2},{7,3},{8,12},{9,13},{10,... | collective-permute-start | bytes 786440 | tf_op jit(solution)/shard_map/ppermute | solution.py:36
  807.6 42.8 %collective-permute-start.87 = (bf16[128,1024]{1,0:T(8,128)(2,1)}, bf16[128,1024]{1,0:T(8,128)(2,1)}, u32[]{:S(2)}, u32[]{:S(2)}) collective-permute-start(bf16[128,1024]{1,0:T(8,128)(2,1)} %fusion.124), channel_id=1, source_target_pairs={{0,16},{8,24},{16,0},{24,8},{1,17},{9,25},{17,1},{25,9},{2,18},{10... | collective-permute-start | bytes 786440 | tf_op jit(solution)/shard_map/ppermute | solution.py:36
  814.7 62.5 %collective-permute-start.93 = (bf16[128,1024]{1,0:T(8,128)(2,1)}, bf16[128,1024]{1,0:T(8,128)(2,1)}, u32[]{:S(2)}, u32[]{:S(2)}) collective-permute-start(bf16[128,1024]{1,0:T(8,128)(2,1)} %fusion.124), channel_id=1, source_target_pairs={{0,8},{8,0},{16,24},{24,16},{1,9},{9,1},{17,25},{25,17},{2,10},{10... | collective-permute-start | bytes 786440 | tf_op jit(solution)/shard_map/ppermute | solution.py:36
  848.9 28.5 %collective-permute-start.92 = (bf16[4,192,256]{2,1,0:T(8,128)(2,1)}, bf16[4,192,256]{2,1,0:T(8,128)(2,1)}, u32[]{:S(2)}, u32[]{:S(2)}) collective-permute-start(bf16[4,192,256]{2,1,0:T(8,128)(2,1)} %fusion.102), channel_id=1, source_target_pairs={{0,1},{1,0},{2,3},{3,2},{4,5},{5,4},{6,7},{7,6},{8,24},{9,25},{10,... | collective-permute-start | bytes 1179656 | tf_op jit(solution)/shard_map/ppermute | solution.py:89
  863.9 45.2 %collective-permute-start.91 = (bf16[2,128,1024]{2,1,0:T(8,128)(2,1)}, bf16[2,128,1024]{2,1,0:T(8,128)(2,1)}, u32[]{:S(2)}, u32[]{:S(2)}) collective-permute-start(bf16[2,128,1024]{2,1,0:T(8,128)(2,1)} %dynamic-slice_bitcast_fusion.7), channel_id=1, source_target_pairs={{0,2},{1,3},{2,0},{3,1},{4,6},{5,7},{6,4},{7,5},{8,10},{9,11},{10,... | collective-permute-start | bytes 1572872 | tf_op jit(solution)/shard_map/ppermute | solution.py:36
  869.0 46.7 %collective-permute-start.89 = (bf16[2,192,1536]{2,1,0:T(8,128)(2,1)}, bf16[2,192,1536]{2,1,0:T(8,128)(2,1)}, u32[]{:S(2)}, u32[]{:S(2)}) collective-permute-start(bf16[2,192,1536]{2,1,0:T(8,128)(2,1)} %dynamic-slice_bitcast_fusion.2), channel_id=1, source_target_pairs={{0,2},{1,3},{2,0},{3,1},{4,6},{5,7},{6,4},{7,5},{8,10},{9,11},{10,... | collective-permute-start | bytes 3538952 | tf_op jit(solution)/shard_map/ppermute | solution.py:36
  872.1 41.4 %collective-permute-start.90 = (bf16[1,192,1536]{2,1,0:T(8,128)(2,1)}, bf16[1,192,1536]{2,1,0:T(8,128)(2,1)}, u32[]{:S(2)}, u32[]{:S(2)}) collective-permute-start(bf16[1,192,1536]{2,1,0:T(8,128)(2,1)} %constant_dynamic-slice_fusion.13), channel_id=1, source_target_pairs={{0,4},{1,5},{2,6},{3,7},{4,0},{5,1},{6,2},{7,3},{8,12},{9,13},{10,... | collective-permute-start | bytes 1769480 | tf_op jit(solution)/shard_map/ppermute | solution.py:36
  877.2 31.4 %collective-permute-start.95 = (bf16[128,1024]{1,0:T(8,128)(2,1)S(1)}, bf16[128,1024]{1,0:T(8,128)(2,1)S(1)}, u32[]{:S(2)}, u32[]{:S(2)}) collective-permute-start(bf16[128,1024]{1,0:T(8,128)(2,1)S(1)} %fusion.125.refs_0_), channel_id=1, source_target_pairs={{0,16},{8,24},{16,0},{24,8},{1,17},{9,25},{17,1},{25,9},{2,18},{10... | collective-permute-start | bytes 786440 | tf_op jit(solution)/shard_map/ppermute | solution.py:36
  877.5 31.6 %collective-permute-start.94 = (bf16[128,1024]{1,0:T(8,128)(2,1)}, bf16[128,1024]{1,0:T(8,128)(2,1)}, u32[]{:S(2)}, u32[]{:S(2)}) collective-permute-start(bf16[128,1024]{1,0:T(8,128)(2,1)} %collective-permute-done.87), channel_id=1, source_target_pairs={{0,8},{8,0},{16,24},{24,16},{1,9},{9,1},{17,25},{25,17},{2,10},{10... | collective-permute-start | bytes 786440 | tf_op jit(solution)/shard_map/ppermute | solution.py:36
  908.6 36.7 %collective-permute-start.101 = (bf16[128,1024]{1,0:T(8,128)(2,1)S(1)}, bf16[128,1024]{1,0:T(8,128)(2,1)S(1)}, u32[]{:S(2)}, u32[]{:S(2)}) collective-permute-start(bf16[128,1024]{1,0:T(8,128)(2,1)S(1)} %fusion.125.refs_0_), channel_id=1, source_target_pairs={{0,8},{8,0},{16,24},{24,16},{1,9},{9,1},{17,25},{25,17},{2,10},{10... | collective-permute-start | bytes 786440 | tf_op jit(solution)/shard_map/ppermute | solution.py:36
  917.7 31.8 %collective-permute-start.100 = (bf16[2,192,256]{2,1,0:T(8,128)(2,1)}, bf16[2,192,256]{2,1,0:T(8,128)(2,1)}, u32[]{:S(2)}, u32[]{:S(2)}) collective-permute-start(bf16[2,192,256]{2,1,0:T(8,128)(2,1)} %dynamic-slice_bitcast_fusion.11), channel_id=1, source_target_pairs={{0,2},{1,3},{2,0},{3,1},{4,6},{5,7},{6,4},{7,5},{8,10},{9,11},{10,... | collective-permute-start | bytes 589832 | tf_op jit(solution)/shard_map/ppermute | solution.py:36
  923.1 40.8 %collective-permute-start.98 = (bf16[192,1536]{1,0:T(8,128)(2,1)}, bf16[192,1536]{1,0:T(8,128)(2,1)}, u32[]{:S(2)}, u32[]{:S(2)}) collective-permute-start(bf16[192,1536]{1,0:T(8,128)(2,1)} %fusion.103), channel_id=1, source_target_pairs={{0,16},{8,24},{16,0},{24,8},{1,17},{9,25},{17,1},{25,9},{2,18},{10... | collective-permute-start | bytes 1769480 | tf_op jit(solution)/shard_map/ppermute | solution.py:36
  926.0 38.0 %collective-permute-start.97 = (bf16[1,192,1536]{2,1,0:T(8,128)(2,1)}, bf16[1,192,1536]{2,1,0:T(8,128)(2,1)}, u32[]{:S(2)}, u32[]{:S(2)}) collective-permute-start(bf16[1,192,1536]{2,1,0:T(8,128)(2,1)} %constant_dynamic-slice_fusion.11), channel_id=1, source_target_pairs={{0,4},{1,5},{2,6},{3,7},{4,0},{5,1},{6,2},{7,3},{8,12},{9,13},{10,... | collective-permute-start | bytes 1769480 | tf_op jit(solution)/shard_map/ppermute | solution.py:36
  949.5 54.8 %collective-permute-start.116 = (bf16[192,1536]{1,0:T(8,128)(2,1)}, bf16[192,1536]{1,0:T(8,128)(2,1)S(1)}, u32[]{:S(2)}, u32[]{:S(2)}) collective-permute-start(bf16[192,1536]{1,0:T(8,128)(2,1)} %fusion.103), channel_id=1, source_target_pairs={{0,8},{8,0},{16,24},{24,16},{1,9},{9,1},{17,25},{25,17},{2,10},{10... | collective-permute-start | bytes 1769480 | tf_op jit(solution)/shard_map/ppermute | solution.py:36
  (294 other events, 4647.0 us)
